TPU v7x, 32 devices: a whole 2x2x4 slice. The times are simulated.
32 devices in a mesh: client: 8 (over y, x, core), unit: 4 (over z).
Axes of the slice: x: 2, y: 2, z: 4, core: 2. Of those that a mesh axis runs over, the one named last changes fastest.
Arguments:
- token_ids: int32 [256], replicated, may hold values from 0 to 65535
- embed_table: bfloat16 [65536, 4096], P(('client', 'unit')), may hold values from -6 to 6
- norm_gain: float32 [4096], replicated, may hold values from 0.5 to 1.5
- client_gate: bfloat16 [8, 4096, 7168], P('client', None, 'unit'), may hold values from -0.09375 to 0.09375
- client_up: bfloat16 [8, 4096, 7168], P('client', None, 'unit'), may hold values from -0.09375 to 0.09375
- ref_gate: bfloat16 [4096, 7168], P('client', 'unit'), may hold values from -0.09375 to 0.09375
- ref_up: bfloat16 [4096, 7168], P('client', 'unit'), may hold values from -0.09375 to 0.09375
Outputs:
- merged: float32 [7168, 256], P('unit')
- score: float32 [8, 7168], P('client', 'unit')
All inputs are finite; a program needn't handle non-finite values.
Results may differ from a plain program's by a relative error of at most 0.014.
Values may be sent and summed in bfloat16 or wider, within the bound.
No kernel may reach another device: no remote copies, remote signals or barrier semaphores. Data moves between devices by JAX's collectives and lax.ppermute only.
A program may use at most 128 MiB of HBM per device.

v0:
```python
import jax
import jax.numpy as jnp
from jax import lax
from jax.sharding import PartitionSpec as P

sharpness = 40.0
block_cols = 2048


def standardize(hidden):
    center = jnp.mean(hidden, axis=0, keepdims=True)
    shifted = hidden - center
    spread = jnp.sqrt(jnp.mean(shifted * shifted, axis=0, keepdims=True) + 1e-06)
    return (shifted / spread).astype(jnp.bfloat16)


def block_ranges(length):
    return [(offset, min(block_cols, length - offset)) for offset in range(0, length, block_cols)]


def rms_scaled(values, norm_gain):
    scale = lax.rsqrt(jnp.mean(values * values, axis=1, keepdims=True) + 1e-05)
    return (values * scale * norm_gain[None, :]).astype(jnp.bfloat16)


def body(token_ids, embed_table, norm_gain, client_gate, client_up, ref_gate, ref_up):
    rows_here = embed_table.shape[0]
    table_start = (
        lax.axis_index("client") * lax.axis_size("unit") + lax.axis_index("unit")
    ) * rows_here
    table_rows = table_start + jnp.arange(rows_here, dtype=jnp.int32)
    selector = (token_ids[:, None] == table_rows[None, :]).astype(jnp.bfloat16)
    partial_rows = jnp.dot(selector, embed_table, preferred_element_type=jnp.float32)
    embedded = lax.psum(partial_rows, ("client", "unit"))
    normed = rms_scaled(embedded, norm_gain)
    token_count = normed.shape[0]
    inverse_tokens = 1.0 / token_count
    gate_local = jnp.dot(normed, client_gate[0], preferred_element_type=jnp.float32)
    up_local = jnp.dot(normed, client_up[0], preferred_element_type=jnp.float32)
    client_std = standardize(jax.nn.silu(gate_local) * up_local)
    row_span = ref_gate.shape[0]
    normed_slice = lax.dynamic_slice_in_dim(
        normed, lax.axis_index("client") * row_span, row_span, 1
    )
    gate_part = jnp.dot(normed_slice, ref_gate, preferred_element_type=jnp.float32)
    up_part = jnp.dot(normed_slice, ref_up, preferred_element_type=jnp.float32)
    gate_sum, up_sum = lax.psum((gate_part, up_part), "client")
    ref_std = standardize(jax.nn.silu(gate_sum) * up_sum)
    local_units = client_std.shape[1]
    segment = lax.all_gather(client_std, "unit", axis=1, tiled=True)
    numerator = jnp.zeros((local_units, token_count), jnp.float32)
    colsum = jnp.zeros((local_units,), jnp.float32)
    weighted = jnp.zeros((local_units,), jnp.float32)
    for offset, width in block_ranges(segment.shape[1]):
        columns = segment[:, offset : offset + width]
        correlation = (
            jnp.dot(columns.T, ref_std, preferred_element_type=jnp.float32) * inverse_tokens
        )
        weights = jnp.exp(sharpness * correlation)
        numerator = numerator + lax.dot_general(
            weights.astype(jnp.bfloat16),
            columns,
            (((0,), (1,)), ((), ())),
            preferred_element_type=jnp.float32,
        )
        colsum = colsum + jnp.sum(weights, axis=0)
        weighted = weighted + jnp.sum(weights * correlation, axis=0)
    numerator, colsum, weighted = (numerator, colsum, weighted)
    matched = numerator / colsum[:, None]
    score = (weighted / colsum)[None, :]
    merged = lax.psum(matched.astype(jnp.bfloat16), "client").astype(jnp.float32) / lax.axis_size(
        "client"
    )
    return (merged, score)


def solution(mesh):
    in_specs = (
        P(),
        P(("client", "unit"), None),
        P(),
        P("client", None, "unit"),
        P("client", None, "unit"),
        P("client", "unit"),
        P("client", "unit"),
    )
    out_specs = (P("unit", None), P("client", "unit"))
    return jax.shard_map(body, mesh=mesh, in_specs=in_specs, out_specs=out_specs, check_vma=False)
```

profile of v0, /device:TPU:0, one launch (start us, length us, event | category | flops | bytes accessed | tf_op | source)
XLA Modules:
  0.0 440.3 jit_solution(6551167433018301328)
XLA Ops:
  7.2 10.3 %fusion.36 = f32[256,4096]{1,0:T(8,128)} fusion(bf16[2048,4096]{1,0:T(8,128)(2,1)} %param.8, s32[2048]{0:T(1024)S(1)} %iota_add_fusion, s32[256]{0:T(256)} %param.7), kind=kOutput, calls=%fused_computation.34 | convolution fusion | flops 4295491584 | bytes 20980736 | tf_op jit(solution)/shard_map/dot_general | solution.py:33
  17.6 144.6 %all-reduce.5.cloned.1.call-done = f32[256,4096]{1,0:T(8,128)} async-done(((f32[256,4096]{1,0:T(8,128)}), f32[256,4096]{1,0:T(8,128)}) %all-reduce.5.cloned.1.call-update) | async-done | bytes 4194320 | tf_op jit(solution)/shard_map/psum | solution.py:34
  162.2 2.7 multiply_reduce_fusion.4
  165.0 0.7 copy-done.2
  165.7 0.6 multiply_convert_fusion
  166.3 1.9 fusion.58
  168.2 1.9 fusion.60
  170.1 11.1 %fusion.2 = f32[256,1792]{1,0:T(8,128)} fusion(bf16[256,4096]{1,0:T(8,128)(2,1)} %copy-done.3, bf16[1,4096,1792]{2,1,0:T(8,128)(2,1)} %param.10), kind=kOutput, calls=%fused_computation.2 | convolution fusion | flops 3758096384 | bytes 18612224 | tf_op jit(solution)/shard_map/dot_general | solution.py:38
  181.2 11.0 %fusion.69 = (f32[1792]{0:T(1024)S(1)}, f32[256,1792]{1,0:T(8,128)S(1)}) fusion(bf16[256,4096]{1,0:T(8,128)(2,1)} %copy-done.3, bf16[1,4096,1792]{2,1,0:T(8,128)(2,1)} %param.11, f32[256,1792]{1,0:T(8,128)} %fusion.2), kind=kOutput, calls=%fused_computation.77 | convolution fusion | flops 3760847104 | bytes 20454400 | tf_op jit(solution)/shard_map/dot_general | solution.py:39
  192.4 1.1 divide_convert_fusion.1
  193.8 61.9 %all-reduce.9.cloned.1.call-done = (f32[256,1792]{1,0:T(8,128)}, f32[256,1792]{1,0:T(8,128)}) async-done(((f32[256,1792]{1,0:T(8,128)}, f32[256,1792]{1,0:T(8,128)}), (f32[256,1792]{1,0:T(8,128)}, f32[256,1792]{1,0:T(8,128)})) %all-reduce.9.cloned.1.call-update) | async-done | bytes 3670032 | tf_op jit(solution)/shard_map/psum | solution.py:47
  255.7 2.6 fusion.68
  258.6 70.9 %all-gather.2.cloned.1.call-done = bf16[256,7168]{1,0:T(8,128)(2,1)} async-done(((bf16[256,1792]{1,0:T(8,128)(2,1)}), bf16[256,7168]{1,0:T(8,128)(2,1)}) %all-gather.2.cloned.1.call-update) | async-done | bytes 3670032 | tf_op jit(solution)/shard_map/all_gather | solution.py:50
  329.5 8.6 %multiply_reduce_fusion.2 = (f32[1792]{0:T(1024)S(1)}, f32[1792]{0:T(1024)S(1)}, f32[2048,1792]{1,0:T(8,128)}) fusion(bf16[256,1792]{1,0:T(8,128)(2,1)S(1)} %divide_convert_fusion, bf16[256,7168]{1,0:T(8,128)(2,1)} %all-gather.2.cloned.1.call-done), kind=kOutput, calls=%fused_computation.6 | convolution fusion | flops 1897394688 | bytes 16660480 | tf_op jit(solution)/shard_map/dot_general | solution.py:57
  338.1 3.8 multiply_reduce_fusion.1
  341.9 7.1 %multiply_reduce_fusion = (f32[1792]{0:T(1024)S(1)}, f32[1792]{0:T(1024)S(1)}, f32[2048,1792]{1,0:T(8,128)}) fusion(bf16[256,1792]{1,0:T(8,128)(2,1)S(1)} %divide_convert_fusion, bf16[256,7168]{1,0:T(8,128)(2,1)S(1)} %copy-done.4), kind=kOutput, calls=%fused_computation.4 | convolution fusion | flops 1897394688 | bytes 16660480 | tf_op jit(solution)/shard_map/dot_general | solution.py:57
  349.1 4.0 multiply_reduce_fusion.3
  353.1 7.6 %fusion.10 = f32[1792,256]{1,0:T(8,128)S(1)} fusion(f32[2048,1792]{1,0:T(8,128)} %get-tuple-element.20, bf16[256,7168]{1,0:T(8,128)(2,1)S(1)} %copy-done.4), kind=kOutput, calls=%fused_computation.16 | convolution fusion | flops 1886388224 | bytes 17563648 | tf_op jit(solution)/shard_map/dot_general | solution.py:60
  360.7 2.5 fusion.33
  363.2 7.7 %fusion.30 = f32[1792,256]{1,0:T(8,128)S(1)} fusion(f32[1792,256]{1,0:T(8,128)S(1)} %fusion.33, f32[2048,1792]{1,0:T(8,128)} %get-tuple-element.19, bf16[256,7168]{1,0:T(8,128)(2,1)S(1)} %copy-done.4), kind=kOutput, calls=%fused_computation.32 | convolution fusion | flops 1886846976 | bytes 19398656 | tf_op jit(solution)/shard_map/dot_general | solution.py:60
  370.9 5.5 %fusion.41 = bf16[1792,256]{1,0:T(8,128)(2,1)} fusion(f32[1792,256]{1,0:T(8,128)S(1)} %fusion.30, f32[1024,1792]{1,0:T(8,128)} %get-tuple-element.18, f32[1792]{0:T(1024)S(1)} %get-tuple-element.13, bf16[256,7168]{1,0:T(8,128)(2,1)S(1)} %copy-done.4), kind=kOutput, calls=%fused_computation.37 | convolution fusion | flops 944570368 | bytes 10625024 | tf_op jit(solution)/shard_map/dot_general | solution.py:60
  376.5 0.6 div.85
  377.1 54.1 %all-reduce.7.cloned.1.call-done = bf16[1792,256]{1,0:T(8,128)(2,1)} async-done(((bf16[1792,256]{1,0:T(8,128)(2,1)}), bf16[1792,256]{1,0:T(8,128)(2,1)}) %all-reduce.7.cloned.1.call-update) | async-done | bytes 917520 | tf_op jit(solution)/shard_map/psum | solution.py:71
  431.2 2.5 convert_multiply_fusion
  (31 shorter events, 1.1 us)
Async XLA Ops:
  7.2 159.1 %copy-start = (bf16[512,1792]{1,0:T(8,128)(2,1)S(1)}, bf16[512,1792]{1,0:T(8,128)(2,1)}, u32[]{:S(2)}) copy-start(bf16[512,1792]{1,0:T(8,128)(2,1)} %param.13) | copy-start | bytes 5505028
  7.2 155.1 %all-reduce.5.cloned.1.call-start = ((), (), s32[]{:S(2)}) async-start(), calls=%async_computation | async-start | bytes 8388608 | tf_op jit(solution)/shard_map/psum | solution.py:34
  17.6 147.4 %copy-start.6 = (f32[4096]{0:T(1024)S(1)}, f32[4096]{0:T(1024)}, u32[]{:S(2)}) copy-start(f32[4096]{0:T(1024)} %param.9) | copy-start | bytes 49156
  17.6 238.1 %all-reduce.9.cloned.1.call-start = ((), (), s32[]{:S(2)}) async-start(), calls=%async_computation.3 | async-start | bytes 7340032 | tf_op jit(solution)/shard_map/psum | solution.py:47
  162.2 3.4 copy-start.2
  165.7 2.5 copy-start.5
  166.3 1.9 copy-start.3
  181.2 148.4 %all-gather.2.cloned.1.call-start = ((), (), s32[]{:S(2)}) async-start(), calls=%async_computation.1 | async-start | bytes 4587520 | tf_op jit(solution)/shard_map/all_gather | solution.py:50
  193.6 237.7 %all-reduce.7.cloned.1.call-start = ((), (), s32[]{:S(2)}) async-start(), calls=%async_computation.2 | async-start | bytes 1835008 | tf_op jit(solution)/shard_map/psum | solution.py:71
  329.5 8.6 %copy-start.4 = (bf16[256,7168]{1,0:T(8,128)(2,1)S(1)}, bf16[256,7168]{1,0:T(8,128)(2,1)}, u32[]{:S(2)}) copy-start(bf16[256,7168]{1,0:T(8,128)(2,1)} %all-gather.2.cloned.1.call-done) | copy-start | bytes 11010052
  370.9 62.9 %copy-start.1 = (bf16[512,1792]{1,0:T(8,128)(2,1)S(1)}, bf16[512,1792]{1,0:T(8,128)(2,1)}, u32[]{:S(2)}) copy-start(bf16[512,1792]{1,0:T(8,128)(2,1)} %param.13) | copy-start | bytes 5505028
Sparse Core Ops, SparseCore 0:
  17.7 144.4 all-reduce.4
  181.3 74.3 all-reduce.8
  257.3 72.1 all-gather.1
  376.6 54.5 all-reduce.6
where the time goes:
time: 441 us; the launch traced here: 440 us
  waiting for transfers between devices  332 us (75%)
  matrix products  83 us (19%)
  between operations  13.9 us (3%)
  other arithmetic  10.1 us (2%)
    psum x1, waiting for transfers between devices, body(): embedded = lax.psum(partial_rows, ('client', 'unit'))  145 us
    all_gather x1, waiting for transfers between devices, body(): segment = lax.all_gather(client_std, 'unit', axis=1, tiled=True)  70.9 us
    psum x1, waiting for transfers between devices, body(): gate_sum, up_sum = lax.psum((gate_part, up_part), 'client')  61.9 us
    psum x1, waiting for transfers between devices, body(): lax.psum(matched.astype(jnp.bfloat16), 'client').astype(jnp.float32)  54.1 us
    dot_general x4, matrix products, body(): jnp.dot(columns.T, ref_std, preferred_element_type=jnp.float32)  23.5 us
    dot_general x4, matrix products, body(): lax.dot_general(weights.astype(jnp.bfloat16), columns, (((0,), (1,)), (()...  23.3 us
    dot_general x1, matrix products, body(): jnp.dot(normed, client_gate[0], preferred_element_type=jnp.float32)  11.1 us
    dot_general x1, matrix products, body(): up_local = jnp.dot(normed, client_up[0], preferred_element_type=jnp.float32)  11 us
  transfers between devices with their start and end apart: 4, of which 4 were waited for; matrix products, arithmetic and copies ran while one was open for 4% of the time, Pallas kernels for 0%

commit v1 on v0

v1 whole, which is shorter than its diff:
```python
import functools

import jax
import jax.numpy as jnp
from jax import lax
from jax.experimental import pallas as pl
from jax.experimental.pallas import tpu as pltpu
from jax.sharding import PartitionSpec as P

sharpness = 40.0
log2_e = 1.4426950408889634
group_rows = 16
fetch_slots = 16
bf16 = jnp.bfloat16
f32 = jnp.float32
whole = pl.BlockSpec(memory_space=pltpu.VMEM)
scalars = pl.BlockSpec(memory_space=pltpu.SMEM)
anywhere = pl.BlockSpec(memory_space=pl.ANY)


def vmem_params(mib):
    return pltpu.CompilerParams(vmem_limit_bytes=mib * 1024 * 1024)


def cost(flops, bytes_accessed, transcendentals=0):
    return pl.CostEstimate(
        flops=int(flops), bytes_accessed=int(bytes_accessed), transcendentals=int(transcendentals)
    )


def xor_permute(value, axis, size, mask):
    return lax.ppermute(value, axis, [(i, i ^ mask) for i in range(size)])


def select_kernel(ids, place, gain, table, keep, send, rows, held, slots, sems):
    tokens, width = rows.shape
    rows_here = table.shape[0]
    start = place[0] * rows_here
    client = place[1]

    def note(t, count):
        local = ids[t] - start
        mine = jnp.logical_and(local >= 0, local < rows_here)

        @pl.when(mine)
        def _():
            held[count] = t

        return count + jnp.where(mine, 1, 0)

    def fetch(k):
        t = held[k]
        group = pl.multiple_of((ids[t] - start) // group_rows * group_rows, group_rows)
        slot = lax.rem(k, fetch_slots)
        return pltpu.make_async_copy(
            table.at[pl.ds(group, group_rows), :], slots.at[slot], sems.at[slot]
        )

    count = lax.fori_loop(0, tokens, note, jnp.int32(0))

    def begin(k, carry):
        fetch(k).start()
        return carry

    lax.fori_loop(0, jnp.minimum(count, fetch_slots), begin, 0)
    rows[...] = jnp.zeros_like(rows)
    sublane = lax.broadcasted_iota(jnp.int32, (group_rows, width), 0)

    def place_row(k, carry):
        fetch(k).wait()
        t = held[k]
        row_in_group = lax.rem(ids[t] - start, group_rows)
        block = slots[lax.rem(k, fetch_slots)].astype(f32)
        row = jnp.sum(jnp.where(sublane == row_in_group, block, 0.0), axis=0, keepdims=True)
        scale = lax.rsqrt(jnp.sum(row * row, axis=1, keepdims=True) * (1.0 / width) + 1e-05)
        rows[pl.ds(t, 1), :] = row * scale * gain[...]

        @pl.when(k + fetch_slots < count)
        def _():
            fetch(k + fetch_slots).start()

        return carry

    lax.fori_loop(0, count, place_row, 0)
    span = keep.shape[2]
    for p in range(2 * keep.shape[0]):
        source = pl.multiple_of((client ^ p) * span, span)
        target = send if p % 2 else keep
        target[p // 2] = rows[:, pl.ds(source, span)].astype(bf16)


def select_rows(token_ids, place, norm_gain, embed_table, clients):
    tokens, width = token_ids.shape[0], embed_table.shape[1]
    half = jax.ShapeDtypeStruct((clients // 2, tokens, width // clients), bf16)
    return pl.pallas_call(
        select_kernel,
        out_shape=(half, half),
        in_specs=[scalars, scalars, whole, anywhere],
        out_specs=(whole, whole),
        scratch_shapes=[
            pltpu.VMEM((tokens, width), f32),
            pltpu.SMEM((tokens,), jnp.int32),
            pltpu.VMEM((fetch_slots, group_rows, width), bf16),
            pltpu.SemaphoreType.DMA((fetch_slots,)),
        ],
        compiler_params=vmem_params(24),
        cost_estimate=cost(4e6, 4e6),
        name="select_rows",
    )(token_ids, place, norm_gain[None, :], embed_table)


def standardized(hidden, axis):
    count = hidden.shape[axis]
    center = jnp.sum(hidden, axis=axis, keepdims=True) * (1.0 / count)
    shifted = hidden - center
    spread = jnp.sum(shifted * shifted, axis=axis, keepdims=True) * (1.0 / count)
    return (shifted * lax.rsqrt(spread + 1e-06)).astype(bf16)


def gated(gate, up):
    return gate / (1.0 + jnp.exp(-gate)) * up


def client_kernel(place, *refs):
    *blocks, gate_w, up_w, out = refs
    client = place[1]
    span = blocks[0].shape[1]
    gate = jnp.zeros(out.shape, f32)
    up = jnp.zeros(out.shape, f32)
    for p, block in enumerate(blocks):
        at = pl.ds(pl.multiple_of((client ^ p) * span, span), span)
        gate += jnp.dot(block[...], gate_w[0, at, :], preferred_element_type=f32)
        up += jnp.dot(block[...], up_w[0, at, :], preferred_element_type=f32)
    out[...] = standardized(gated(gate, up), 0)


def unit_block(units, most=256):
    return most if units % most == 0 else most // 2


def client_activations(place, blocks, client_gate, client_up):
    tokens, span = blocks[0].shape
    _, width, units = client_gate.shape
    wide = unit_block(units)
    weights = pl.BlockSpec((1, width, wide), lambda i: (0, 0, i))
    return pl.pallas_call(
        client_kernel,
        grid=(units // wide,),
        out_shape=jax.ShapeDtypeStruct((tokens, units), bf16),
        in_specs=[scalars]
        + [pl.BlockSpec((tokens, span), lambda i: (0, 0))] * len(blocks)
        + [weights, weights],
        out_specs=pl.BlockSpec((tokens, wide), lambda i: (0, i)),
        compiler_params=vmem_params(40),
        cost_estimate=cost(4 * tokens * width * units, 4 * width * units),
        name="client_activations",
    )(place, *blocks, client_gate, client_up)


def partial_kernel(place, rows, gate_w, up_w, keep, send, total):
    step = pl.program_id(0)
    wide = gate_w.shape[1]
    at = pl.ds(pl.multiple_of(step * wide, wide), wide)
    total[0, at, :] = jnp.dot(rows[...], gate_w[...], preferred_element_type=f32).T
    total[1, at, :] = jnp.dot(rows[...], up_w[...], preferred_element_type=f32).T

    @pl.when(step == pl.num_programs(0) - 1)
    def _():
        piece = keep.shape[2]
        for p in range(2 * keep.shape[0]):
            source = pl.ds(pl.multiple_of((place[1] ^ p) * piece, 8), piece)
            for which in range(2):
                if p % 2:
                    send[p // 2, which] = total[which, source, :].astype(bf16)
                else:
                    keep[p // 2, which] = total[which, source, :]


def reference_partials(place, rows, ref_gate, ref_up, clients):
    tokens, span = rows.shape
    units = ref_gate.shape[1]
    wide = unit_block(units)
    shape = (clients // 2, 2, units // clients, tokens)
    weights = pl.BlockSpec((span, wide), lambda i: (0, i))
    pieces = pl.BlockSpec(shape, lambda i: (0, 0, 0, 0))
    return pl.pallas_call(
        partial_kernel,
        grid=(units // wide,),
        out_shape=(jax.ShapeDtypeStruct(shape, f32), jax.ShapeDtypeStruct(shape, bf16)),
        in_specs=[scalars, pl.BlockSpec((tokens, span), lambda i: (0, 0)), weights, weights],
        out_specs=(pieces, pieces),
        scratch_shapes=[pltpu.VMEM((2, units, tokens), f32)],
        compiler_params=vmem_params(32),
        cost_estimate=cost(4 * tokens * span * units, 4 * span * units),
        name="reference_partials",
    )(place, rows, ref_gate, ref_up)


def match_kernel(refs, columns, numerator, sums, turned):
    tokens, units = columns.shape
    wide = unit_block(units)

    @pl.when(pl.program_id(0) == 0)
    def _():
        for i in range(0, units, wide):
            turned[i : i + wide, :] = columns[:, i : i + wide].T

    rows = refs[...]
    total = jnp.zeros(numerator.shape, f32)
    colsum = jnp.zeros((rows.shape[0], 128), f32)
    weighted = jnp.zeros((rows.shape[0], 128), f32)
    for i in range(0, units, wide):
        r = jnp.dot(rows, columns[:, i : i + wide], preferred_element_type=f32)
        w = jnp.exp2(r * (sharpness * log2_e / tokens))
        total += jnp.dot(w.astype(bf16), turned[i : i + wide, :], preferred_element_type=f32)
        wr = w * r
        for k in range(0, wide, 128):
            colsum += w[:, k : k + 128]
            weighted += wr[:, k : k + 128]
    numerator[...] = total
    sums[0] = jnp.sum(colsum, axis=1, keepdims=True)
    sums[1] = jnp.sum(weighted, axis=1, keepdims=True) * (1.0 / tokens)


def match(refs, columns):
    rows, tokens = refs.shape
    units = columns.shape[1]
    high = 512
    return pl.pallas_call(
        match_kernel,
        grid=(rows // high,),
        out_shape=(
            jax.ShapeDtypeStruct((rows, tokens), f32),
            jax.ShapeDtypeStruct((2, rows, 1), f32),
        ),
        in_specs=[
            pl.BlockSpec((high, tokens), lambda j: (j, 0)),
            pl.BlockSpec((tokens, units), lambda j: (0, 0)),
        ],
        out_specs=(
            pl.BlockSpec((high, tokens), lambda j: (j, 0)),
            pl.BlockSpec((2, high, 1), lambda j: (0, j, 0)),
        ),
        scratch_shapes=[pltpu.VMEM((units, tokens), bf16)],
        compiler_params=vmem_params(32),
        cost_estimate=cost(4 * rows * units * tokens, 8 * rows * tokens, rows * units),
        name="match",
    )(refs, columns)


def place_kernel(place, *refs):
    *pieces, out = refs
    size = pieces[0].shape[0]
    for p, piece in enumerate(pieces):
        at = pl.ds(pl.multiple_of((place[1] ^ p) * size, 8), size)
        out[at, :] = piece[...].astype(f32)


def placed(place, pieces):
    size, tokens = pieces[0].shape
    return pl.pallas_call(
        place_kernel,
        out_shape=jax.ShapeDtypeStruct((size * len(pieces), tokens), f32),
        in_specs=[scalars] + [whole] * len(pieces),
        out_specs=whole,
        compiler_params=vmem_params(16),
        cost_estimate=cost(1e5, 6 * size * len(pieces) * tokens),
        name="placed",
    )(place, *pieces)


def body(clients, parts, token_ids, embed_table, norm_gain, client_gate, client_up, ref_gate, ref_up):
    client = lax.axis_index("client")
    unit = lax.axis_index("unit")
    place = jnp.stack([client * parts + unit, client]).astype(jnp.int32)
    over_clients = functools.partial(xor_permute, axis="client", size=clients)
    over_units = functools.partial(xor_permute, axis="unit", size=parts)

    def gathered(own):
        blocks = [None] * clients
        for p in range(0, clients, 2):
            blocks[p] = over_clients(own, mask=p) if p else own
        for p in range(0, clients, 2):
            blocks[p + 1] = over_clients(blocks[p], mask=1)
        return blocks

    def scattered(keep, send):
        total = keep.astype(f32) + over_clients(send, mask=1).astype(f32)
        arrived = [over_clients(total[p // 2].astype(bf16), mask=p) for p in range(2, clients, 2)]
        mine = total[0]
        for other in arrived:
            mine = mine + other.astype(f32)
        return mine

    keep, send = select_rows(token_ids, place, norm_gain, embed_table, clients)
    own_rows = scattered(keep, send).astype(bf16)
    bit = 1
    while bit < parts:
        own_rows = own_rows + over_units(own_rows, mask=bit)
        bit *= 2

    blocks = gathered(own_rows)
    ref_keep, ref_send = reference_partials(place, own_rows, ref_gate, ref_up, clients)
    pre = scattered(ref_keep, ref_send)
    ref_piece = standardized(gated(pre[0], pre[1]), 1)
    even = range(0, parts, 2)
    ref_pieces = jnp.stack([over_units(ref_piece, mask=k) if k else ref_piece for k in even])
    refs = jnp.stack(gathered(ref_pieces), axis=1)
    groups, _, piece, tokens = refs.shape
    refs = refs.reshape(groups * clients * piece, tokens)

    columns = client_activations(place, blocks, client_gate, client_up)
    other = over_units(columns, mask=1)
    numerator_a, sums_a = match(refs, columns)
    numerator_b, sums_b = match(refs, other)
    sums = (sums_a + sums_b).reshape(2, groups, clients * piece)
    all_sums = sums
    for k in even[1:]:
        theirs = over_units(sums, mask=k)
        all_sums = all_sums + jnp.stack([theirs[:, g ^ (k // 2)] for g in range(groups)], axis=1)
    colsum, weighted = all_sums[0], all_sums[1]
    score = (weighted[0] / colsum[0]).reshape(clients, piece)
    score = score[jnp.arange(clients) ^ client].reshape(1, clients * piece)

    inverse = (1.0 / clients) / colsum
    numerator = (numerator_a + numerator_b).reshape(groups, clients * piece, tokens)
    matched = (numerator * inverse[:, :, None]).astype(bf16)
    matched = matched.reshape(groups, clients // 2, 2, piece, tokens)
    summed = scattered(
        matched[:, :, 0].transpose(1, 0, 2, 3), matched[:, :, 1].transpose(1, 0, 2, 3)
    )
    mine = summed[0]
    for k in even[1:]:
        mine = mine + over_units(summed[k // 2].astype(bf16), mask=k).astype(f32)
    merged = placed(place, gathered(mine.astype(bf16)))
    return (merged, score)


def solution(mesh):
    in_specs = (
        P(),
        P(("client", "unit"), None),
        P(),
        P("client", None, "unit"),
        P("client", None, "unit"),
        P("client", "unit"),
        P("client", "unit"),
    )
    out_specs = (P("unit", None), P("client", "unit"))
    local = functools.partial(body, mesh.shape["client"], mesh.shape["unit"])
    return jax.shard_map(local, mesh=mesh, in_specs=in_specs, out_specs=out_specs, check_vma=False)
```

time: 441 us -> 197 us (0.45)
  waiting for transfers between devices: 332 us -> 86.8 us
  matrix products: 83 us -> 0 us
  Pallas kernels: 0 us -> 47.8 us
  starting transfers between devices: 0.34 us -> 35.6 us
  between operations: 13.9 us -> 1.08 us
  local copies, waits for them, and re-layouts: 1.36 us -> 12.7 us
    psum x3 -> x0, waiting for transfers between devices: 261 us -> none  [the longest x1 145 us: body(): embedded = lax.psum(partial_rows, ('client', 'unit'))]
    ppermute x0 -> x39, waiting for transfers between devices: none -> 86.8 us  [xor_permute(): return lax.ppermute(value, axis, [(i, i ^ mask) for i in range(size)])]
    dot_general x13 -> x0, matrix products: 83 us -> none  [the longest x4 23.5 us: body(): jnp.dot(columns.T, ref_std, preferred_element_type=jnp.float32)]
    all_gather x1 -> x0, waiting for transfers between devices: 70.9 us -> none  [body(): segment = lax.all_gather(client_std, 'unit', axis=1, tiled=True)]
    pallas_call x0 -> x6, Pallas kernels: none -> 47.8 us  [the longest x2 21.3 us: match(): pl.pallas_call(match_kernel, grid=(rows // high,), out_shape=(jax.ShapeDt...]
    ppermute x0 -> x39, starting transfers between devices: none -> 35.6 us  [xor_permute(): return lax.ppermute(value, axis, [(i, i ^ mask) for i in range(size)])]
    unnamed x14 -> x20, local copies, waits for them, and re-layouts: 0.76 us -> 10.8 us
    add x1 -> x7, other arithmetic: 0.01 us -> 6.98 us  [the longest x1 5.54 us: body(): numerator_a + numerator_b]
  transfers between devices with their start and end apart: 4 -> 39, of which waited for: 4 -> 21; matrix products, arithmetic and copies ran while one was open for 4% -> 4% of each run, Pallas kernels for 0% -> 13%
where the time goes in v1:
time: 197 us; the launch traced here: 195 us
  waiting for transfers between devices  86.8 us (44%)
  Pallas kernels  47.8 us (24%)
  starting transfers between devices  35.6 us (18%)
  local copies, waits for them, and re-layouts  12.7 us (6%)
  other arithmetic  11.3 us (6%)
    ppermute x39, waiting for transfers between devices, xor_permute(): return lax.ppermute(value, axis, [(i, i ^ mask) for i in range(size)])  86.8 us
    ppermute x39, starting transfers between devices, xor_permute(): return lax.ppermute(value, axis, [(i, i ^ mask) for i in range(size)])  35.6 us
    pallas_call x2, Pallas kernels, match(): pl.pallas_call(match_kernel, grid=(rows // high,), out_shape=(jax.ShapeDt...  21.3 us
    pallas_call x1, Pallas kernels, client_activations(): pl.pallas_call(client_kernel, grid=(units // wide,), out_shape=jax.ShapeD...  14.7 us
    unnamed x20, local copies, waits for them, and re-layouts  10.8 us
    pallas_call x1, Pallas kernels, select_rows(): pl.pallas_call(select_kernel, out_shape=(half, half), in_specs=[scalars,...  5.8 us
    add x1, other arithmetic, body(): numerator_a + numerator_b  5.54 us
    pallas_call x1, Pallas kernels, reference_partials(): pl.pallas_call(partial_kernel, grid=(units // wide,), out_shape=(jax.Shap...  4.19 us
  transfers between devices with their start and end apart: 39, of which 21 were waited for; matrix products, arithmetic and copies ran while one was open for 4% of the time, Pallas kernels for 13%

profile of v1, /device:TPU:0, one launch (start us, length us, event | category | flops | bytes accessed | tf_op | source)
XLA Modules:
  0.0 195.4 jit_solution(12255277604584086671)
XLA Ops:
  0.7 5.8 %copy-done = bf16[2048,4096]{1,0:T(8,128)(2,1)S(1)} copy-done((bf16[2048,4096]{1,0:T(8,128)(2,1)S(1)}, bf16[2048,4096]{1,0:T(8,128)(2,1)}, u32[]{:S(2)}) %copy-start) | copy-done | bytes 16777240
  7.9 5.8 %select_rows.1 = (bf16[4,256,512]{2,1,0:T(8,128)(2,1)S(1)}, bf16[4,256,512]{2,1,0:T(8,128)(2,1)S(1)}) custom-call(s32[256]{0:T(256)S(1)} %copy-done.6, s32[2]{0:T(128)S(1)} %pad_add_fusion.place, f32[1,4096]{1,0:T(1,128)S(1)} %bitcast.110, bf16[2048,4096]{1,0:T(8,128)(2,1)S(1)} %copy-done), custom_call_target="tpu_custom_call" | custom-call | flops 4000000 | bytes 4000000 | tf_op jit(solution)/shard_map/select_rows/pallas_call | solution.py:95
  17.7 3.3 %collective-permute-start.1 = (bf16[256,512]{1,0:T(8,128)(2,1)S(1)}, bf16[256,512]{1,0:T(8,128)(2,1)S(1)}, u32[]{:S(2)}, u32[]{:S(2)}) collective-permute-start(bf16[256,512]{1,0:T(8,128)(2,1)S(1)} %get-tuple-element.26), channel_id=1, source_target_pairs={{0,8},{4,12},{8,0},{12,4},{16,24},{20,28},{24,16},{28,20},{1,9},{5... | collective-permute-start | bytes 786440 | tf_op jit(solution)/shard_map/ppermute | solution.py:32
  22.9 5.2 %collective-permute-done.1 = bf16[256,512]{1,0:T(8,128)(2,1)S(1)} collective-permute-done((bf16[256,512]{1,0:T(8,128)(2,1)S(1)}, bf16[256,512]{1,0:T(8,128)(2,1)S(1)}, u32[]{:S(2)}, u32[]{:S(2)}) %collective-permute-start.1) | collective-permute-done | bytes 262176 | tf_op jit(solution)/shard_map/ppermute | solution.py:32
  28.1 6.7 %collective-permute-done.2 = bf16[256,512]{1,0:T(8,128)(2,1)S(1)} collective-permute-done((bf16[256,512]{1,0:T(8,128)(2,1)S(1)}, bf16[256,512]{1,0:T(8,128)(2,1)S(1)}, u32[]{:S(2)}, u32[]{:S(2)}) %collective-permute-start.2) | collective-permute-done | bytes 262176 | tf_op jit(solution)/shard_map/ppermute | solution.py:32
  35.0 4.1 %collective-permute-start.4 = (bf16[256,512]{1,0:T(8,128)(2,1)S(1)}, bf16[256,512]{1,0:T(8,128)(2,1)S(1)}, u32[]{:S(2)}, u32[]{:S(2)}) collective-permute-start(bf16[256,512]{1,0:T(8,128)(2,1)S(1)} %fusion.5), channel_id=1, source_target_pairs={{0,1},{1,0},{2,3},{3,2},{4,5},{5,4},{6,7},{7,6},{8,9},{9,8},{10,11... | collective-permute-start | bytes 786440 | tf_op jit(solution)/shard_map/ppermute | solution.py:32
  39.0 5.7 %collective-permute-done.4 = bf16[256,512]{1,0:T(8,128)(2,1)S(1)} collective-permute-done((bf16[256,512]{1,0:T(8,128)(2,1)S(1)}, bf16[256,512]{1,0:T(8,128)(2,1)S(1)}, u32[]{:S(2)}, u32[]{:S(2)}) %collective-permute-start.4) | collective-permute-done | bytes 262176 | tf_op jit(solution)/shard_map/ppermute | solution.py:32
  44.8 3.7 %collective-permute-start.5 = (bf16[256,512]{1,0:T(8,128)(2,1)S(1)}, bf16[256,512]{1,0:T(8,128)(2,1)S(1)}, u32[]{:S(2)}, u32[]{:S(2)}) collective-permute-start(bf16[256,512]{1,0:T(8,128)(2,1)S(1)} %add.94), channel_id=1, source_target_pairs={{0,2},{1,3},{2,0},{3,1},{4,6},{5,7},{6,4},{7,5},{8,10},{9,11},{10,... | collective-permute-start | bytes 786440 | tf_op jit(solution)/shard_map/ppermute | solution.py:32
  48.6 10.6 %collective-permute-done.5 = bf16[256,512]{1,0:T(8,128)(2,1)S(1)} collective-permute-done((bf16[256,512]{1,0:T(8,128)(2,1)S(1)}, bf16[256,512]{1,0:T(8,128)(2,1)S(1)}, u32[]{:S(2)}, u32[]{:S(2)}) %collective-permute-start.5) | collective-permute-done | bytes 262176 | tf_op jit(solution)/shard_map/ppermute | solution.py:32
  59.2 4.2 %reference_partials.1 = (f32[4,2,224,256]{3,2,1,0:T(8,128)S(1)}, bf16[4,2,224,256]{3,2,1,0:T(8,128)(2,1)S(1)}) custom-call(s32[2]{0:T(128)S(1)} %pad_add_fusion.place, bf16[256,512]{1,0:T(8,128)(2,1)S(1)} %add.95.rows.refs_0_, bf16[512,1792]{1,0:T(8,128)(2,1)S(1)} %copy-done.3, bf16[512,1792]{1,0:T(8,128)(2,1)S(1)} %copy-done.4), custom_call_target="tpu_custom_call" | custom-call | flops 939524096 | bytes 3670016 | tf_op jit(solution)/shard_map/reference_partials/pallas_call | solution.py:186
  69.0 3.6 %collective-permute-done.19.refs_2_ = bf16[256,512]{1,0:T(8,128)(2,1)S(1)} collective-permute-done((bf16[256,512]{1,0:T(8,128)(2,1)S(1)}, bf16[256,512]{1,0:T(8,128)(2,1)S(1)}, u32[]{:S(2)}, u32[]{:S(2)}) %collective-permute-start.19) | collective-permute-done | bytes 262176 | tf_op jit(solution)/shard_map/ppermute | solution.py:32
  73.6 6.0 %collective-permute-done.21.refs_4_ = bf16[256,512]{1,0:T(8,128)(2,1)S(1)} collective-permute-done((bf16[256,512]{1,0:T(8,128)(2,1)S(1)}, bf16[256,512]{1,0:T(8,128)(2,1)S(1)}, u32[]{:S(2)}, u32[]{:S(2)}) %collective-permute-start.21) | collective-permute-done | bytes 262176 | tf_op jit(solution)/shard_map/ppermute | solution.py:32
  80.1 3.1 %collective-permute-done.7 = bf16[2,224,256]{2,1,0:T(8,128)(2,1)S(1)} collective-permute-done((bf16[2,224,256]{2,1,0:T(8,128)(2,1)S(1)}, bf16[2,224,256]{2,1,0:T(8,128)(2,1)S(1)}, u32[]{:S(2)}, u32[]{:S(2)}) %collective-permute-start.7) | collective-permute-done | bytes 229408 | tf_op jit(solution)/shard_map/ppermute | solution.py:32
  83.2 5.4 %collective-permute-done.8 = bf16[2,224,256]{2,1,0:T(8,128)(2,1)S(1)} collective-permute-done((bf16[2,224,256]{2,1,0:T(8,128)(2,1)S(1)}, bf16[2,224,256]{2,1,0:T(8,128)(2,1)S(1)}, u32[]{:S(2)}, u32[]{:S(2)}) %collective-permute-start.8) | collective-permute-done | bytes 229408 | tf_op jit(solution)/shard_map/ppermute | solution.py:32
  89.5 8.8 %collective-permute-done.10 = bf16[224,256]{1,0:T(8,128)(2,1)S(1)} collective-permute-done((bf16[224,256]{1,0:T(8,128)(2,1)S(1)}, bf16[224,256]{1,0:T(8,128)(2,1)S(1)}, u32[]{:S(2)}, u32[]{:S(2)}) %collective-permute-start.10) | collective-permute-done | bytes 114720 | tf_op jit(solution)/shard_map/ppermute | solution.py:32
  101.9 14.7 %client_activations.1.columns = bf16[256,1792]{1,0:T(8,128)(2,1)S(1)} custom-call(s32[2]{0:T(128)S(1)} %pad_add_fusion.place, bf16[256,512]{1,0:T(8,128)(2,1)S(1)} %add.95.rows.refs_0_, bf16[256,512]{1,0:T(8,128)(2,1)S(1)} %collective-permute-done.18.refs_1_, bf16[256,512]{1,0:T(8,128)(2,1)S(1)} %collective-permute-done.19.refs_2_, ...), custom_call_target="tpu_custom_call" | custom-call | flops 7516192768 | bytes 29360128 | tf_op jit(solution)/shard_map/client_activations/pallas_call | solution.py:146
  119.1 10.7 %match.2 = (f32[3584,256]{1,0:T(8,128)S(1)}, f32[2,3584,1]{2,1,0:T(8,128)S(1)}) custom-call(bf16[3584,256]{1,0:T(8,128)(2,1)S(1)} %bitcast.108, bf16[256,1792]{1,0:T(8,128)(2,1)S(1)} %client_activations.1.columns), custom_call_target="tpu_custom_call" | custom-call | flops 6576668672 | bytes 7340032 | tf_op jit(solution)/shard_map/match/pallas_call | solution.py:229
  131.6 7.0 %collective-permute-done.25.columns = bf16[256,1792]{1,0:T(8,128)(2,1)S(1)} collective-permute-done((bf16[256,1792]{1,0:T(8,128)(2,1)S(1)}, bf16[256,1792]{1,0:T(8,128)(2,1)S(1)}, u32[]{:S(2)}, u32[]{:S(2)}) %collective-permute-start.25) | collective-permute-done | bytes 917536 | tf_op jit(solution)/shard_map/ppermute | solution.py:32
  138.5 10.6 %match.3 = (f32[3584,256]{1,0:T(8,128)S(1)}, f32[2,3584,1]{2,1,0:T(8,128)S(1)}) custom-call(bf16[3584,256]{1,0:T(8,128)(2,1)S(1)} %bitcast.109, bf16[256,1792]{1,0:T(8,128)(2,1)S(1)} %collective-permute-done.25.columns), custom_call_target="tpu_custom_call" | custom-call | flops 6576668672 | bytes 7340032 | tf_op jit(solution)/shard_map/match/pallas_call | solution.py:229
  152.2 5.5 %add.106 = f32[3584,256]{1,0:T(8,128)} add(f32[3584,256]{1,0:T(8,128)} %copy-done.1, f32[3584,256]{1,0:T(8,128)} %copy-done.2) | non-fusion elementwise | flops 917504 | bytes 11010048 | tf_op jit(solution)/shard_map/add | solution.py:326
  166.8 5.0 %collective-permute-done.28 = bf16[2,224,256]{2,1,0:T(8,128)(2,1)S(1)} collective-permute-done((bf16[2,224,256]{2,1,0:T(8,128)(2,1)S(1)}, bf16[2,224,256]{2,1,0:T(8,128)(2,1)S(1)}, u32[]{:S(2)}, u32[]{:S(2)}) %collective-permute-start.28) | collective-permute-done | bytes 229408 | tf_op jit(solution)/shard_map/ppermute | solution.py:32
  171.8 4.6 %collective-permute-done.29 = bf16[2,224,256]{2,1,0:T(8,128)(2,1)S(1)} collective-permute-done((bf16[2,224,256]{2,1,0:T(8,128)(2,1)S(1)}, bf16[2,224,256]{2,1,0:T(8,128)(2,1)S(1)}, u32[]{:S(2)}, u32[]{:S(2)}) %collective-permute-start.29) | collective-permute-done | bytes 229408 | tf_op jit(solution)/shard_map/ppermute | solution.py:32
  176.4 3.0 %collective-permute-start.31 = (bf16[224,256]{1,0:T(8,128)(2,1)S(1)}, bf16[224,256]{1,0:T(8,128)(2,1)S(1)}, u32[]{:S(2)}, u32[]{:S(2)}) collective-permute-start(bf16[224,256]{1,0:T(8,128)(2,1)S(1)} %fusion.16), channel_id=1, source_target_pairs={{0,2},{1,3},{2,0},{3,1},{4,6},{5,7},{6,4},{7,5},{8,10},{9,11},{10,... | collective-permute-start | bytes 344072 | tf_op jit(solution)/shard_map/ppermute | solution.py:32
  179.4 4.5 %collective-permute-done.31 = bf16[224,256]{1,0:T(8,128)(2,1)S(1)} collective-permute-done((bf16[224,256]{1,0:T(8,128)(2,1)S(1)}, bf16[224,256]{1,0:T(8,128)(2,1)S(1)}, u32[]{:S(2)}, u32[]{:S(2)}) %collective-permute-start.31) | collective-permute-done | bytes 114720 | tf_op jit(solution)/shard_map/ppermute | solution.py:32
  (120 shorter events, 46.9 us)
Async XLA Ops:
  17.7 10.4 %collective-permute-start.1 = (bf16[256,512]{1,0:T(8,128)(2,1)S(1)}, bf16[256,512]{1,0:T(8,128)(2,1)S(1)}, u32[]{:S(2)}, u32[]{:S(2)}) collective-permute-start(bf16[256,512]{1,0:T(8,128)(2,1)S(1)} %get-tuple-element.26), channel_id=1, source_target_pairs={{0,8},{4,12},{8,0},{12,4},{16,24},{20,28},{24,16},{28,20},{1,9},{5... | collective-permute-start | bytes 786440 | tf_op jit(solution)/shard_map/ppermute | solution.py:32
  21.0 13.8 %collective-permute-start.2 = (bf16[256,512]{1,0:T(8,128)(2,1)S(1)}, bf16[256,512]{1,0:T(8,128)(2,1)S(1)}, u32[]{:S(2)}, u32[]{:S(2)}) collective-permute-start(bf16[256,512]{1,0:T(8,128)(2,1)S(1)} %get-tuple-element.28), channel_id=1, source_target_pairs={{0,16},{4,20},{8,24},{12,28},{16,0},{20,4},{24,8},{28,12},{1,17},{... | collective-permute-start | bytes 786440 | tf_op jit(solution)/shard_map/ppermute | solution.py:32
  22.9 11.9 %collective-permute-start.3 = (bf16[256,512]{1,0:T(8,128)(2,1)S(1)}, bf16[256,512]{1,0:T(8,128)(2,1)S(1)}, u32[]{:S(2)}, u32[]{:S(2)}) collective-permute-start(bf16[256,512]{1,0:T(8,128)(2,1)S(1)} %get-tuple-element.27), channel_id=1, source_target_pairs={{0,24},{4,28},{8,16},{12,20},{16,8},{20,12},{24,0},{28,4},{1,25},{... | collective-permute-start | bytes 786440 | tf_op jit(solution)/shard_map/ppermute | solution.py:32
  35.0 9.8 %collective-permute-start.4 = (bf16[256,512]{1,0:T(8,128)(2,1)S(1)}, bf16[256,512]{1,0:T(8,128)(2,1)S(1)}, u32[]{:S(2)}, u32[]{:S(2)}) collective-permute-start(bf16[256,512]{1,0:T(8,128)(2,1)S(1)} %fusion.5), channel_id=1, source_target_pairs={{0,1},{1,0},{2,3},{3,2},{4,5},{5,4},{6,7},{7,6},{8,9},{9,8},{10,11... | collective-permute-start | bytes 786440 | tf_op jit(solution)/shard_map/ppermute | solution.py:32
  44.8 14.3 %collective-permute-start.5 = (bf16[256,512]{1,0:T(8,128)(2,1)S(1)}, bf16[256,512]{1,0:T(8,128)(2,1)S(1)}, u32[]{:S(2)}, u32[]{:S(2)}) collective-permute-start(bf16[256,512]{1,0:T(8,128)(2,1)S(1)} %add.94), channel_id=1, source_target_pairs={{0,2},{1,3},{2,0},{3,1},{4,6},{5,7},{6,4},{7,5},{8,10},{9,11},{10,... | collective-permute-start | bytes 786440 | tf_op jit(solution)/shard_map/ppermute | solution.py:32
  63.5 9.2 %collective-permute-start.19 = (bf16[256,512]{1,0:T(8,128)(2,1)S(1)}, bf16[256,512]{1,0:T(8,128)(2,1)S(1)}, u32[]{:S(2)}, u32[]{:S(2)}) collective-permute-start(bf16[256,512]{1,0:T(8,128)(2,1)S(1)} %add.95.rows.refs_0_), channel_id=1, source_target_pairs={{0,8},{4,12},{8,0},{12,4},{16,24},{20,28},{24,16},{28,20},{1,9},{5... | collective-permute-start | bytes 786440 | tf_op jit(solution)/shard_map/ppermute | solution.py:32
  64.8 14.8 %collective-permute-start.21 = (bf16[256,512]{1,0:T(8,128)(2,1)S(1)}, bf16[256,512]{1,0:T(8,128)(2,1)S(1)}, u32[]{:S(2)}, u32[]{:S(2)}) collective-permute-start(bf16[256,512]{1,0:T(8,128)(2,1)S(1)} %add.95.rows.refs_0_), channel_id=1, source_target_pairs={{0,16},{4,20},{8,24},{12,28},{16,0},{20,4},{24,8},{28,12},{1,17},{... | collective-permute-start | bytes 786440 | tf_op jit(solution)/shard_map/ppermute | solution.py:32
  65.1 14.6 %collective-permute-start.23 = (bf16[256,512]{1,0:T(8,128)(2,1)S(1)}, bf16[256,512]{1,0:T(8,128)(2,1)S(1)}, u32[]{:S(2)}, u32[]{:S(2)}) collective-permute-start(bf16[256,512]{1,0:T(8,128)(2,1)S(1)} %add.95.rows.refs_0_), channel_id=1, source_target_pairs={{0,24},{4,28},{8,16},{12,20},{16,8},{20,12},{24,0},{28,4},{1,25},{... | collective-permute-start | bytes 786440 | tf_op jit(solution)/shard_map/ppermute | solution.py:32
  67.4 15.8 %collective-permute-start.7 = (bf16[2,224,256]{2,1,0:T(8,128)(2,1)S(1)}, bf16[2,224,256]{2,1,0:T(8,128)(2,1)S(1)}, u32[]{:S(2)}, u32[]{:S(2)}) collective-permute-start(bf16[2,224,256]{2,1,0:T(8,128)(2,1)S(1)} %get-tuple-element.32), channel_id=1, source_target_pairs={{0,8},{4,12},{8,0},{12,4},{16,24},{20,28},{24,16},{28,20},{1,9},{5... | collective-permute-start | bytes 688136 | tf_op jit(solution)/shard_map/ppermute | solution.py:32
  68.8 19.9 %collective-permute-start.8 = (bf16[2,224,256]{2,1,0:T(8,128)(2,1)S(1)}, bf16[2,224,256]{2,1,0:T(8,128)(2,1)S(1)}, u32[]{:S(2)}, u32[]{:S(2)}) collective-permute-start(bf16[2,224,256]{2,1,0:T(8,128)(2,1)S(1)} %get-tuple-element.34), channel_id=1, source_target_pairs={{0,16},{4,20},{8,24},{12,28},{16,0},{20,4},{24,8},{28,12},{1,17},{... | collective-permute-start | bytes 688136 | tf_op jit(solution)/shard_map/ppermute | solution.py:32
  72.6 16.0 %collective-permute-start.9 = (bf16[2,224,256]{2,1,0:T(8,128)(2,1)S(1)}, bf16[2,224,256]{2,1,0:T(8,128)(2,1)S(1)}, u32[]{:S(2)}, u32[]{:S(2)}) collective-permute-start(bf16[2,224,256]{2,1,0:T(8,128)(2,1)S(1)} %get-tuple-element.33), channel_id=1, source_target_pairs={{0,24},{4,28},{8,16},{12,20},{16,8},{20,12},{24,0},{28,4},{1,25},{... | collective-permute-start | bytes 688136 | tf_op jit(solution)/shard_map/ppermute | solution.py:32
  79.6 18.8 %collective-permute-start.18 = (bf16[256,512]{1,0:T(8,128)(2,1)S(1)}, bf16[256,512]{1,0:T(8,128)(2,1)S(1)}, u32[]{:S(2)}, u32[]{:S(2)}) collective-permute-start(bf16[256,512]{1,0:T(8,128)(2,1)S(1)} %add.95.rows.refs_0_), channel_id=1, source_target_pairs={{0,4},{4,0},{8,12},{12,8},{16,20},{20,16},{24,28},{28,24},{1,5},{5... | collective-permute-start | bytes 786440 | tf_op jit(solution)/shard_map/ppermute | solution.py:32
  79.6 19.5 %collective-permute-start.20 = (bf16[256,512]{1,0:T(8,128)(2,1)S(1)}, bf16[256,512]{1,0:T(8,128)(2,1)S(1)}, u32[]{:S(2)}, u32[]{:S(2)}) collective-permute-start(bf16[256,512]{1,0:T(8,128)(2,1)S(1)} %collective-permute-done.19.refs_2_), channel_id=1, source_target_pairs={{0,4},{4,0},{8,12},{12,8},{16,20},{20,16},{24,28},{28,24},{1,5},{5... | collective-permute-start | bytes 786440 | tf_op jit(solution)/shard_map/ppermute | solution.py:32
  83.2 16.2 %collective-permute-start.22 = (bf16[256,512]{1,0:T(8,128)(2,1)S(1)}, bf16[256,512]{1,0:T(8,128)(2,1)S(1)}, u32[]{:S(2)}, u32[]{:S(2)}) collective-permute-start(bf16[256,512]{1,0:T(8,128)(2,1)S(1)} %collective-permute-done.21.refs_4_), channel_id=1, source_target_pairs={{0,4},{4,0},{8,12},{12,8},{16,20},{20,16},{24,28},{28,24},{1,5},{5... | collective-permute-start | bytes 786440 | tf_op jit(solution)/shard_map/ppermute | solution.py:32
  88.7 13.3 %collective-permute-start.24 = (bf16[256,512]{1,0:T(8,128)(2,1)S(1)}, bf16[256,512]{1,0:T(8,128)(2,1)S(1)}, u32[]{:S(2)}, u32[]{:S(2)}) collective-permute-start(bf16[256,512]{1,0:T(8,128)(2,1)S(1)} %collective-permute-done.23.refs_6_), channel_id=1, source_target_pairs={{0,4},{4,0},{8,12},{12,8},{16,20},{20,16},{24,28},{28,24},{1,5},{5... | collective-permute-start | bytes 786440 | tf_op jit(solution)/shard_map/ppermute | solution.py:32
  89.3 9.0 %collective-permute-start.10 = (bf16[224,256]{1,0:T(8,128)(2,1)S(1)}, bf16[224,256]{1,0:T(8,128)(2,1)S(1)}, u32[]{:S(2)}, u32[]{:S(2)}) collective-permute-start(bf16[224,256]{1,0:T(8,128)(2,1)S(1)} %multiply_convert_fusion), channel_id=1, source_target_pairs={{0,2},{1,3},{2,0},{3,1},{4,6},{5,7},{6,4},{7,5},{8,10},{9,11},{10,... | collective-permute-start | bytes 344072 | tf_op jit(solution)/shard_map/ppermute | solution.py:32
  98.3 19.1 %collective-permute-start.11 = (bf16[2,224,256]{2,1,0:T(8,128)(2,1)S(1)}, bf16[2,224,256]{2,1,0:T(8,128)(2,1)S(1)}, u32[]{:S(2)}, u32[]{:S(2)}) collective-permute-start(bf16[2,224,256]{2,1,0:T(8,128)(2,1)S(1)} %pad_maximum_fusion), channel_id=1, source_target_pairs={{0,4},{4,0},{8,12},{12,8},{16,20},{20,16},{24,28},{28,24},{1,5},{5... | collective-permute-start | bytes 688136 | tf_op jit(solution)/shard_map/ppermute | solution.py:32
  98.4 18.3 %collective-permute-start.12 = (bf16[2,224,256]{2,1,0:T(8,128)(2,1)S(1)}, bf16[2,224,256]{2,1,0:T(8,128)(2,1)S(1)}, u32[]{:S(2)}, u32[]{:S(2)}) collective-permute-start(bf16[2,224,256]{2,1,0:T(8,128)(2,1)S(1)} %pad_maximum_fusion), channel_id=1, source_target_pairs={{0,8},{4,12},{8,0},{12,4},{16,24},{20,28},{24,16},{28,20},{1,9},{5... | collective-permute-start | bytes 688136 | tf_op jit(solution)/shard_map/ppermute | solution.py:32
  99.2 17.6 %collective-permute-start.14 = (bf16[2,224,256]{2,1,0:T(8,128)(2,1)S(1)}, bf16[2,224,256]{2,1,0:T(8,128)(2,1)S(1)}, u32[]{:S(2)}, u32[]{:S(2)}) collective-permute-start(bf16[2,224,256]{2,1,0:T(8,128)(2,1)S(1)} %pad_maximum_fusion), channel_id=1, source_target_pairs={{0,16},{4,20},{8,24},{12,28},{16,0},{20,4},{24,8},{28,12},{1,17},{... | collective-permute-start | bytes 688136 | tf_op jit(solution)/shard_map/ppermute | solution.py:32
  99.4 17.9 %collective-permute-start.16 = (bf16[2,224,256]{2,1,0:T(8,128)(2,1)S(1)}, bf16[2,224,256]{2,1,0:T(8,128)(2,1)S(1)}, u32[]{:S(2)}, u32[]{:S(2)}) collective-permute-start(bf16[2,224,256]{2,1,0:T(8,128)(2,1)S(1)} %pad_maximum_fusion), channel_id=1, source_target_pairs={{0,24},{4,28},{8,16},{12,20},{16,8},{20,12},{24,0},{28,4},{1,25},{... | collective-permute-start | bytes 688136 | tf_op jit(solution)/shard_map/ppermute | solution.py:32
  116.6 21.9 %collective-permute-start.25 = (bf16[256,1792]{1,0:T(8,128)(2,1)S(1)}, bf16[256,1792]{1,0:T(8,128)(2,1)S(1)}, u32[]{:S(2)}, u32[]{:S(2)}) collective-permute-start(bf16[256,1792]{1,0:T(8,128)(2,1)S(1)} %client_activations.1.columns), channel_id=1, source_target_pairs={{0,1},{1,0},{2,3},{3,2},{4,5},{5,4},{6,7},{7,6},{8,9},{9,8},{10,11... | collective-permute-start | bytes 2752520 | tf_op jit(solution)/shard_map/ppermute | solution.py:32
  163.2 8.5 %collective-permute-start.28 = (bf16[2,224,256]{2,1,0:T(8,128)(2,1)S(1)}, bf16[2,224,256]{2,1,0:T(8,128)(2,1)S(1)}, u32[]{:S(2)}, u32[]{:S(2)}) collective-permute-start(bf16[2,224,256]{2,1,0:T(8,128)(2,1)S(1)} %get-tuple-element.29), channel_id=1, source_target_pairs={{0,8},{4,12},{8,0},{12,4},{16,24},{20,28},{24,16},{28,20},{1,9},{5... | collective-permute-start | bytes 688136 | tf_op jit(solution)/shard_map/ppermute | solution.py:32
  164.0 12.3 %collective-permute-start.29 = (bf16[2,224,256]{2,1,0:T(8,128)(2,1)S(1)}, bf16[2,224,256]{2,1,0:T(8,128)(2,1)S(1)}, u32[]{:S(2)}, u32[]{:S(2)}) collective-permute-start(bf16[2,224,256]{2,1,0:T(8,128)(2,1)S(1)} %get-tuple-element.31), channel_id=1, source_target_pairs={{0,16},{4,20},{8,24},{12,28},{16,0},{20,4},{24,8},{28,12},{1,17},{... | collective-permute-start | bytes 688136 | tf_op jit(solution)/shard_map/ppermute | solution.py:32
  164.4 11.9 %collective-permute-start.30 = (bf16[2,224,256]{2,1,0:T(8,128)(2,1)S(1)}, bf16[2,224,256]{2,1,0:T(8,128)(2,1)S(1)}, u32[]{:S(2)}, u32[]{:S(2)}) collective-permute-start(bf16[2,224,256]{2,1,0:T(8,128)(2,1)S(1)} %get-tuple-element.30), channel_id=1, source_target_pairs={{0,24},{4,28},{8,16},{12,20},{16,8},{20,12},{24,0},{28,4},{1,25},{... | collective-permute-start | bytes 688136 | tf_op jit(solution)/shard_map/ppermute | solution.py:32
  (22 other events, 152.5 us)

commit v2 on v1

--- a/solution.py
+++ b/solution.py
@@ -16,6 +16,7 @@
 whole = pl.BlockSpec(memory_space=pltpu.VMEM)
 scalars = pl.BlockSpec(memory_space=pltpu.SMEM)
 anywhere = pl.BlockSpec(memory_space=pl.ANY)
+in_hbm = pl.BlockSpec(memory_space=pltpu.HBM)
 
 
 def vmem_params(mib):
@@ -40,13 +41,8 @@
 
     def note(t, count):
         local = ids[t] - start
-        mine = jnp.logical_and(local >= 0, local < rows_here)
-
-        @pl.when(mine)
-        def _():
-            held[count] = t
-
-        return count + jnp.where(mine, 1, 0)
+        held[count] = t
+        return count + jnp.logical_and(local >= 0, local < rows_here).astype(jnp.int32)
 
     def fetch(k):
         t = held[k]
@@ -56,7 +52,7 @@
             table.at[pl.ds(group, group_rows), :], slots.at[slot], sems.at[slot]
         )
 
-    count = lax.fori_loop(0, tokens, note, jnp.int32(0))
+    count = lax.fori_loop(0, tokens, note, jnp.int32(0), unroll=8)
 
     def begin(k, carry):
         fetch(k).start()
@@ -95,15 +91,15 @@
     return pl.pallas_call(
         select_kernel,
         out_shape=(half, half),
-        in_specs=[scalars, scalars, whole, anywhere],
+        in_specs=[scalars, scalars, whole, in_hbm],
         out_specs=(whole, whole),
         scratch_shapes=[
             pltpu.VMEM((tokens, width), f32),
-            pltpu.SMEM((tokens,), jnp.int32),
+            pltpu.SMEM((tokens + 1,), jnp.int32),
             pltpu.VMEM((fetch_slots, group_rows, width), bf16),
             pltpu.SemaphoreType.DMA((fetch_slots,)),
         ],
-        compiler_params=vmem_params(24),
+        compiler_params=vmem_params(48),
         cost_estimate=cost(4e6, 4e6),
         name="select_rows",
     )(token_ids, place, norm_gain[None, :], embed_table)
@@ -121,37 +117,35 @@
     return gate / (1.0 + jnp.exp(-gate)) * up
 
 
-def client_kernel(place, *refs):
+def client_kernel(first, place, *refs):
     *blocks, gate_w, up_w, out = refs
     client = place[1]
-    span = blocks[0].shape[1]
-    gate = jnp.zeros(out.shape, f32)
-    up = jnp.zeros(out.shape, f32)
-    for p, block in enumerate(blocks):
-        at = pl.ds(pl.multiple_of((client ^ p) * span, span), span)
-        gate += jnp.dot(block[...], gate_w[0, at, :], preferred_element_type=f32)
-        up += jnp.dot(block[...], up_w[0, at, :], preferred_element_type=f32)
-    out[...] = standardized(gated(gate, up), 0)
+    tokens, span = blocks[0].shape
+    wide = unit_block(gate_w.shape[2])
+    for at in range(0, out.shape[1], wide):
+        units = slice(first + at, first + at + wide)
+        gate = jnp.zeros((tokens, wide), f32)
+        up = jnp.zeros((tokens, wide), f32)
+        for p, block in enumerate(blocks):
+            features = pl.ds(pl.multiple_of((client ^ p) * span, span), span)
+            gate += jnp.dot(block[...], gate_w[0, features, units], preferred_element_type=f32)
+            up += jnp.dot(block[...], up_w[0, features, units], preferred_element_type=f32)
+        out[:, at : at + wide] = standardized(gated(gate, up), 0)
 
 
 def unit_block(units, most=256):
     return most if units % most == 0 else most // 2
 
 
-def client_activations(place, blocks, client_gate, client_up):
-    tokens, span = blocks[0].shape
-    _, width, units = client_gate.shape
-    wide = unit_block(units)
-    weights = pl.BlockSpec((1, width, wide), lambda i: (0, 0, i))
-    return pl.pallas_call(
-        client_kernel,
-        grid=(units // wide,),
+def client_activations(place, blocks, client_gate, client_up, first, last):
+    tokens = blocks[0].shape[0]
+    width, units = client_gate.shape[1], last - first
+    return pl.pallas_call(
+        functools.partial(client_kernel, first),
         out_shape=jax.ShapeDtypeStruct((tokens, units), bf16),
-        in_specs=[scalars]
-        + [pl.BlockSpec((tokens, span), lambda i: (0, 0))] * len(blocks)
-        + [weights, weights],
-        out_specs=pl.BlockSpec((tokens, wide), lambda i: (0, i)),
-        compiler_params=vmem_params(40),
+        in_specs=[scalars] + [whole] * (len(blocks) + 2),
+        out_specs=whole,
+        compiler_params=vmem_params(8),
         cost_estimate=cost(4 * tokens * width * units, 4 * width * units),
         name="client_activations",
     )(place, *blocks, client_gate, client_up)
@@ -190,62 +184,116 @@
         in_specs=[scalars, pl.BlockSpec((tokens, span), lambda i: (0, 0)), weights, weights],
         out_specs=(pieces, pieces),
         scratch_shapes=[pltpu.VMEM((2, units, tokens), f32)],
-        compiler_params=vmem_params(32),
+        compiler_params=vmem_params(18),
         cost_estimate=cost(4 * tokens * span * units, 4 * span * units),
         name="reference_partials",
     )(place, rows, ref_gate, ref_up)
 
 
-def match_kernel(refs, columns, numerator, sums, turned):
-    tokens, units = columns.shape
-    wide = unit_block(units)
-
-    @pl.when(pl.program_id(0) == 0)
-    def _():
-        for i in range(0, units, wide):
-            turned[i : i + wide, :] = columns[:, i : i + wide].T
-
+def match_kernel(sources, *args):
+    refs, *rest = args
+    columns, rest = rest[:sources], rest[sources:]
+    numerator, sums = rest[-2:]
+    tokens = refs.shape[1]
     rows = refs[...]
-    total = jnp.zeros(numerator.shape, f32)
+    if len(rest) > 2:
+        total = rest[0][...]
+    else:
+        total = jnp.zeros(numerator.shape, f32)
     colsum = jnp.zeros((rows.shape[0], 128), f32)
     weighted = jnp.zeros((rows.shape[0], 128), f32)
-    for i in range(0, units, wide):
-        r = jnp.dot(rows, columns[:, i : i + wide], preferred_element_type=f32)
-        w = jnp.exp2(r * (sharpness * log2_e / tokens))
-        total += jnp.dot(w.astype(bf16), turned[i : i + wide, :], preferred_element_type=f32)
-        wr = w * r
-        for k in range(0, wide, 128):
-            colsum += w[:, k : k + 128]
-            weighted += wr[:, k : k + 128]
+    for source in columns:
+        wide = unit_block(source.shape[1])
+        for i in range(0, source.shape[1], wide):
+            some = source[:, i : i + wide]
+            r = jnp.dot(rows, some, preferred_element_type=f32)
+            w = jnp.exp2(r * (sharpness * log2_e / tokens))
+            total += lax.dot_general(
+                w.astype(bf16), some, (((1,), (1,)), ((), ())), preferred_element_type=f32
+            )
+            wr = w * r
+            for k in range(0, wide, 128):
+                colsum += w[:, k : k + 128]
+                weighted += wr[:, k : k + 128]
     numerator[...] = total
-    sums[0] = jnp.sum(colsum, axis=1, keepdims=True)
-    sums[1] = jnp.sum(weighted, axis=1, keepdims=True) * (1.0 / tokens)
-
-
-def match(refs, columns):
+    row = jnp.sum(colsum.T, axis=0, keepdims=True)
+    row_weighted = jnp.sum(weighted.T, axis=0, keepdims=True) * (1.0 / tokens)
+    if len(rest) > 2:
+        row = row + rest[1][0:1, :]
+        row_weighted = row_weighted + rest[1][1:2, :]
+    sums[0:1, :] = row
+    sums[1:2, :] = row_weighted
+
+
+def match(refs, columns, before=()):
     rows, tokens = refs.shape
-    units = columns.shape[1]
-    high = 512
-    return pl.pallas_call(
-        match_kernel,
+    units = sum(source.shape[1] for source in columns)
+    high = 896
+    numerators = pl.BlockSpec((high, tokens), lambda j: (j, 0))
+    sums = pl.BlockSpec((2, high), lambda j: (0, j))
+    return pl.pallas_call(
+        functools.partial(match_kernel, len(columns)),
         grid=(rows // high,),
         out_shape=(
             jax.ShapeDtypeStruct((rows, tokens), f32),
-            jax.ShapeDtypeStruct((2, rows, 1), f32),
+            jax.ShapeDtypeStruct((2, rows), f32),
         ),
-        in_specs=[
-            pl.BlockSpec((high, tokens), lambda j: (j, 0)),
-            pl.BlockSpec((tokens, units), lambda j: (0, 0)),
-        ],
-        out_specs=(
-            pl.BlockSpec((high, tokens), lambda j: (j, 0)),
-            pl.BlockSpec((2, high, 1), lambda j: (0, j, 0)),
-        ),
-        scratch_shapes=[pltpu.VMEM((units, tokens), bf16)],
-        compiler_params=vmem_params(32),
+        in_specs=[numerators]
+        + [pl.BlockSpec(source.shape, lambda j: (0, 0)) for source in columns]
+        + [numerators, sums][: len(before)],
+        out_specs=(numerators, sums),
+        compiler_params=vmem_params(20),
         cost_estimate=cost(4 * rows * units * tokens, 8 * rows * tokens, rows * units),
         name="match",
-    )(refs, columns)
+    )(refs, *columns, *before)
+
+
+def scale_kernel(numerator, factor, keep, send):
+    pieces, size = 2 * keep.shape[0], keep.shape[2]
+    lanes = 128
+    by_row = jnp.broadcast_to(factor[...], (lanes, pieces * size)).T
+    for p in range(pieces):
+        target = send if p % 2 else keep
+        units = slice(p * size, (p + 1) * size)
+        for k in range(0, numerator.shape[1], lanes):
+            target[p // 2, 0, :, k : k + lanes] = (
+                numerator[units, k : k + lanes] * by_row[units]
+            ).astype(target.dtype)
+
+
+def scaled(numerator, factor, clients, groups):
+    rows, tokens = numerator.shape
+    units = rows // groups
+    shape = (clients // 2, groups, units // clients, tokens)
+    pieces = pl.BlockSpec((shape[0], 1, shape[2], tokens), lambda g: (0, g, 0, 0))
+    return pl.pallas_call(
+        scale_kernel,
+        grid=(groups,),
+        out_shape=(jax.ShapeDtypeStruct(shape, f32), jax.ShapeDtypeStruct(shape, bf16)),
+        in_specs=[
+            pl.BlockSpec((units, tokens), lambda g: (g, 0)),
+            pl.BlockSpec((1, units), lambda g: (0, g)),
+        ],
+        out_specs=(pieces, pieces),
+        compiler_params=vmem_params(20),
+        cost_estimate=cost(rows * tokens, 7 * rows * tokens),
+        name="scaled",
+    )(numerator, factor)
+
+
+def tie_kernel(value, *rest):
+    rest[-1][...] = value[...]
+
+
+def tied(value, *others):
+    return pl.pallas_call(
+        tie_kernel,
+        out_shape=jax.ShapeDtypeStruct(value.shape, value.dtype),
+        in_specs=[whole] + [anywhere] * len(others),
+        out_specs=whole,
+        compiler_params=vmem_params(8),
+        name="tied",
+    )(value, *others)
 
 
 def place_kernel(place, *refs):
@@ -276,62 +324,78 @@
     over_clients = functools.partial(xor_permute, axis="client", size=clients)
     over_units = functools.partial(xor_permute, axis="unit", size=parts)
 
-    def gathered(own):
-        blocks = [None] * clients
-        for p in range(0, clients, 2):
-            blocks[p] = over_clients(own, mask=p) if p else own
+    def gathered(own, after=()):
+        blocks = [own] + [None] * (clients - 1)
+        far = tied(own, *after) if after else own
+        for p in range(2, clients, 2):
+            blocks[p] = over_clients(far, mask=p)
         for p in range(0, clients, 2):
             blocks[p + 1] = over_clients(blocks[p], mask=1)
         return blocks
 
-    def scattered(keep, send):
-        total = keep.astype(f32) + over_clients(send, mask=1).astype(f32)
-        arrived = [over_clients(total[p // 2].astype(bf16), mask=p) for p in range(2, clients, 2)]
+    def summed_pairs(keep, send):
+        return keep.astype(f32) + over_clients(send, mask=1).astype(f32)
+
+    def sent(total):
+        return [over_clients(total[p // 2].astype(bf16), mask=p) for p in range(2, clients, 2)]
+
+    def summed(total, arrived):
         mine = total[0]
         for other in arrived:
             mine = mine + other.astype(f32)
         return mine
 
     keep, send = select_rows(token_ids, place, norm_gain, embed_table, clients)
-    own_rows = scattered(keep, send).astype(bf16)
+    total = summed_pairs(keep, send)
+    half = total.shape[1] // 2
+    halves = [total[:, :half], total[:, half:]]
+    halves = [(part, sent(part)) for part in halves]
+    halves = [summed(*part).astype(bf16) for part in halves]
     bit = 1
     while bit < parts:
-        own_rows = own_rows + over_units(own_rows, mask=bit)
+        halves = [part + over_units(part, mask=bit) for part in halves]
         bit *= 2
-
-    blocks = gathered(own_rows)
+    own_rows = jnp.concatenate(halves, axis=0)
+
     ref_keep, ref_send = reference_partials(place, own_rows, ref_gate, ref_up, clients)
-    pre = scattered(ref_keep, ref_send)
+    total = summed_pairs(ref_keep, ref_send)
+    arrived = sent(total)
+    blocks = gathered(own_rows, [total])
+    pre = summed(total, arrived)
     ref_piece = standardized(gated(pre[0], pre[1]), 1)
     even = range(0, parts, 2)
+    groups, (piece, tokens) = len(even), ref_piece.shape
     ref_pieces = jnp.stack([over_units(ref_piece, mask=k) if k else ref_piece for k in even])
-    refs = jnp.stack(gathered(ref_pieces), axis=1)
-    groups, _, piece, tokens = refs.shape
-    refs = refs.reshape(groups * clients * piece, tokens)
-
-    columns = client_activations(place, blocks, client_gate, client_up)
-    other = over_units(columns, mask=1)
-    numerator_a, sums_a = match(refs, columns)
-    numerator_b, sums_b = match(refs, other)
-    sums = (sums_a + sums_b).reshape(2, groups, clients * piece)
+    refs = jnp.stack(gathered(ref_pieces), axis=1).reshape(groups * clients * piece, tokens)
+
+    units = client_gate.shape[2]
+    cuts = [0, 2 * units // 7, 5 * units // 7, units]
+    own = [
+        client_activations(place, blocks, client_gate, client_up, first, last)
+        for first, last in zip(cuts, cuts[1:])
+    ]
+    theirs = [over_units(part, mask=1) for part in own]
+    sofar = match(refs, own)
+    for part in theirs:
+        sofar = match(refs, [part], sofar)
+    numerator, sums = sofar
+    sums = sums.reshape(2, groups, clients * piece)
     all_sums = sums
     for k in even[1:]:
-        theirs = over_units(sums, mask=k)
-        all_sums = all_sums + jnp.stack([theirs[:, g ^ (k // 2)] for g in range(groups)], axis=1)
+        other = over_units(sums, mask=k)
+        all_sums = all_sums + jnp.stack([other[:, g ^ (k // 2)] for g in range(groups)], axis=1)
     colsum, weighted = all_sums[0], all_sums[1]
     score = (weighted[0] / colsum[0]).reshape(clients, piece)
-    score = score[jnp.arange(clients) ^ client].reshape(1, clients * piece)
-
-    inverse = (1.0 / clients) / colsum
-    numerator = (numerator_a + numerator_b).reshape(groups, clients * piece, tokens)
-    matched = (numerator * inverse[:, :, None]).astype(bf16)
-    matched = matched.reshape(groups, clients // 2, 2, piece, tokens)
-    summed = scattered(
-        matched[:, :, 0].transpose(1, 0, 2, 3), matched[:, :, 1].transpose(1, 0, 2, 3)
-    )
-    mine = summed[0]
+    here = jnp.arange(clients)[:, None] ^ client == jnp.arange(clients)[None, :]
+    score = jnp.sum(jnp.where(here[:, :, None], score[None], 0.0), axis=1)
+    score = score.reshape(1, clients * piece)
+
+    inverse = ((1.0 / clients) / colsum).reshape(1, groups * clients * piece)
+    total = summed_pairs(*scaled(numerator, inverse, clients, groups))
+    reduced = summed(total, sent(total))
+    mine = reduced[0]
     for k in even[1:]:
-        mine = mine + over_units(summed[k // 2].astype(bf16), mask=k).astype(f32)
+        mine = mine + over_units(reduced[k // 2].astype(bf16), mask=k).astype(f32)
     merged = placed(place, gathered(mine.astype(bf16)))
     return (merged, score)
 

time: 197 us -> 170 us (0.86)
  waiting for transfers between devices: 86.8 us -> 68.9 us
  starting transfers between devices: 35.6 us -> 45.1 us
  other arithmetic: 11.3 us -> 2.55 us
  Pallas kernels: 47.8 us -> 40.2 us
    ppermute x39 -> x46, waiting for transfers between devices: 86.8 us -> 68.9 us  [xor_permute(): return lax.ppermute(value, axis, [(i, i ^ mask) for i in range(size)])]
    ppermute x39 -> x46, starting transfers between devices: 35.6 us -> 45.1 us  [xor_permute(): return lax.ppermute(value, axis, [(i, i ^ mask) for i in range(size)])]
    add x7, other arithmetic: 6.98 us -> 0.41 us  [the longest x2 0.24 us: summed(): mine = mine + other.astype(f32)]
    pallas_call x3 -> x9, Pallas kernels: 36 us -> 30.7 us  [the longest x4 19.7 us: match(): pl.pallas_call(functools.partial(match_kernel, len(columns)), grid=(rows...]
    pallas_call x1, Pallas kernels: 5.8 us -> 3.25 us  [select_rows(): pl.pallas_call(select_kernel, out_shape=(half, half), in_specs=[scalars,...]
    convert_element_type x2 -> x1, other arithmetic: 2.54 us -> 0.14 us  [body(): halves = [summed(*part).astype(bf16) for part in halves]]
    unnamed x20 -> x29, local copies, waits for them, and re-layouts: 10.8 us -> 10.5 us
  transfers between devices with their start and end apart: 39 -> 46, of which waited for: 21 -> 26; matrix products, arithmetic and copies ran while one was open for 4% -> 1% of each run, Pallas kernels for 13% -> 16%
where the time goes in v2:
time: 170 us
  waiting for transfers between devices  68.9 us (41%)
  starting transfers between devices  45.1 us (27%)
  Pallas kernels  40.2 us (24%)
  local copies, waits for them, and re-layouts  11.6 us (7%)
  other arithmetic  2.55 us (1%)
    ppermute x46, waiting for transfers between devices, xor_permute(): return lax.ppermute(value, axis, [(i, i ^ mask) for i in range(size)])  68.9 us
    ppermute x46, starting transfers between devices, xor_permute(): return lax.ppermute(value, axis, [(i, i ^ mask) for i in range(size)])  45.1 us
    pallas_call x4, Pallas kernels, match(): pl.pallas_call(functools.partial(match_kernel, len(columns)), grid=(rows...  19.7 us
    unnamed x29, local copies, waits for them, and re-layouts  10.5 us
    pallas_call x3, Pallas kernels, client_activations(): pl.pallas_call(functools.partial(client_kernel, first), out_shape=jax.Sha...  10.1 us
    pallas_call x1, Pallas kernels, reference_partials(): pl.pallas_call(partial_kernel, grid=(units // wide,), out_shape=(jax.Shap...  4.37 us
  transfers between devices with their start and end apart: 46, of which 26 were waited for; matrix products, arithmetic and copies ran while one was open for 1% of the time, Pallas kernels for 16%

profile of v2, /device:TPU:0, one launch (start us, length us, event | category | flops | bytes accessed | tf_op | source)
XLA Modules:
  0.0 169.6 jit_solution(1215690545442511517)
XLA Ops:
  2.1 3.3 %select_rows.1 = (bf16[4,256,512]{2,1,0:T(8,128)(2,1)S(1)}, bf16[4,256,512]{2,1,0:T(8,128)(2,1)S(1)}) custom-call(s32[256]{0:T(256)S(1)} %copy-done.6, s32[2]{0:T(128)S(1)} %pad_add_fusion.place, f32[1,4096]{1,0:T(1,128)S(1)} %bitcast.114, bf16[2048,4096]{1,0:T(8,128)(2,1)} %table.1), custom_call_target="tpu_custom_call" | custom-call | flops 4000000 | bytes 4000000 | tf_op jit(solution)/shard_map/select_rows/pallas_call | solution.py:91
  9.5 2.9 %collective-permute-start.1 = (bf16[128,512]{1,0:T(8,128)(2,1)S(1)}, bf16[128,512]{1,0:T(8,128)(2,1)S(1)}, u32[]{:S(2)}, u32[]{:S(2)}) collective-permute-start(bf16[128,512]{1,0:T(8,128)(2,1)S(1)} %get-tuple-element.40), channel_id=1, source_target_pairs={{0,8},{4,12},{8,0},{12,4},{16,24},{20,28},{24,16},{28,20},{1,9},{5... | collective-permute-start | bytes 393224 | tf_op jit(solution)/shard_map/ppermute | solution.py:33
  28.9 4.1 %collective-permute-done.4 = bf16[128,512]{1,0:T(8,128)(2,1)S(1)} collective-permute-done((bf16[128,512]{1,0:T(8,128)(2,1)S(1)}, bf16[128,512]{1,0:T(8,128)(2,1)S(1)}, u32[]{:S(2)}, u32[]{:S(2)}) %collective-permute-start.4) | collective-permute-done | bytes 131104 | tf_op jit(solution)/shard_map/ppermute | solution.py:33
  33.1 5.3 %collective-permute-start.5 = (bf16[128,512]{1,0:T(8,128)(2,1)S(1)}, bf16[128,512]{1,0:T(8,128)(2,1)S(1)}, u32[]{:S(2)}, u32[]{:S(2)}) collective-permute-start(bf16[128,512]{1,0:T(8,128)(2,1)S(1)} %add.93), channel_id=1, source_target_pairs={{0,2},{1,3},{2,0},{3,1},{4,6},{5,7},{6,4},{7,5},{8,10},{9,11},{10,... | collective-permute-start | bytes 393224 | tf_op jit(solution)/shard_map/ppermute | solution.py:33
  38.4 2.8 %collective-permute-start.10 = (bf16[128,512]{1,0:T(8,128)(2,1)S(1)}, bf16[128,512]{1,0:T(8,128)(2,1)S(1)}, u32[]{:S(2)}, u32[]{:S(2)}) collective-permute-start(bf16[128,512]{1,0:T(8,128)(2,1)S(1)} %add.98), channel_id=1, source_target_pairs={{0,2},{1,3},{2,0},{3,1},{4,6},{5,7},{6,4},{7,5},{8,10},{9,11},{10,... | collective-permute-start | bytes 393224 | tf_op jit(solution)/shard_map/ppermute | solution.py:33
  41.2 5.5 %collective-permute-done.5 = bf16[128,512]{1,0:T(8,128)(2,1)S(1)} collective-permute-done((bf16[128,512]{1,0:T(8,128)(2,1)S(1)}, bf16[128,512]{1,0:T(8,128)(2,1)S(1)}, u32[]{:S(2)}, u32[]{:S(2)}) %collective-permute-start.5) | collective-permute-done | bytes 131104 | tf_op jit(solution)/shard_map/ppermute | solution.py:33
  48.2 4.4 %reference_partials.1 = (f32[4,2,224,256]{3,2,1,0:T(8,128)S(1)}, bf16[4,2,224,256]{3,2,1,0:T(8,128)(2,1)S(1)}) custom-call(s32[2]{0:T(128)S(1)} %pad_add_fusion.place, bf16[256,512]{1,0:T(8,128)(2,1)S(1)} %pad_maximum_fusion.rows.value.refs_0_, bf16[512,1792]{1,0:T(8,128)(2,1)S(1)} %copy-done.3, bf16[512,1792]{1,0:T(8,128)(2,1)S(1)} %copy-done.4), custom_call_target="tpu_custom_call" | custom-call | flops 939524096 | bytes 3670016 | tf_op jit(solution)/shard_map/reference_partials/pallas_call | solution.py:180
  52.6 2.5 %collective-permute-done.11 = bf16[4,2,224,256]{3,2,1,0:T(8,128)(2,1)S(1)} collective-permute-done((bf16[4,2,224,256]{3,2,1,0:T(8,128)(2,1)S(1)}, bf16[4,2,224,256]{3,2,1,0:T(8,128)(2,1)S(1)}, u32[]{:S(2)}, u32[]{:S(2)}) %collective-permute-start.11) | collective-permute-done | bytes 917536 | tf_op jit(solution)/shard_map/ppermute | solution.py:33
  59.8 4.2 %collective-permute-done.12 = bf16[2,224,256]{2,1,0:T(8,128)(2,1)S(1)} collective-permute-done((bf16[2,224,256]{2,1,0:T(8,128)(2,1)S(1)}, bf16[2,224,256]{2,1,0:T(8,128)(2,1)S(1)}, u32[]{:S(2)}, u32[]{:S(2)}) %collective-permute-start.12) | collective-permute-done | bytes 229408 | tf_op jit(solution)/shard_map/ppermute | solution.py:33
  64.0 4.9 %collective-permute-done.13 = bf16[2,224,256]{2,1,0:T(8,128)(2,1)S(1)} collective-permute-done((bf16[2,224,256]{2,1,0:T(8,128)(2,1)S(1)}, bf16[2,224,256]{2,1,0:T(8,128)(2,1)S(1)}, u32[]{:S(2)}, u32[]{:S(2)}) %collective-permute-start.13) | collective-permute-done | bytes 229408 | tf_op jit(solution)/shard_map/ppermute | solution.py:33
  69.6 4.9 %collective-permute-done.24.refs_2_ = bf16[256,512]{1,0:T(8,128)(2,1)S(1)} collective-permute-done((bf16[256,512]{1,0:T(8,128)(2,1)S(1)}, bf16[256,512]{1,0:T(8,128)(2,1)S(1)}, u32[]{:S(2)}, u32[]{:S(2)}) %collective-permute-start.24) | collective-permute-done | bytes 262176 | tf_op jit(solution)/shard_map/ppermute | solution.py:33
  74.5 5.2 %collective-permute-done.26.refs_4_ = bf16[256,512]{1,0:T(8,128)(2,1)S(1)} collective-permute-done((bf16[256,512]{1,0:T(8,128)(2,1)S(1)}, bf16[256,512]{1,0:T(8,128)(2,1)S(1)}, u32[]{:S(2)}, u32[]{:S(2)}) %collective-permute-start.26) | collective-permute-done | bytes 262176 | tf_op jit(solution)/shard_map/ppermute | solution.py:33
  84.1 5.2 %copy-done = bf16[1,4096,1792]{2,1,0:T(8,128)(2,1)S(1)} copy-done((bf16[1,4096,1792]{2,1,0:T(8,128)(2,1)S(1)}, bf16[1,4096,1792]{2,1,0:T(8,128)(2,1)}, u32[]{:S(2)}) %copy-start) | copy-done | bytes 14680088
  89.3 3.0 %client_activations.5.args_1_ = bf16[256,512]{1,0:T(8,128)(2,1)S(1)} custom-call(s32[2]{0:T(128)S(1)} %pad_add_fusion.place, bf16[256,512]{1,0:T(8,128)(2,1)S(1)} %pad_maximum_fusion.rows.value.refs_0_, bf16[256,512]{1,0:T(8,128)(2,1)S(1)} %collective-permute-done.23.refs_1_, bf16[256,512]{1,0:T(8,128)(2,1)S(1)} %collective-permute-done.24.refs_2_, ...), custom_call_target="tpu_custom_call" | custom-call | flops 2147483648 | bytes 8388608 | tf_op jit(solution)/shard_map/client_activations/pallas_call | solution.py:143
  92.4 4.1 %client_activations.4.args_2_ = bf16[256,768]{1,0:T(8,128)(2,1)S(1)} custom-call(s32[2]{0:T(128)S(1)} %pad_add_fusion.place, bf16[256,512]{1,0:T(8,128)(2,1)S(1)} %pad_maximum_fusion.rows.value.refs_0_, bf16[256,512]{1,0:T(8,128)(2,1)S(1)} %collective-permute-done.23.refs_1_, bf16[256,512]{1,0:T(8,128)(2,1)S(1)} %collective-permute-done.24.refs_2_, ...), custom_call_target="tpu_custom_call" | custom-call | flops 3221225472 | bytes 12582912 | tf_op jit(solution)/shard_map/client_activations/pallas_call | solution.py:143
  96.5 3.0 %client_activations.3.args_3_ = bf16[256,512]{1,0:T(8,128)(2,1)S(1)} custom-call(s32[2]{0:T(128)S(1)} %pad_add_fusion.place, bf16[256,512]{1,0:T(8,128)(2,1)S(1)} %pad_maximum_fusion.rows.value.refs_0_, bf16[256,512]{1,0:T(8,128)(2,1)S(1)} %collective-permute-done.23.refs_1_, bf16[256,512]{1,0:T(8,128)(2,1)S(1)} %collective-permute-done.24.refs_2_, ...), custom_call_target="tpu_custom_call" | custom-call | flops 2147483648 | bytes 8388608 | tf_op jit(solution)/shard_map/client_activations/pallas_call | solution.py:143
  104.8 9.1 %match.4 = (f32[3584,256]{1,0:T(8,128)S(1)}, f32[2,3584]{1,0:T(2,128)S(1)}) custom-call(bf16[3584,256]{1,0:T(8,128)(2,1)S(1)} %bitcast.109, bf16[256,512]{1,0:T(8,128)(2,1)S(1)} %client_activations.5.args_1_, bf16[256,768]{1,0:T(8,128)(2,1)S(1)} %client_activations.4.args_2_, bf16[256,512]{1,0:T(8,128)(2,1)S(1)} %client_activations.3.args_3_), custom_call_target="tpu_custom_call" | custom-call | flops 6576668672 | bytes 7340032 | tf_op jit(solution)/shard_map/match/pallas_call | solution.py:234
  113.9 3.4 %match.5 = (f32[3584,256]{1,0:T(8,128)S(1)}, f32[2,3584]{1,0:T(2,128)S(1)}) custom-call(bf16[3584,256]{1,0:T(8,128)(2,1)S(1)} %bitcast.110, bf16[256,512]{1,0:T(8,128)(2,1)S(1)} %collective-permute-done.32.args_1_, f32[3584,256]{1,0:T(8,128)S(1)} %get-tuple-element.20.args_2_, f32[2,3584]{1,0:T(2,128)S(1)} %get-tuple-element.21.args_3_), custom_call_target="tpu_custom_call" | custom-call | flops 1879048192 | bytes 7340032 | tf_op jit(solution)/shard_map/match/pallas_call | solution.py:234
  117.2 4.1 %match.6 = (f32[3584,256]{1,0:T(8,128)S(1)}, f32[2,3584]{1,0:T(2,128)S(1)}) custom-call(bf16[3584,256]{1,0:T(8,128)(2,1)S(1)} %bitcast.111, bf16[256,768]{1,0:T(8,128)(2,1)S(1)} %collective-permute-done.31.args_1_, f32[3584,256]{1,0:T(8,128)S(1)} %get-tuple-element.22.args_2_, f32[2,3584]{1,0:T(2,128)S(1)} %get-tuple-element.23.args_3_), custom_call_target="tpu_custom_call" | custom-call | flops 2818572288 | bytes 7340032 | tf_op jit(solution)/shard_map/match/pallas_call | solution.py:234
  121.4 3.2 %match.7 = (f32[3584,256]{1,0:T(8,128)S(1)}, f32[2,3584]{1,0:T(2,128)S(1)}) custom-call(bf16[3584,256]{1,0:T(8,128)(2,1)S(1)} %bitcast.112, bf16[256,512]{1,0:T(8,128)(2,1)S(1)} %collective-permute-done.30.args_1_, f32[3584,256]{1,0:T(8,128)S(1)} %get-tuple-element.24.args_2_, f32[2,3584]{1,0:T(2,128)S(1)} %get-tuple-element.25.args_3_), custom_call_target="tpu_custom_call" | custom-call | flops 1879048192 | bytes 7340032 | tf_op jit(solution)/shard_map/match/pallas_call | solution.py:234
  134.3 2.5 %collective-permute-done.34 = bf16[4,2,224,256]{3,2,1,0:T(8,128)(2,1)S(1)} collective-permute-done((bf16[4,2,224,256]{3,2,1,0:T(8,128)(2,1)S(1)}, bf16[4,2,224,256]{3,2,1,0:T(8,128)(2,1)S(1)}, u32[]{:S(2)}, u32[]{:S(2)}) %collective-permute-start.34) | collective-permute-done | bytes 917536 | tf_op jit(solution)/shard_map/ppermute | solution.py:33
  140.7 5.0 %collective-permute-done.35 = bf16[2,224,256]{2,1,0:T(8,128)(2,1)S(1)} collective-permute-done((bf16[2,224,256]{2,1,0:T(8,128)(2,1)S(1)}, bf16[2,224,256]{2,1,0:T(8,128)(2,1)S(1)}, u32[]{:S(2)}, u32[]{:S(2)}) %collective-permute-start.35) | collective-permute-done | bytes 229408 | tf_op jit(solution)/shard_map/ppermute | solution.py:33
  145.6 5.2 %collective-permute-done.36 = bf16[2,224,256]{2,1,0:T(8,128)(2,1)S(1)} collective-permute-done((bf16[2,224,256]{2,1,0:T(8,128)(2,1)S(1)}, bf16[2,224,256]{2,1,0:T(8,128)(2,1)S(1)}, u32[]{:S(2)}, u32[]{:S(2)}) %collective-permute-start.36) | collective-permute-done | bytes 229408 | tf_op jit(solution)/shard_map/ppermute | solution.py:33
  153.3 5.3 %collective-permute-done.38 = bf16[224,256]{1,0:T(8,128)(2,1)S(1)} collective-permute-done((bf16[224,256]{1,0:T(8,128)(2,1)S(1)}, bf16[224,256]{1,0:T(8,128)(2,1)S(1)}, u32[]{:S(2)}, u32[]{:S(2)}) %collective-permute-start.38) | collective-permute-done | bytes 114720 | tf_op jit(solution)/shard_map/ppermute | solution.py:33
  (147 shorter events, 65.6 us)
Async XLA Ops:
  12.5 8.8 %collective-permute-start.2 = (bf16[128,512]{1,0:T(8,128)(2,1)S(1)}, bf16[128,512]{1,0:T(8,128)(2,1)S(1)}, u32[]{:S(2)}, u32[]{:S(2)}) collective-permute-start(bf16[128,512]{1,0:T(8,128)(2,1)S(1)} %get-tuple-element.45), channel_id=1, source_target_pairs={{0,16},{4,20},{8,24},{12,28},{16,0},{20,4},{24,8},{28,12},{1,17},{... | collective-permute-start | bytes 393224 | tf_op jit(solution)/shard_map/ppermute | solution.py:33
  14.6 8.5 %collective-permute-start.6 = (bf16[128,512]{1,0:T(8,128)(2,1)S(1)}, bf16[128,512]{1,0:T(8,128)(2,1)S(1)}, u32[]{:S(2)}, u32[]{:S(2)}) collective-permute-start(bf16[128,512]{1,0:T(8,128)(2,1)S(1)} %get-tuple-element.43), channel_id=1, source_target_pairs={{0,8},{4,12},{8,0},{12,4},{16,24},{20,28},{24,16},{28,20},{1,9},{5... | collective-permute-start | bytes 393224 | tf_op jit(solution)/shard_map/ppermute | solution.py:33
  16.0 9.2 %collective-permute-start.7 = (bf16[128,512]{1,0:T(8,128)(2,1)S(1)}, bf16[128,512]{1,0:T(8,128)(2,1)S(1)}, u32[]{:S(2)}, u32[]{:S(2)}) collective-permute-start(bf16[128,512]{1,0:T(8,128)(2,1)S(1)} %get-tuple-element.42), channel_id=1, source_target_pairs={{0,16},{4,20},{8,24},{12,28},{16,0},{20,4},{24,8},{28,12},{1,17},{... | collective-permute-start | bytes 393224 | tf_op jit(solution)/shard_map/ppermute | solution.py:33
  17.5 9.2 %collective-permute-start.8 = (bf16[128,512]{1,0:T(8,128)(2,1)S(1)}, bf16[128,512]{1,0:T(8,128)(2,1)S(1)}, u32[]{:S(2)}, u32[]{:S(2)}) collective-permute-start(bf16[128,512]{1,0:T(8,128)(2,1)S(1)} %get-tuple-element.41), channel_id=1, source_target_pairs={{0,24},{4,28},{8,16},{12,20},{16,8},{20,12},{24,0},{28,4},{1,25},{... | collective-permute-start | bytes 393224 | tf_op jit(solution)/shard_map/ppermute | solution.py:33
  28.4 9.9 %collective-permute-start.9 = (bf16[128,512]{1,0:T(8,128)(2,1)S(1)}, bf16[128,512]{1,0:T(8,128)(2,1)S(1)}, u32[]{:S(2)}, u32[]{:S(2)}) collective-permute-start(bf16[128,512]{1,0:T(8,128)(2,1)S(1)} %get-tuple-element.37), channel_id=1, source_target_pairs={{0,1},{1,0},{2,3},{3,2},{4,5},{5,4},{6,7},{7,6},{8,9},{9,8},{10,11... | collective-permute-start | bytes 393224 | tf_op jit(solution)/shard_map/ppermute | solution.py:33
  33.1 13.6 %collective-permute-start.5 = (bf16[128,512]{1,0:T(8,128)(2,1)S(1)}, bf16[128,512]{1,0:T(8,128)(2,1)S(1)}, u32[]{:S(2)}, u32[]{:S(2)}) collective-permute-start(bf16[128,512]{1,0:T(8,128)(2,1)S(1)} %add.93), channel_id=1, source_target_pairs={{0,2},{1,3},{2,0},{3,1},{4,6},{5,7},{6,4},{7,5},{8,10},{9,11},{10,... | collective-permute-start | bytes 393224 | tf_op jit(solution)/shard_map/ppermute | solution.py:33
  38.4 9.7 %collective-permute-start.10 = (bf16[128,512]{1,0:T(8,128)(2,1)S(1)}, bf16[128,512]{1,0:T(8,128)(2,1)S(1)}, u32[]{:S(2)}, u32[]{:S(2)}) collective-permute-start(bf16[128,512]{1,0:T(8,128)(2,1)S(1)} %add.98), channel_id=1, source_target_pairs={{0,2},{1,3},{2,0},{3,1},{4,6},{5,7},{6,4},{7,5},{8,10},{9,11},{10,... | collective-permute-start | bytes 393224 | tf_op jit(solution)/shard_map/ppermute | solution.py:33
  55.4 8.5 %collective-permute-start.12 = (bf16[2,224,256]{2,1,0:T(8,128)(2,1)S(1)}, bf16[2,224,256]{2,1,0:T(8,128)(2,1)S(1)}, u32[]{:S(2)}, u32[]{:S(2)}) collective-permute-start(bf16[2,224,256]{2,1,0:T(8,128)(2,1)S(1)} %get-tuple-element.49), channel_id=1, source_target_pairs={{0,8},{4,12},{8,0},{12,4},{16,24},{20,28},{24,16},{28,20},{1,9},{5... | collective-permute-start | bytes 688136 | tf_op jit(solution)/shard_map/ppermute | solution.py:33
  56.2 12.7 %collective-permute-start.13 = (bf16[2,224,256]{2,1,0:T(8,128)(2,1)S(1)}, bf16[2,224,256]{2,1,0:T(8,128)(2,1)S(1)}, u32[]{:S(2)}, u32[]{:S(2)}) collective-permute-start(bf16[2,224,256]{2,1,0:T(8,128)(2,1)S(1)} %get-tuple-element.51), channel_id=1, source_target_pairs={{0,16},{4,20},{8,24},{12,28},{16,0},{20,4},{24,8},{28,12},{1,17},{... | collective-permute-start | bytes 688136 | tf_op jit(solution)/shard_map/ppermute | solution.py:33
  57.6 11.3 %collective-permute-start.14 = (bf16[2,224,256]{2,1,0:T(8,128)(2,1)S(1)}, bf16[2,224,256]{2,1,0:T(8,128)(2,1)S(1)}, u32[]{:S(2)}, u32[]{:S(2)}) collective-permute-start(bf16[2,224,256]{2,1,0:T(8,128)(2,1)S(1)} %get-tuple-element.50), channel_id=1, source_target_pairs={{0,24},{4,28},{8,16},{12,20},{16,8},{20,12},{24,0},{28,4},{1,25},{... | collective-permute-start | bytes 688136 | tf_op jit(solution)/shard_map/ppermute | solution.py:33
  59.0 21.5 %collective-permute-start.23 = (bf16[256,512]{1,0:T(8,128)(2,1)S(1)}, bf16[256,512]{1,0:T(8,128)(2,1)S(1)}, u32[]{:S(2)}, u32[]{:S(2)}) collective-permute-start(bf16[256,512]{1,0:T(8,128)(2,1)S(1)} %pad_maximum_fusion.rows.value.refs_0_), channel_id=1, source_target_pairs={{0,4},{4,0},{8,12},{12,8},{16,20},{20,16},{24,28},{28,24},{1,5},{5... | collective-permute-start | bytes 786440 | tf_op jit(solution)/shard_map/ppermute | solution.py:33
  59.0 15.5 %collective-permute-start.24 = (bf16[256,512]{1,0:T(8,128)(2,1)S(1)}, bf16[256,512]{1,0:T(8,128)(2,1)S(1)}, u32[]{:S(2)}, u32[]{:S(2)}) collective-permute-start(bf16[256,512]{1,0:T(8,128)(2,1)S(1)} %tied.1), channel_id=1, source_target_pairs={{0,8},{4,12},{8,0},{12,4},{16,24},{20,28},{24,16},{28,20},{1,9},{5... | collective-permute-start | bytes 786440 | tf_op jit(solution)/shard_map/ppermute | solution.py:33
  64.0 15.8 %collective-permute-start.26 = (bf16[256,512]{1,0:T(8,128)(2,1)S(1)}, bf16[256,512]{1,0:T(8,128)(2,1)S(1)}, u32[]{:S(2)}, u32[]{:S(2)}) collective-permute-start(bf16[256,512]{1,0:T(8,128)(2,1)S(1)} %tied.1), channel_id=1, source_target_pairs={{0,16},{4,20},{8,24},{12,28},{16,0},{20,4},{24,8},{28,12},{1,17},{... | collective-permute-start | bytes 786440 | tf_op jit(solution)/shard_map/ppermute | solution.py:33
  68.9 10.8 %collective-permute-start.28 = (bf16[256,512]{1,0:T(8,128)(2,1)S(1)}, bf16[256,512]{1,0:T(8,128)(2,1)S(1)}, u32[]{:S(2)}, u32[]{:S(2)}) collective-permute-start(bf16[256,512]{1,0:T(8,128)(2,1)S(1)} %tied.1), channel_id=1, source_target_pairs={{0,24},{4,28},{8,16},{12,20},{16,8},{20,12},{24,0},{28,4},{1,25},{... | collective-permute-start | bytes 786440 | tf_op jit(solution)/shard_map/ppermute | solution.py:33
  69.6 10.8 %collective-permute-start.15 = (bf16[224,256]{1,0:T(8,128)(2,1)S(1)}, bf16[224,256]{1,0:T(8,128)(2,1)S(1)}, u32[]{:S(2)}, u32[]{:S(2)}) collective-permute-start(bf16[224,256]{1,0:T(8,128)(2,1)S(1)} %multiply_convert_fusion), channel_id=1, source_target_pairs={{0,2},{1,3},{2,0},{3,1},{4,6},{5,7},{6,4},{7,5},{8,10},{9,11},{10,... | collective-permute-start | bytes 344072 | tf_op jit(solution)/shard_map/ppermute | solution.py:33
  80.4 19.2 %collective-permute-start.16 = (bf16[2,224,256]{2,1,0:T(8,128)(2,1)S(1)}, bf16[2,224,256]{2,1,0:T(8,128)(2,1)S(1)}, u32[]{:S(2)}, u32[]{:S(2)}) collective-permute-start(bf16[2,224,256]{2,1,0:T(8,128)(2,1)S(1)} %pad_maximum_fusion.1), channel_id=1, source_target_pairs={{0,4},{4,0},{8,12},{12,8},{16,20},{20,16},{24,28},{28,24},{1,5},{5... | collective-permute-start | bytes 688136 | tf_op jit(solution)/shard_map/ppermute | solution.py:33
  80.5 21.1 %collective-permute-start.17 = (bf16[2,224,256]{2,1,0:T(8,128)(2,1)S(1)}, bf16[2,224,256]{2,1,0:T(8,128)(2,1)S(1)}, u32[]{:S(2)}, u32[]{:S(2)}) collective-permute-start(bf16[2,224,256]{2,1,0:T(8,128)(2,1)S(1)} %pad_maximum_fusion.1), channel_id=1, source_target_pairs={{0,8},{4,12},{8,0},{12,4},{16,24},{20,28},{24,16},{28,20},{1,9},{5... | collective-permute-start | bytes 688136 | tf_op jit(solution)/shard_map/ppermute | solution.py:33
  82.0 19.7 %collective-permute-start.19 = (bf16[2,224,256]{2,1,0:T(8,128)(2,1)S(1)}, bf16[2,224,256]{2,1,0:T(8,128)(2,1)S(1)}, u32[]{:S(2)}, u32[]{:S(2)}) collective-permute-start(bf16[2,224,256]{2,1,0:T(8,128)(2,1)S(1)} %pad_maximum_fusion.1), channel_id=1, source_target_pairs={{0,16},{4,20},{8,24},{12,28},{16,0},{20,4},{24,8},{28,12},{1,17},{... | collective-permute-start | bytes 688136 | tf_op jit(solution)/shard_map/ppermute | solution.py:33
  82.4 19.5 %collective-permute-start.21 = (bf16[2,224,256]{2,1,0:T(8,128)(2,1)S(1)}, bf16[2,224,256]{2,1,0:T(8,128)(2,1)S(1)}, u32[]{:S(2)}, u32[]{:S(2)}) collective-permute-start(bf16[2,224,256]{2,1,0:T(8,128)(2,1)S(1)} %pad_maximum_fusion.1), channel_id=1, source_target_pairs={{0,24},{4,28},{8,16},{12,20},{16,8},{20,12},{24,0},{28,4},{1,25},{... | collective-permute-start | bytes 688136 | tf_op jit(solution)/shard_map/ppermute | solution.py:33
  92.3 21.5 %collective-permute-start.32 = (bf16[256,512]{1,0:T(8,128)(2,1)S(1)}, bf16[256,512]{1,0:T(8,128)(2,1)S(1)}, u32[]{:S(2)}, u32[]{:S(2)}) collective-permute-start(bf16[256,512]{1,0:T(8,128)(2,1)S(1)} %client_activations.5.args_1_), channel_id=1, source_target_pairs={{0,1},{1,0},{2,3},{3,2},{4,5},{5,4},{6,7},{7,6},{8,9},{9,8},{10,11... | collective-permute-start | bytes 786440 | tf_op jit(solution)/shard_map/ppermute | solution.py:33
  99.6 17.6 %collective-permute-start.31 = (bf16[256,768]{1,0:T(8,128)(2,1)S(1)}, bf16[256,768]{1,0:T(8,128)(2,1)S(1)}, u32[]{:S(2)}, u32[]{:S(2)}) collective-permute-start(bf16[256,768]{1,0:T(8,128)(2,1)S(1)} %client_activations.4.args_2_), channel_id=1, source_target_pairs={{0,1},{1,0},{2,3},{3,2},{4,5},{5,4},{6,7},{7,6},{8,9},{9,8},{10,11... | collective-permute-start | bytes 1179656 | tf_op jit(solution)/shard_map/ppermute | solution.py:33
  101.7 19.7 %collective-permute-start.30 = (bf16[256,512]{1,0:T(8,128)(2,1)S(1)}, bf16[256,512]{1,0:T(8,128)(2,1)S(1)}, u32[]{:S(2)}, u32[]{:S(2)}) collective-permute-start(bf16[256,512]{1,0:T(8,128)(2,1)S(1)} %client_activations.3.args_3_), channel_id=1, source_target_pairs={{0,1},{1,0},{2,3},{3,2},{4,5},{5,4},{6,7},{7,6},{8,9},{9,8},{10,11... | collective-permute-start | bytes 786440 | tf_op jit(solution)/shard_map/ppermute | solution.py:33
  138.6 12.3 %collective-permute-start.36 = (bf16[2,224,256]{2,1,0:T(8,128)(2,1)S(1)}, bf16[2,224,256]{2,1,0:T(8,128)(2,1)S(1)}, u32[]{:S(2)}, u32[]{:S(2)}) collective-permute-start(bf16[2,224,256]{2,1,0:T(8,128)(2,1)S(1)} %get-tuple-element.48), channel_id=1, source_target_pairs={{0,16},{4,20},{8,24},{12,28},{16,0},{20,4},{24,8},{28,12},{1,17},{... | collective-permute-start | bytes 688136 | tf_op jit(solution)/shard_map/ppermute | solution.py:33
  138.9 11.9 %collective-permute-start.37 = (bf16[2,224,256]{2,1,0:T(8,128)(2,1)S(1)}, bf16[2,224,256]{2,1,0:T(8,128)(2,1)S(1)}, u32[]{:S(2)}, u32[]{:S(2)}) collective-permute-start(bf16[2,224,256]{2,1,0:T(8,128)(2,1)S(1)} %get-tuple-element.47), channel_id=1, source_target_pairs={{0,24},{4,28},{8,16},{12,20},{16,8},{20,12},{24,0},{28,4},{1,25},{... | collective-permute-start | bytes 688136 | tf_op jit(solution)/shard_map/ppermute | solution.py:33
  (33 other events, 455.9 us)

commit v3 on v2

--- a/solution.py
+++ b/solution.py
@@ -33,7 +33,15 @@
     return lax.ppermute(value, axis, [(i, i ^ mask) for i in range(size)])
 
 
-def select_kernel(ids, place, gain, table, keep, send, rows, held, slots, sems):
+def select_kernel(place, ids_far, gain_far, table, keep, send, ids, gain, rows, held, slots, sems, first):
+    arrivals = [
+        pltpu.make_async_copy(ids_far, ids, first.at[0]),
+        pltpu.make_async_copy(gain_far, gain, first.at[1]),
+    ]
+    for arrival in arrivals:
+        arrival.start()
+    for arrival in arrivals:
+        arrival.wait()
     tokens, width = rows.shape
     rows_here = table.shape[0]
     start = place[0] * rows_here
@@ -91,18 +99,21 @@
     return pl.pallas_call(
         select_kernel,
         out_shape=(half, half),
-        in_specs=[scalars, scalars, whole, in_hbm],
+        in_specs=[scalars, in_hbm, in_hbm, in_hbm],
         out_specs=(whole, whole),
         scratch_shapes=[
+            pltpu.SMEM((tokens,), jnp.int32),
+            pltpu.VMEM((1, width), f32),
             pltpu.VMEM((tokens, width), f32),
             pltpu.SMEM((tokens + 1,), jnp.int32),
             pltpu.VMEM((fetch_slots, group_rows, width), bf16),
             pltpu.SemaphoreType.DMA((fetch_slots,)),
+            pltpu.SemaphoreType.DMA((2,)),
         ],
         compiler_params=vmem_params(48),
         cost_estimate=cost(4e6, 4e6),
         name="select_rows",
-    )(token_ids, place, norm_gain[None, :], embed_table)
+    )(place, token_ids, norm_gain[None, :], embed_table)
 
 
 def standardized(hidden, axis):
@@ -121,85 +132,78 @@
     *blocks, gate_w, up_w, out = refs
     client = place[1]
     tokens, span = blocks[0].shape
-    wide = unit_block(gate_w.shape[2])
-    for at in range(0, out.shape[1], wide):
-        units = slice(first + at, first + at + wide)
-        gate = jnp.zeros((tokens, wide), f32)
-        up = jnp.zeros((tokens, wide), f32)
-        for p, block in enumerate(blocks):
-            features = pl.ds(pl.multiple_of((client ^ p) * span, span), span)
-            gate += jnp.dot(block[...], gate_w[0, features, units], preferred_element_type=f32)
-            up += jnp.dot(block[...], up_w[0, features, units], preferred_element_type=f32)
-        out[:, at : at + wide] = standardized(gated(gate, up), 0)
-
-
-def unit_block(units, most=256):
-    return most if units % most == 0 else most // 2
+    wide = out.shape[1]
+    units = pl.ds(pl.multiple_of((first + pl.program_id(0)) * wide, wide), wide)
+    gate = jnp.zeros((tokens, wide), f32)
+    up = jnp.zeros((tokens, wide), f32)
+    for p, block in enumerate(blocks):
+        features = pl.ds(pl.multiple_of((client ^ p) * span, span), span)
+        gate += jnp.dot(block[...], gate_w[0, features, :], preferred_element_type=f32)
+        up += jnp.dot(block[...], up_w[0, features, units], preferred_element_type=f32)
+    out[...] = standardized(gated(gate, up), 0)
 
 
 def client_activations(place, blocks, client_gate, client_up, first, last):
     tokens = blocks[0].shape[0]
     width, units = client_gate.shape[1], last - first
-    return pl.pallas_call(
-        functools.partial(client_kernel, first),
+    wide = unit_block(client_gate.shape[2])
+    start = first // wide
+    return pl.pallas_call(
+        functools.partial(client_kernel, start),
+        grid=(units // wide,),
         out_shape=jax.ShapeDtypeStruct((tokens, units), bf16),
-        in_specs=[scalars] + [whole] * (len(blocks) + 2),
-        out_specs=whole,
-        compiler_params=vmem_params(8),
+        in_specs=[scalars]
+        + [whole] * len(blocks)
+        + [pl.BlockSpec((1, width, wide), lambda i: (0, 0, start + i)), whole],
+        out_specs=pl.BlockSpec((tokens, wide), lambda i: (0, i)),
+        compiler_params=vmem_params(12),
         cost_estimate=cost(4 * tokens * width * units, 4 * width * units),
         name="client_activations",
     )(place, *blocks, client_gate, client_up)
 
 
+def unit_block(units, most=256):
+    return most if units % most == 0 else most // 2
+
+
 def partial_kernel(place, rows, gate_w, up_w, keep, send, total):
-    step = pl.program_id(0)
-    wide = gate_w.shape[1]
-    at = pl.ds(pl.multiple_of(step * wide, wide), wide)
-    total[0, at, :] = jnp.dot(rows[...], gate_w[...], preferred_element_type=f32).T
-    total[1, at, :] = jnp.dot(rows[...], up_w[...], preferred_element_type=f32).T
-
-    @pl.when(step == pl.num_programs(0) - 1)
-    def _():
-        piece = keep.shape[2]
-        for p in range(2 * keep.shape[0]):
-            source = pl.ds(pl.multiple_of((place[1] ^ p) * piece, 8), piece)
-            for which in range(2):
-                if p % 2:
-                    send[p // 2, which] = total[which, source, :].astype(bf16)
-                else:
-                    keep[p // 2, which] = total[which, source, :]
+    wide = unit_block(gate_w.shape[1])
+    for which, weights in enumerate((gate_w, up_w)):
+        for at in range(0, weights.shape[1], wide):
+            total[which, at : at + wide, :] = lax.dot_general(
+                weights[:, at : at + wide],
+                rows[...],
+                (((0,), (1,)), ((), ())),
+                preferred_element_type=f32,
+            )
+    piece = keep.shape[2]
+    for p in range(2 * keep.shape[0]):
+        source = pl.ds(pl.multiple_of((place[1] ^ p) * piece, 8), piece)
+        for which in range(2):
+            if p % 2:
+                send[p // 2, which] = total[which, source, :].astype(bf16)
+            else:
+                keep[p // 2, which] = total[which, source, :]
 
 
 def reference_partials(place, rows, ref_gate, ref_up, clients):
     tokens, span = rows.shape
     units = ref_gate.shape[1]
-    wide = unit_block(units)
     shape = (clients // 2, 2, units // clients, tokens)
-    weights = pl.BlockSpec((span, wide), lambda i: (0, i))
-    pieces = pl.BlockSpec(shape, lambda i: (0, 0, 0, 0))
     return pl.pallas_call(
         partial_kernel,
-        grid=(units // wide,),
         out_shape=(jax.ShapeDtypeStruct(shape, f32), jax.ShapeDtypeStruct(shape, bf16)),
-        in_specs=[scalars, pl.BlockSpec((tokens, span), lambda i: (0, 0)), weights, weights],
-        out_specs=(pieces, pieces),
+        in_specs=[scalars] + [whole] * 3,
+        out_specs=(whole, whole),
         scratch_shapes=[pltpu.VMEM((2, units, tokens), f32)],
-        compiler_params=vmem_params(18),
+        compiler_params=vmem_params(16),
         cost_estimate=cost(4 * tokens * span * units, 4 * span * units),
         name="reference_partials",
     )(place, rows, ref_gate, ref_up)
 
 
-def match_kernel(sources, *args):
-    refs, *rest = args
-    columns, rest = rest[:sources], rest[sources:]
-    numerator, sums = rest[-2:]
-    tokens = refs.shape[1]
-    rows = refs[...]
-    if len(rest) > 2:
-        total = rest[0][...]
-    else:
-        total = jnp.zeros(numerator.shape, f32)
+def matched(rows, columns, total, with_sums):
+    tokens = rows.shape[1]
     colsum = jnp.zeros((rows.shape[0], 128), f32)
     weighted = jnp.zeros((rows.shape[0], 128), f32)
     for source in columns:
@@ -208,29 +212,113 @@
             some = source[:, i : i + wide]
             r = jnp.dot(rows, some, preferred_element_type=f32)
             w = jnp.exp2(r * (sharpness * log2_e / tokens))
-            total += lax.dot_general(
-                w.astype(bf16), some, (((1,), (1,)), ((), ())), preferred_element_type=f32
-            )
-            wr = w * r
-            for k in range(0, wide, 128):
-                colsum += w[:, k : k + 128]
-                weighted += wr[:, k : k + 128]
-    numerator[...] = total
+            if total is not None:
+                total += lax.dot_general(
+                    w.astype(bf16), some, (((1,), (1,)), ((), ())), preferred_element_type=f32
+                )
+            if with_sums:
+                wr = w * r
+                for k in range(0, wide, 128):
+                    colsum += w[:, k : k + 128]
+                    weighted += wr[:, k : k + 128]
+    if not with_sums:
+        return total
     row = jnp.sum(colsum.T, axis=0, keepdims=True)
     row_weighted = jnp.sum(weighted.T, axis=0, keepdims=True) * (1.0 / tokens)
-    if len(rest) > 2:
-        row = row + rest[1][0:1, :]
-        row_weighted = row_weighted + rest[1][1:2, :]
+    return total, row, row_weighted
+
+
+def match_kernel(sources, refs, *rest):
+    columns, rest = rest[:sources], rest[sources:]
+    numerator, sums = rest[-2:]
+    before = rest[:-2]
+    start = before[0][...] if before else jnp.zeros(numerator.shape, f32)
+    total, row, row_weighted = matched(refs[...], columns, start, True)
+    numerator[...] = total
+    if before:
+        row = row + before[1][0:1, :]
+        row_weighted = row_weighted + before[1][1:2, :]
     sums[0:1, :] = row
     sums[1:2, :] = row_weighted
+
+
+def match_last_kernel(refs, columns, before, sums_before, keep, send, sums):
+    total, row, row_weighted = matched(refs[...], [columns], before[...], True)
+    row = row + sums_before[0:1, :]
+    sums[0:1, :] = row
+    sums[1:2, :] = row_weighted + sums_before[1:2, :]
+    lanes = 128
+    by_row = jnp.broadcast_to(1.0 / row, (lanes, total.shape[0])).T
+    size = keep.shape[2]
+    for p in range(2 * keep.shape[0]):
+        target = send if p % 2 else keep
+        units = slice(p * size, (p + 1) * size)
+        for k in range(0, total.shape[1], lanes):
+            target[p // 2, 0, :, k : k + lanes] = (total[units, k : k + lanes] * by_row[units]).astype(
+                target.dtype
+            )
+
+
+def join_kernel(keep, arrived, factor, factor_arrived, first, others):
+    pairs, groups, size, tokens = keep.shape
+    lanes = 128
+    units = 2 * pairs * size
+    for g in range(groups):
+        rows = [
+            jnp.broadcast_to(source[:, g * units : (g + 1) * units], (lanes, units)).T
+            for source in (factor, factor_arrived)
+        ]
+        for h in range(pairs):
+            ours = slice(2 * h * size, (2 * h + 1) * size)
+            theirs = slice((2 * h + 1) * size, (2 * h + 2) * size)
+            for k in range(0, tokens, lanes):
+                at = slice(k, k + lanes)
+                total = keep[h, g, :, at].astype(f32) * rows[0][ours]
+                total += arrived[h, g, :, at].astype(f32) * rows[1][theirs]
+                if h:
+                    others[h - 1, g, :, at] = total.astype(bf16)
+                else:
+                    first[g, :, at] = total
+
+
+def joined(keep, arrived, factor, factor_arrived):
+    pairs, groups, size, tokens = keep.shape
+    return pl.pallas_call(
+        join_kernel,
+        out_shape=(
+            jax.ShapeDtypeStruct((groups, size, tokens), f32),
+            jax.ShapeDtypeStruct((pairs - 1, groups, size, tokens), bf16),
+        ),
+        in_specs=[whole] * 4,
+        out_specs=(whole, whole),
+        compiler_params=vmem_params(16),
+        cost_estimate=cost(4 * keep.size, 6 * keep.size),
+        name="joined",
+    )(keep, arrived, factor, factor_arrived)
+
+
+high = 896
+
+
+def match_cost(rows, tokens, units):
+    return cost(4 * rows * units * tokens, 8 * rows * tokens, rows * units)
+
+
+def by_rows(width):
+    return pl.BlockSpec((high, width), lambda j: (j, 0))
+
+
+def by_columns(rows):
+    return pl.BlockSpec((rows, high), lambda j: (0, j))
+
+
+def unblocked(value):
+    return pl.BlockSpec(value.shape, lambda j: (0, 0))
 
 
 def match(refs, columns, before=()):
     rows, tokens = refs.shape
     units = sum(source.shape[1] for source in columns)
-    high = 896
-    numerators = pl.BlockSpec((high, tokens), lambda j: (j, 0))
-    sums = pl.BlockSpec((2, high), lambda j: (0, j))
     return pl.pallas_call(
         functools.partial(match_kernel, len(columns)),
         grid=(rows // high,),
@@ -238,47 +326,34 @@
             jax.ShapeDtypeStruct((rows, tokens), f32),
             jax.ShapeDtypeStruct((2, rows), f32),
         ),
-        in_specs=[numerators]
-        + [pl.BlockSpec(source.shape, lambda j: (0, 0)) for source in columns]
-        + [numerators, sums][: len(before)],
-        out_specs=(numerators, sums),
+        in_specs=[by_rows(tokens)]
+        + [unblocked(source) for source in columns]
+        + [by_rows(tokens), by_columns(2)][: len(before)],
+        out_specs=(by_rows(tokens), by_columns(2)),
         compiler_params=vmem_params(20),
-        cost_estimate=cost(4 * rows * units * tokens, 8 * rows * tokens, rows * units),
+        cost_estimate=match_cost(rows, tokens, units),
         name="match",
     )(refs, *columns, *before)
 
 
-def scale_kernel(numerator, factor, keep, send):
-    pieces, size = 2 * keep.shape[0], keep.shape[2]
-    lanes = 128
-    by_row = jnp.broadcast_to(factor[...], (lanes, pieces * size)).T
-    for p in range(pieces):
-        target = send if p % 2 else keep
-        units = slice(p * size, (p + 1) * size)
-        for k in range(0, numerator.shape[1], lanes):
-            target[p // 2, 0, :, k : k + lanes] = (
-                numerator[units, k : k + lanes] * by_row[units]
-            ).astype(target.dtype)
-
-
-def scaled(numerator, factor, clients, groups):
-    rows, tokens = numerator.shape
-    units = rows // groups
-    shape = (clients // 2, groups, units // clients, tokens)
-    pieces = pl.BlockSpec((shape[0], 1, shape[2], tokens), lambda g: (0, g, 0, 0))
-    return pl.pallas_call(
-        scale_kernel,
-        grid=(groups,),
-        out_shape=(jax.ShapeDtypeStruct(shape, f32), jax.ShapeDtypeStruct(shape, bf16)),
-        in_specs=[
-            pl.BlockSpec((units, tokens), lambda g: (g, 0)),
-            pl.BlockSpec((1, units), lambda g: (0, g)),
-        ],
-        out_specs=(pieces, pieces),
+def match_last(refs, columns, before, sums, clients, groups):
+    rows, tokens = refs.shape
+    size = rows // groups // clients
+    steps = rows // groups // high
+    pairs = max(1, clients // 2 // steps)
+    shape = (clients // 2, groups, size, tokens)
+    pieces = pl.BlockSpec((pairs, 1, size, tokens), lambda j: (j % steps, j // steps, 0, 0))
+    halves = jax.ShapeDtypeStruct(shape, bf16)
+    return pl.pallas_call(
+        match_last_kernel,
+        grid=(rows // high,),
+        out_shape=(halves, halves, jax.ShapeDtypeStruct((2, rows), f32)),
+        in_specs=[by_rows(tokens), unblocked(columns), by_rows(tokens), by_columns(2)],
+        out_specs=(pieces, pieces, by_columns(2)),
         compiler_params=vmem_params(20),
-        cost_estimate=cost(rows * tokens, 7 * rows * tokens),
-        name="scaled",
-    )(numerator, factor)
+        cost_estimate=match_cost(rows, tokens, columns.shape[1]),
+        name="match_last",
+    )(refs, columns, before, sums)
 
 
 def tie_kernel(value, *rest):
@@ -369,30 +444,34 @@
     refs = jnp.stack(gathered(ref_pieces), axis=1).reshape(groups * clients * piece, tokens)
 
     units = client_gate.shape[2]
-    cuts = [0, 2 * units // 7, 5 * units // 7, units]
+    cuts = [0, 5 * units // 7, units]
     own = [
         client_activations(place, blocks, client_gate, client_up, first, last)
         for first, last in zip(cuts, cuts[1:])
     ]
     theirs = [over_units(part, mask=1) for part in own]
-    sofar = match(refs, own)
-    for part in theirs:
-        sofar = match(refs, [part], sofar)
-    numerator, sums = sofar
+    numerator, sums = match(refs, own)
+    numerator, sums = match(refs, theirs[:1], (numerator, sums))
+    keep, send, sums = match_last(refs, theirs[1], numerator, sums, clients, groups)
+    arrived = over_clients(send, mask=1)
     sums = sums.reshape(2, groups, clients * piece)
     all_sums = sums
     for k in even[1:]:
         other = over_units(sums, mask=k)
         all_sums = all_sums + jnp.stack([other[:, g ^ (k // 2)] for g in range(groups)], axis=1)
     colsum, weighted = all_sums[0], all_sums[1]
+    factor = (sums[0] * (1.0 / clients) / colsum).reshape(1, groups * clients * piece)
+    first, others = joined(keep, arrived, factor, over_clients(factor, mask=1))
+    arrived = [over_clients(others[p // 2 - 1], mask=p) for p in range(2, clients, 2)]
+    reduced = first
+    for other in arrived:
+        reduced = reduced + other.astype(f32)
+
     score = (weighted[0] / colsum[0]).reshape(clients, piece)
     here = jnp.arange(clients)[:, None] ^ client == jnp.arange(clients)[None, :]
     score = jnp.sum(jnp.where(here[:, :, None], score[None], 0.0), axis=1)
     score = score.reshape(1, clients * piece)
 
-    inverse = ((1.0 / clients) / colsum).reshape(1, groups * clients * piece)
-    total = summed_pairs(*scaled(numerator, inverse, clients, groups))
-    reduced = summed(total, sent(total))
     mine = reduced[0]
     for k in even[1:]:
         mine = mine + over_units(reduced[k // 2].astype(bf16), mask=k).astype(f32)

time: 170 us -> 158 us (0.929)
  local copies, waits for them, and re-layouts: 11.6 us -> 2.65 us
  waiting for transfers between devices: 68.9 us -> 65.1 us
    unnamed x29 -> x26, local copies, waits for them, and re-layouts: 10.5 us -> 1.54 us
    pallas_call x4 -> x2, Pallas kernels: 19.7 us -> 15.2 us  [match(): pl.pallas_call(functools.partial(match_kernel, len(columns)), grid=(rows...]
    ppermute x46, waiting for transfers between devices: 68.9 us -> 65.1 us  [xor_permute(): return lax.ppermute(value, axis, [(i, i ^ mask) for i in range(size)])]
    pallas_call x5, Pallas kernels: 15.3 us -> 18.4 us  [the longest x2 11.7 us: client_activations(): pl.pallas_call(functools.partial(client_kernel, start), grid=(units // wi...]
    pallas_call x1, Pallas kernels: 3.25 us -> 5.49 us  [select_rows(): pl.pallas_call(select_kernel, out_shape=(half, half), in_specs=[scalars,...]
  transfers between devices with their start and end apart: 46 -> 46, of which waited for: 26 -> 27; matrix products, arithmetic and copies ran while one was open for 1% -> 1% of each run, Pallas kernels for 16% -> 17%
where the time goes in v3:
time: 158 us; the launch traced here: 157 us
  waiting for transfers between devices  65.1 us (41%)
  starting transfers between devices  44.8 us (28%)
  Pallas kernels  41 us (26%)
  local copies, waits for them, and re-layouts  2.65 us (2%)
  other arithmetic  2.18 us (1%)
    ppermute x46, waiting for transfers between devices, xor_permute(): return lax.ppermute(value, axis, [(i, i ^ mask) for i in range(size)])  65.1 us
    ppermute x46, starting transfers between devices, xor_permute(): return lax.ppermute(value, axis, [(i, i ^ mask) for i in range(size)])  44.8 us
    pallas_call x2, Pallas kernels, match(): pl.pallas_call(functools.partial(match_kernel, len(columns)), grid=(rows...  15.2 us
    pallas_call x2, Pallas kernels, client_activations(): pl.pallas_call(functools.partial(client_kernel, start), grid=(units // wi...  11.7 us
    pallas_call x1, Pallas kernels, select_rows(): pl.pallas_call(select_kernel, out_shape=(half, half), in_specs=[scalars,...  5.49 us
    pallas_call x1, Pallas kernels, match_last(): pl.pallas_call(match_last_kernel, grid=(rows // high,), out_shape=(halves...  3.99 us
  transfers between devices with their start and end apart: 46, of which 27 were waited for; matrix products, arithmetic and copies ran while one was open for 1% of the time, Pallas kernels for 17%

profile of v3, /device:TPU:0, one launch (start us, length us, event | category | flops | bytes accessed | tf_op | source)
XLA Modules:
  0.0 156.9 jit_solution(2158348108983437310)
XLA Ops:
  2.1 5.5 %select_rows.1 = (bf16[4,256,512]{2,1,0:T(8,128)(2,1)S(1)}, bf16[4,256,512]{2,1,0:T(8,128)(2,1)S(1)}) custom-call(s32[2]{0:T(128)S(1)} %pad_add_fusion.place, s32[256]{0:T(256)S(1)} %copy-done.4, f32[1,4096]{1,0:T(1,128)S(1)} %bitcast.104, bf16[2048,4096]{1,0:T(8,128)(2,1)} %table.1), custom_call_target="tpu_custom_call" | custom-call | flops 4000000 | bytes 4000000 | tf_op jit(solution)/shard_map/select_rows/pallas_call | solution.py:99
  7.7 2.6 %collective-permute-done = bf16[4,256,512]{2,1,0:T(8,128)(2,1)S(1)} collective-permute-done((bf16[4,256,512]{2,1,0:T(8,128)(2,1)S(1)}, bf16[4,256,512]{2,1,0:T(8,128)(2,1)S(1)}, u32[]{:S(2)}, u32[]{:S(2)}) %collective-permute-start) | collective-permute-done | bytes 1048608 | tf_op jit(solution)/shard_map/ppermute | solution.py:33
  10.8 2.2 %collective-permute-start.1 = (bf16[128,512]{1,0:T(8,128)(2,1)S(1)}, bf16[128,512]{1,0:T(8,128)(2,1)S(1)}, u32[]{:S(2)}, u32[]{:S(2)}) collective-permute-start(bf16[128,512]{1,0:T(8,128)(2,1)S(1)} %get-tuple-element.36), channel_id=1, source_target_pairs={{0,8},{4,12},{8,0},{12,4},{16,24},{20,28},{24,16},{28,20},{1,9},{5... | collective-permute-start | bytes 393224 | tf_op jit(solution)/shard_map/ppermute | solution.py:33
  18.0 2.3 %collective-permute-start.8 = (bf16[128,512]{1,0:T(8,128)(2,1)S(1)}, bf16[128,512]{1,0:T(8,128)(2,1)S(1)}, u32[]{:S(2)}, u32[]{:S(2)}) collective-permute-start(bf16[128,512]{1,0:T(8,128)(2,1)S(1)} %get-tuple-element.37), channel_id=1, source_target_pairs={{0,24},{4,28},{8,16},{12,20},{16,8},{20,12},{24,0},{28,4},{1,25},{... | collective-permute-start | bytes 393224 | tf_op jit(solution)/shard_map/ppermute | solution.py:33
  27.1 3.3 %collective-permute-start.4 = (bf16[128,512]{1,0:T(8,128)(2,1)S(1)}, bf16[128,512]{1,0:T(8,128)(2,1)S(1)}, u32[]{:S(2)}, u32[]{:S(2)}) collective-permute-start(bf16[128,512]{1,0:T(8,128)(2,1)S(1)} %get-tuple-element.32), channel_id=1, source_target_pairs={{0,1},{1,0},{2,3},{3,2},{4,5},{5,4},{6,7},{7,6},{8,9},{9,8},{10,11... | collective-permute-start | bytes 393224 | tf_op jit(solution)/shard_map/ppermute | solution.py:33
  30.5 4.2 %collective-permute-done.4 = bf16[128,512]{1,0:T(8,128)(2,1)S(1)} collective-permute-done((bf16[128,512]{1,0:T(8,128)(2,1)S(1)}, bf16[128,512]{1,0:T(8,128)(2,1)S(1)}, u32[]{:S(2)}, u32[]{:S(2)}) %collective-permute-start.4) | collective-permute-done | bytes 131104 | tf_op jit(solution)/shard_map/ppermute | solution.py:33
  34.8 2.1 %collective-permute-start.5 = (bf16[128,512]{1,0:T(8,128)(2,1)S(1)}, bf16[128,512]{1,0:T(8,128)(2,1)S(1)}, u32[]{:S(2)}, u32[]{:S(2)}) collective-permute-start(bf16[128,512]{1,0:T(8,128)(2,1)S(1)} %add.90), channel_id=1, source_target_pairs={{0,2},{1,3},{2,0},{3,1},{4,6},{5,7},{6,4},{7,5},{8,10},{9,11},{10,... | collective-permute-start | bytes 393224 | tf_op jit(solution)/shard_map/ppermute | solution.py:33
  39.3 6.7 %collective-permute-done.5 = bf16[128,512]{1,0:T(8,128)(2,1)S(1)} collective-permute-done((bf16[128,512]{1,0:T(8,128)(2,1)S(1)}, bf16[128,512]{1,0:T(8,128)(2,1)S(1)}, u32[]{:S(2)}, u32[]{:S(2)}) %collective-permute-start.5) | collective-permute-done | bytes 131104 | tf_op jit(solution)/shard_map/ppermute | solution.py:33
  49.5 2.5 %collective-permute-done.11 = bf16[4,2,224,256]{3,2,1,0:T(8,128)(2,1)S(1)} collective-permute-done((bf16[4,2,224,256]{3,2,1,0:T(8,128)(2,1)S(1)}, bf16[4,2,224,256]{3,2,1,0:T(8,128)(2,1)S(1)}, u32[]{:S(2)}, u32[]{:S(2)}) %collective-permute-start.11) | collective-permute-done | bytes 917536 | tf_op jit(solution)/shard_map/ppermute | solution.py:33
  56.4 4.5 %collective-permute-done.12 = bf16[2,224,256]{2,1,0:T(8,128)(2,1)S(1)} collective-permute-done((bf16[2,224,256]{2,1,0:T(8,128)(2,1)S(1)}, bf16[2,224,256]{2,1,0:T(8,128)(2,1)S(1)}, u32[]{:S(2)}, u32[]{:S(2)}) %collective-permute-start.12) | collective-permute-done | bytes 229408 | tf_op jit(solution)/shard_map/ppermute | solution.py:33
  61.9 6.0 %collective-permute-start.28 = (bf16[256,512]{1,0:T(8,128)(2,1)S(1)}, bf16[256,512]{1,0:T(8,128)(2,1)S(1)}, u32[]{:S(2)}, u32[]{:S(2)}) collective-permute-start(bf16[256,512]{1,0:T(8,128)(2,1)S(1)} %tied.1), channel_id=1, source_target_pairs={{0,24},{4,28},{8,16},{12,20},{16,8},{20,12},{24,0},{28,4},{1,25},{... | collective-permute-start | bytes 786440 | tf_op jit(solution)/shard_map/ppermute | solution.py:33
  68.6 2.8 %collective-permute-done.24.refs_2_ = bf16[256,512]{1,0:T(8,128)(2,1)S(1)} collective-permute-done((bf16[256,512]{1,0:T(8,128)(2,1)S(1)}, bf16[256,512]{1,0:T(8,128)(2,1)S(1)}, u32[]{:S(2)}, u32[]{:S(2)}) %collective-permute-start.24) | collective-permute-done | bytes 262176 | tf_op jit(solution)/shard_map/ppermute | solution.py:33
  71.9 4.7 %collective-permute-done.28.refs_6_ = bf16[256,512]{1,0:T(8,128)(2,1)S(1)} collective-permute-done((bf16[256,512]{1,0:T(8,128)(2,1)S(1)}, bf16[256,512]{1,0:T(8,128)(2,1)S(1)}, u32[]{:S(2)}, u32[]{:S(2)}) %collective-permute-start.28) | collective-permute-done | bytes 262176 | tf_op jit(solution)/shard_map/ppermute | solution.py:33
  81.1 8.2 %client_activations.3.rest_0_ = bf16[256,1280]{1,0:T(8,128)(2,1)S(1)} custom-call(s32[2]{0:T(128)S(1)} %pad_add_fusion.place, bf16[256,512]{1,0:T(8,128)(2,1)S(1)} %pad_maximum_fusion.rows.value.refs_0_, bf16[256,512]{1,0:T(8,128)(2,1)S(1)} %collective-permute-done.23.refs_1_, bf16[256,512]{1,0:T(8,128)(2,1)S(1)} %collective-permute-done.24.refs_2_, ...), custom_call_target="tpu_custom_call" | custom-call | flops 5368709120 | bytes 20971520 | tf_op jit(solution)/shard_map/client_activations/pallas_call | solution.py:151
  89.4 3.5 %client_activations.2.rest_1_ = bf16[256,512]{1,0:T(8,128)(2,1)S(1)} custom-call(s32[2]{0:T(128)S(1)} %pad_add_fusion.place, bf16[256,512]{1,0:T(8,128)(2,1)S(1)} %pad_maximum_fusion.rows.value.refs_0_, bf16[256,512]{1,0:T(8,128)(2,1)S(1)} %collective-permute-done.23.refs_1_, bf16[256,512]{1,0:T(8,128)(2,1)S(1)} %collective-permute-done.24.refs_2_, ...), custom_call_target="tpu_custom_call" | custom-call | flops 2147483648 | bytes 8388608 | tf_op jit(solution)/shard_map/client_activations/pallas_call | solution.py:151
  97.3 9.1 %match.2 = (f32[3584,256]{1,0:T(8,128)S(1)}, f32[2,3584]{1,0:T(2,128)S(1)}) custom-call(bf16[3584,256]{1,0:T(8,128)(2,1)S(1)} %bitcast.101, bf16[256,1280]{1,0:T(8,128)(2,1)S(1)} %client_activations.3.rest_0_, bf16[256,512]{1,0:T(8,128)(2,1)S(1)} %client_activations.2.rest_1_), custom_call_target="tpu_custom_call" | custom-call | flops 6576668672 | bytes 7340032 | tf_op jit(solution)/shard_map/match/pallas_call | solution.py:322
  107.1 6.1 %match.3 = (f32[3584,256]{1,0:T(8,128)S(1)}, f32[2,3584]{1,0:T(2,128)S(1)}) custom-call(bf16[3584,256]{1,0:T(8,128)(2,1)S(1)} %bitcast.102, bf16[256,1280]{1,0:T(8,128)(2,1)S(1)} %collective-permute-done.31.rest_0_, f32[3584,256]{1,0:T(8,128)S(1)} %get-tuple-element.19.rest_1_, f32[2,3584]{1,0:T(2,128)S(1)} %get-tuple-element.20.rest_2_), custom_call_target="tpu_custom_call" | custom-call | flops 4697620480 | bytes 7340032 | tf_op jit(solution)/shard_map/match/pallas_call | solution.py:322
  113.2 4.0 %match_last.1 = (bf16[4,2,224,256]{3,2,1,0:T(8,128)(2,1)S(1)}, bf16[4,2,224,256]{3,2,1,0:T(8,128)(2,1)S(1)}, f32[2,3584]{1,0:T(2,128)S(1)}) custom-call(bf16[3584,256]{1,0:T(8,128)(2,1)S(1)} %bitcast.103, bf16[256,512]{1,0:T(8,128)(2,1)S(1)} %collective-permute-done.30.columns, f32[3584,256]{1,0:T(8,128)S(1)} %get-tuple-element.21.before, ...), custom_call_target="tpu_custom_call" | custom-call | flops 1879048192 | bytes 7340032 | tf_op jit(solution)/shard_map/match_last/pallas_call | solution.py:347
  118.4 3.7 %collective-permute-done.33 = f32[2,2,1792]{2,1,0:T(2,128)S(1)} collective-permute-done((f32[2,2,1792]{2,1,0:T(2,128)S(1)}, f32[2,2,1792]{2,1,0:T(2,128)S(1)}, u32[]{:S(2)}, u32[]{:S(2)}) %collective-permute-start.33) | collective-permute-done | bytes 28704 | tf_op jit(solution)/shard_map/ppermute | solution.py:33
  127.8 5.0 %collective-permute-done.35 = bf16[2,224,256]{2,1,0:T(8,128)(2,1)S(1)} collective-permute-done((bf16[2,224,256]{2,1,0:T(8,128)(2,1)S(1)}, bf16[2,224,256]{2,1,0:T(8,128)(2,1)S(1)}, u32[]{:S(2)}, u32[]{:S(2)}) %collective-permute-start.35) | collective-permute-done | bytes 229408 | tf_op jit(solution)/shard_map/ppermute | solution.py:33
  132.8 5.1 %collective-permute-done.36 = bf16[2,224,256]{2,1,0:T(8,128)(2,1)S(1)} collective-permute-done((bf16[2,224,256]{2,1,0:T(8,128)(2,1)S(1)}, bf16[2,224,256]{2,1,0:T(8,128)(2,1)S(1)}, u32[]{:S(2)}, u32[]{:S(2)}) %collective-permute-start.36) | collective-permute-done | bytes 229408 | tf_op jit(solution)/shard_map/ppermute | solution.py:33
  139.1 6.1 %collective-permute-done.38 = bf16[224,256]{1,0:T(8,128)(2,1)S(1)} collective-permute-done((bf16[224,256]{1,0:T(8,128)(2,1)S(1)}, bf16[224,256]{1,0:T(8,128)(2,1)S(1)}, u32[]{:S(2)}, u32[]{:S(2)}) %collective-permute-start.38) | collective-permute-done | bytes 114720 | tf_op jit(solution)/shard_map/ppermute | solution.py:33
  148.9 2.1 %collective-permute-done.40.refs_2_ = bf16[224,256]{1,0:T(8,128)(2,1)S(1)} collective-permute-done((bf16[224,256]{1,0:T(8,128)(2,1)S(1)}, bf16[224,256]{1,0:T(8,128)(2,1)S(1)}, u32[]{:S(2)}, u32[]{:S(2)}) %collective-permute-start.40) | collective-permute-done | bytes 114720 | tf_op jit(solution)/shard_map/ppermute | solution.py:33
  151.0 2.5 %collective-permute-done.42.refs_4_ = bf16[224,256]{1,0:T(8,128)(2,1)S(1)} collective-permute-done((bf16[224,256]{1,0:T(8,128)(2,1)S(1)}, bf16[224,256]{1,0:T(8,128)(2,1)S(1)}, u32[]{:S(2)}, u32[]{:S(2)}) %collective-permute-start.42) | collective-permute-done | bytes 114720 | tf_op jit(solution)/shard_map/ppermute | solution.py:33
  (141 shorter events, 50.8 us)
Async XLA Ops:
  13.0 8.7 %collective-permute-start.2 = (bf16[128,512]{1,0:T(8,128)(2,1)S(1)}, bf16[128,512]{1,0:T(8,128)(2,1)S(1)}, u32[]{:S(2)}, u32[]{:S(2)}) collective-permute-start(bf16[128,512]{1,0:T(8,128)(2,1)S(1)} %get-tuple-element.41), channel_id=1, source_target_pairs={{0,16},{4,20},{8,24},{12,28},{16,0},{20,4},{24,8},{28,12},{1,17},{... | collective-permute-start | bytes 393224 | tf_op jit(solution)/shard_map/ppermute | solution.py:33
  15.0 8.7 %collective-permute-start.6 = (bf16[128,512]{1,0:T(8,128)(2,1)S(1)}, bf16[128,512]{1,0:T(8,128)(2,1)S(1)}, u32[]{:S(2)}, u32[]{:S(2)}) collective-permute-start(bf16[128,512]{1,0:T(8,128)(2,1)S(1)} %get-tuple-element.39), channel_id=1, source_target_pairs={{0,8},{4,12},{8,0},{12,4},{16,24},{20,28},{24,16},{28,20},{1,9},{5... | collective-permute-start | bytes 393224 | tf_op jit(solution)/shard_map/ppermute | solution.py:33
  16.5 9.3 %collective-permute-start.7 = (bf16[128,512]{1,0:T(8,128)(2,1)S(1)}, bf16[128,512]{1,0:T(8,128)(2,1)S(1)}, u32[]{:S(2)}, u32[]{:S(2)}) collective-permute-start(bf16[128,512]{1,0:T(8,128)(2,1)S(1)} %get-tuple-element.38), channel_id=1, source_target_pairs={{0,16},{4,20},{8,24},{12,28},{16,0},{20,4},{24,8},{28,12},{1,17},{... | collective-permute-start | bytes 393224 | tf_op jit(solution)/shard_map/ppermute | solution.py:33
  18.0 9.0 %collective-permute-start.8 = (bf16[128,512]{1,0:T(8,128)(2,1)S(1)}, bf16[128,512]{1,0:T(8,128)(2,1)S(1)}, u32[]{:S(2)}, u32[]{:S(2)}) collective-permute-start(bf16[128,512]{1,0:T(8,128)(2,1)S(1)} %get-tuple-element.37), channel_id=1, source_target_pairs={{0,24},{4,28},{8,16},{12,20},{16,8},{20,12},{24,0},{28,4},{1,25},{... | collective-permute-start | bytes 393224 | tf_op jit(solution)/shard_map/ppermute | solution.py:33
  34.8 11.3 %collective-permute-start.5 = (bf16[128,512]{1,0:T(8,128)(2,1)S(1)}, bf16[128,512]{1,0:T(8,128)(2,1)S(1)}, u32[]{:S(2)}, u32[]{:S(2)}) collective-permute-start(bf16[128,512]{1,0:T(8,128)(2,1)S(1)} %add.90), channel_id=1, source_target_pairs={{0,2},{1,3},{2,0},{3,1},{4,6},{5,7},{6,4},{7,5},{8,10},{9,11},{10,... | collective-permute-start | bytes 393224 | tf_op jit(solution)/shard_map/ppermute | solution.py:33
  37.7 9.8 %collective-permute-start.10 = (bf16[128,512]{1,0:T(8,128)(2,1)S(1)}, bf16[128,512]{1,0:T(8,128)(2,1)S(1)}, u32[]{:S(2)}, u32[]{:S(2)}) collective-permute-start(bf16[128,512]{1,0:T(8,128)(2,1)S(1)} %add.95), channel_id=1, source_target_pairs={{0,2},{1,3},{2,0},{3,1},{4,6},{5,7},{6,4},{7,5},{8,10},{9,11},{10,... | collective-permute-start | bytes 393224 | tf_op jit(solution)/shard_map/ppermute | solution.py:33
  52.3 8.5 %collective-permute-start.12 = (bf16[2,224,256]{2,1,0:T(8,128)(2,1)S(1)}, bf16[2,224,256]{2,1,0:T(8,128)(2,1)S(1)}, u32[]{:S(2)}, u32[]{:S(2)}) collective-permute-start(bf16[2,224,256]{2,1,0:T(8,128)(2,1)S(1)} %get-tuple-element.42), channel_id=1, source_target_pairs={{0,8},{4,12},{8,0},{12,4},{16,24},{20,28},{24,16},{28,20},{1,9},{5... | collective-permute-start | bytes 688136 | tf_op jit(solution)/shard_map/ppermute | solution.py:33
  52.8 9.1 %collective-permute-start.13 = (bf16[2,224,256]{2,1,0:T(8,128)(2,1)S(1)}, bf16[2,224,256]{2,1,0:T(8,128)(2,1)S(1)}, u32[]{:S(2)}, u32[]{:S(2)}) collective-permute-start(bf16[2,224,256]{2,1,0:T(8,128)(2,1)S(1)} %get-tuple-element.44), channel_id=1, source_target_pairs={{0,16},{4,20},{8,24},{12,28},{16,0},{20,4},{24,8},{28,12},{1,17},{... | collective-permute-start | bytes 688136 | tf_op jit(solution)/shard_map/ppermute | solution.py:33
  54.4 13.5 %collective-permute-start.14 = (bf16[2,224,256]{2,1,0:T(8,128)(2,1)S(1)}, bf16[2,224,256]{2,1,0:T(8,128)(2,1)S(1)}, u32[]{:S(2)}, u32[]{:S(2)}) collective-permute-start(bf16[2,224,256]{2,1,0:T(8,128)(2,1)S(1)} %get-tuple-element.43), channel_id=1, source_target_pairs={{0,24},{4,28},{8,16},{12,20},{16,8},{20,12},{24,0},{28,4},{1,25},{... | collective-permute-start | bytes 688136 | tf_op jit(solution)/shard_map/ppermute | solution.py:33
  55.9 21.6 %collective-permute-start.23 = (bf16[256,512]{1,0:T(8,128)(2,1)S(1)}, bf16[256,512]{1,0:T(8,128)(2,1)S(1)}, u32[]{:S(2)}, u32[]{:S(2)}) collective-permute-start(bf16[256,512]{1,0:T(8,128)(2,1)S(1)} %pad_maximum_fusion.rows.value.refs_0_), channel_id=1, source_target_pairs={{0,4},{4,0},{8,12},{12,8},{16,20},{20,16},{24,28},{28,24},{1,5},{5... | collective-permute-start | bytes 786440 | tf_op jit(solution)/shard_map/ppermute | solution.py:33
  55.9 15.5 %collective-permute-start.24 = (bf16[256,512]{1,0:T(8,128)(2,1)S(1)}, bf16[256,512]{1,0:T(8,128)(2,1)S(1)}, u32[]{:S(2)}, u32[]{:S(2)}) collective-permute-start(bf16[256,512]{1,0:T(8,128)(2,1)S(1)} %tied.1), channel_id=1, source_target_pairs={{0,8},{4,12},{8,0},{12,4},{16,24},{20,28},{24,16},{28,20},{1,9},{5... | collective-permute-start | bytes 786440 | tf_op jit(solution)/shard_map/ppermute | solution.py:33
  60.9 10.9 %collective-permute-start.26 = (bf16[256,512]{1,0:T(8,128)(2,1)S(1)}, bf16[256,512]{1,0:T(8,128)(2,1)S(1)}, u32[]{:S(2)}, u32[]{:S(2)}) collective-permute-start(bf16[256,512]{1,0:T(8,128)(2,1)S(1)} %tied.1), channel_id=1, source_target_pairs={{0,16},{4,20},{8,24},{12,28},{16,0},{20,4},{24,8},{28,12},{1,17},{... | collective-permute-start | bytes 786440 | tf_op jit(solution)/shard_map/ppermute | solution.py:33
  61.9 14.8 %collective-permute-start.28 = (bf16[256,512]{1,0:T(8,128)(2,1)S(1)}, bf16[256,512]{1,0:T(8,128)(2,1)S(1)}, u32[]{:S(2)}, u32[]{:S(2)}) collective-permute-start(bf16[256,512]{1,0:T(8,128)(2,1)S(1)} %tied.1), channel_id=1, source_target_pairs={{0,24},{4,28},{8,16},{12,20},{16,8},{20,12},{24,0},{28,4},{1,25},{... | collective-permute-start | bytes 786440 | tf_op jit(solution)/shard_map/ppermute | solution.py:33
  68.5 8.3 %collective-permute-start.15 = (bf16[224,256]{1,0:T(8,128)(2,1)S(1)}, bf16[224,256]{1,0:T(8,128)(2,1)S(1)}, u32[]{:S(2)}, u32[]{:S(2)}) collective-permute-start(bf16[224,256]{1,0:T(8,128)(2,1)S(1)} %multiply_convert_fusion), channel_id=1, source_target_pairs={{0,2},{1,3},{2,0},{3,1},{4,6},{5,7},{6,4},{7,5},{8,10},{9,11},{10,... | collective-permute-start | bytes 344072 | tf_op jit(solution)/shard_map/ppermute | solution.py:33
  71.8 8.0 %collective-permute-start.27 = (bf16[256,512]{1,0:T(8,128)(2,1)S(1)}, bf16[256,512]{1,0:T(8,128)(2,1)S(1)}, u32[]{:S(2)}, u32[]{:S(2)}) collective-permute-start(bf16[256,512]{1,0:T(8,128)(2,1)S(1)} %collective-permute-done.26.refs_4_), channel_id=1, source_target_pairs={{0,4},{4,0},{8,12},{12,8},{16,20},{20,16},{24,28},{28,24},{1,5},{5... | collective-permute-start | bytes 786440 | tf_op jit(solution)/shard_map/ppermute | solution.py:33
  76.9 16.1 %collective-permute-start.16 = (bf16[2,224,256]{2,1,0:T(8,128)(2,1)S(1)}, bf16[2,224,256]{2,1,0:T(8,128)(2,1)S(1)}, u32[]{:S(2)}, u32[]{:S(2)}) collective-permute-start(bf16[2,224,256]{2,1,0:T(8,128)(2,1)S(1)} %pad_maximum_fusion.1), channel_id=1, source_target_pairs={{0,4},{4,0},{8,12},{12,8},{16,20},{20,16},{24,28},{28,24},{1,5},{5... | collective-permute-start | bytes 688136 | tf_op jit(solution)/shard_map/ppermute | solution.py:33
  77.5 17.5 %collective-permute-start.17 = (bf16[2,224,256]{2,1,0:T(8,128)(2,1)S(1)}, bf16[2,224,256]{2,1,0:T(8,128)(2,1)S(1)}, u32[]{:S(2)}, u32[]{:S(2)}) collective-permute-start(bf16[2,224,256]{2,1,0:T(8,128)(2,1)S(1)} %pad_maximum_fusion.1), channel_id=1, source_target_pairs={{0,8},{4,12},{8,0},{12,4},{16,24},{20,28},{24,16},{28,20},{1,9},{5... | collective-permute-start | bytes 688136 | tf_op jit(solution)/shard_map/ppermute | solution.py:33
  78.8 16.2 %collective-permute-start.19 = (bf16[2,224,256]{2,1,0:T(8,128)(2,1)S(1)}, bf16[2,224,256]{2,1,0:T(8,128)(2,1)S(1)}, u32[]{:S(2)}, u32[]{:S(2)}) collective-permute-start(bf16[2,224,256]{2,1,0:T(8,128)(2,1)S(1)} %pad_maximum_fusion.1), channel_id=1, source_target_pairs={{0,16},{4,20},{8,24},{12,28},{16,0},{20,4},{24,8},{28,12},{1,17},{... | collective-permute-start | bytes 688136 | tf_op jit(solution)/shard_map/ppermute | solution.py:33
  79.8 15.7 %collective-permute-start.21 = (bf16[2,224,256]{2,1,0:T(8,128)(2,1)S(1)}, bf16[2,224,256]{2,1,0:T(8,128)(2,1)S(1)}, u32[]{:S(2)}, u32[]{:S(2)}) collective-permute-start(bf16[2,224,256]{2,1,0:T(8,128)(2,1)S(1)} %pad_maximum_fusion.1), channel_id=1, source_target_pairs={{0,24},{4,28},{8,16},{12,20},{16,8},{20,12},{24,0},{28,4},{1,25},{... | collective-permute-start | bytes 688136 | tf_op jit(solution)/shard_map/ppermute | solution.py:33
  89.3 17.7 %collective-permute-start.31 = (bf16[256,1280]{1,0:T(8,128)(2,1)S(1)}, bf16[256,1280]{1,0:T(8,128)(2,1)S(1)}, u32[]{:S(2)}, u32[]{:S(2)}) collective-permute-start(bf16[256,1280]{1,0:T(8,128)(2,1)S(1)} %client_activations.3.rest_0_), channel_id=1, source_target_pairs={{0,1},{1,0},{2,3},{3,2},{4,5},{5,4},{6,7},{7,6},{8,9},{9,8},{10,11... | collective-permute-start | bytes 1966088 | tf_op jit(solution)/shard_map/ppermute | solution.py:33
  92.9 20.2 %collective-permute-start.30 = (bf16[256,512]{1,0:T(8,128)(2,1)S(1)}, bf16[256,512]{1,0:T(8,128)(2,1)S(1)}, u32[]{:S(2)}, u32[]{:S(2)}) collective-permute-start(bf16[256,512]{1,0:T(8,128)(2,1)S(1)} %client_activations.2.rest_1_), channel_id=1, source_target_pairs={{0,1},{1,0},{2,3},{3,2},{4,5},{5,4},{6,7},{7,6},{8,9},{9,8},{10,11... | collective-permute-start | bytes 786440 | tf_op jit(solution)/shard_map/ppermute | solution.py:33
  124.3 8.5 %collective-permute-start.35 = (bf16[2,224,256]{2,1,0:T(8,128)(2,1)S(1)}, bf16[2,224,256]{2,1,0:T(8,128)(2,1)S(1)}, u32[]{:S(2)}, u32[]{:S(2)}) collective-permute-start(bf16[2,224,256]{2,1,0:T(8,128)(2,1)S(1)} %get-tuple-element.45), channel_id=1, source_target_pairs={{0,8},{4,12},{8,0},{12,4},{16,24},{20,28},{24,16},{28,20},{1,9},{5... | collective-permute-start | bytes 688136 | tf_op jit(solution)/shard_map/ppermute | solution.py:33
  125.6 12.3 %collective-permute-start.36 = (bf16[2,224,256]{2,1,0:T(8,128)(2,1)S(1)}, bf16[2,224,256]{2,1,0:T(8,128)(2,1)S(1)}, u32[]{:S(2)}, u32[]{:S(2)}) collective-permute-start(bf16[2,224,256]{2,1,0:T(8,128)(2,1)S(1)} %get-tuple-element.47), channel_id=1, source_target_pairs={{0,16},{4,20},{8,24},{12,28},{16,0},{20,4},{24,8},{28,12},{1,17},{... | collective-permute-start | bytes 688136 | tf_op jit(solution)/shard_map/ppermute | solution.py:33
  126.6 11.3 %collective-permute-start.37 = (bf16[2,224,256]{2,1,0:T(8,128)(2,1)S(1)}, bf16[2,224,256]{2,1,0:T(8,128)(2,1)S(1)}, u32[]{:S(2)}, u32[]{:S(2)}) collective-permute-start(bf16[2,224,256]{2,1,0:T(8,128)(2,1)S(1)} %get-tuple-element.46), channel_id=1, source_target_pairs={{0,24},{4,28},{8,16},{12,20},{16,8},{20,12},{24,0},{28,4},{1,25},{... | collective-permute-start | bytes 688136 | tf_op jit(solution)/shard_map/ppermute | solution.py:33
  (31 other events, 522.0 us)

commit v4 on v3

--- a/solution.py
+++ b/solution.py
@@ -202,30 +202,21 @@
     )(place, rows, ref_gate, ref_up)
 
 
-def matched(rows, columns, total, with_sums):
+def matched(rows, columns, total):
     tokens = rows.shape[1]
     colsum = jnp.zeros((rows.shape[0], 128), f32)
-    weighted = jnp.zeros((rows.shape[0], 128), f32)
     for source in columns:
         wide = unit_block(source.shape[1])
         for i in range(0, source.shape[1], wide):
             some = source[:, i : i + wide]
             r = jnp.dot(rows, some, preferred_element_type=f32)
             w = jnp.exp2(r * (sharpness * log2_e / tokens))
-            if total is not None:
-                total += lax.dot_general(
-                    w.astype(bf16), some, (((1,), (1,)), ((), ())), preferred_element_type=f32
-                )
-            if with_sums:
-                wr = w * r
-                for k in range(0, wide, 128):
-                    colsum += w[:, k : k + 128]
-                    weighted += wr[:, k : k + 128]
-    if not with_sums:
-        return total
-    row = jnp.sum(colsum.T, axis=0, keepdims=True)
-    row_weighted = jnp.sum(weighted.T, axis=0, keepdims=True) * (1.0 / tokens)
-    return total, row, row_weighted
+            total += lax.dot_general(
+                w.astype(bf16), some, (((1,), (1,)), ((), ())), preferred_element_type=f32
+            )
+            for k in range(0, wide, 128):
+                colsum += w[:, k : k + 128]
+    return total, jnp.sum(colsum.T, axis=0, keepdims=True)
 
 
 def match_kernel(sources, refs, *rest):
@@ -233,104 +224,95 @@
     numerator, sums = rest[-2:]
     before = rest[:-2]
     start = before[0][...] if before else jnp.zeros(numerator.shape, f32)
-    total, row, row_weighted = matched(refs[...], columns, start, True)
-    numerator[...] = total
-    if before:
-        row = row + before[1][0:1, :]
-        row_weighted = row_weighted + before[1][1:2, :]
+    numerator[...], row = matched(refs[...], columns, start)
+    sums[...] = row + before[1][...] if before else row
+
+
+def match_last_kernel(refs, columns, before, sums_before, keep, send, sums):
+    total, row = matched(refs[...], [columns], before[...])
+    tokens, lanes = total.shape[1], 128
+    row = row + sums_before[...]
     sums[0:1, :] = row
-    sums[1:2, :] = row_weighted
-
-
-def match_last_kernel(refs, columns, before, sums_before, keep, send, sums):
-    total, row, row_weighted = matched(refs[...], [columns], before[...], True)
-    row = row + sums_before[0:1, :]
-    sums[0:1, :] = row
-    sums[1:2, :] = row_weighted + sums_before[1:2, :]
-    lanes = 128
+    weighted = total * refs[...].astype(f32)
+    weighted = sum(weighted[:, k : k + lanes] for k in range(0, tokens, lanes))
+    sums[1:2, :] = jnp.sum(weighted.T, axis=0, keepdims=True) * (1.0 / tokens)
     by_row = jnp.broadcast_to(1.0 / row, (lanes, total.shape[0])).T
     size = keep.shape[2]
     for p in range(2 * keep.shape[0]):
         target = send if p % 2 else keep
         units = slice(p * size, (p + 1) * size)
-        for k in range(0, total.shape[1], lanes):
+        for k in range(0, tokens, lanes):
             target[p // 2, 0, :, k : k + lanes] = (total[units, k : k + lanes] * by_row[units]).astype(
                 target.dtype
             )
 
 
-def join_kernel(keep, arrived, factor, factor_arrived, first, others):
-    pairs, groups, size, tokens = keep.shape
+def join_kernel(group, keep, arrived, factor, factor_arrived, *refs):
+    pairs, _, size, tokens = keep.shape
+    first, *others = refs[-pairs:]
     lanes = 128
     units = 2 * pairs * size
-    for g in range(groups):
-        rows = [
-            jnp.broadcast_to(source[:, g * units : (g + 1) * units], (lanes, units)).T
-            for source in (factor, factor_arrived)
-        ]
-        for h in range(pairs):
-            ours = slice(2 * h * size, (2 * h + 1) * size)
-            theirs = slice((2 * h + 1) * size, (2 * h + 2) * size)
-            for k in range(0, tokens, lanes):
-                at = slice(k, k + lanes)
-                total = keep[h, g, :, at].astype(f32) * rows[0][ours]
-                total += arrived[h, g, :, at].astype(f32) * rows[1][theirs]
-                if h:
-                    others[h - 1, g, :, at] = total.astype(bf16)
-                else:
-                    first[g, :, at] = total
-
-
-def joined(keep, arrived, factor, factor_arrived):
-    pairs, groups, size, tokens = keep.shape
-    return pl.pallas_call(
-        join_kernel,
-        out_shape=(
-            jax.ShapeDtypeStruct((groups, size, tokens), f32),
-            jax.ShapeDtypeStruct((pairs - 1, groups, size, tokens), bf16),
-        ),
-        in_specs=[whole] * 4,
-        out_specs=(whole, whole),
+    rows = [
+        jnp.broadcast_to(source[:, group * units : (group + 1) * units], (lanes, units)).T
+        for source in (factor, factor_arrived)
+    ]
+    for h in range(pairs):
+        ours = slice(2 * h * size, (2 * h + 1) * size)
+        theirs = slice((2 * h + 1) * size, (2 * h + 2) * size)
+        for k in range(0, tokens, lanes):
+            at = slice(k, k + lanes)
+            total = keep[h, group, :, at].astype(f32) * rows[0][ours]
+            total += arrived[h, group, :, at].astype(f32) * rows[1][theirs]
+            if h:
+                others[h - 1][:, at] = total.astype(bf16)
+            else:
+                first[:, at] = total
+
+
+def joined(group, keep, arrived, factor, factor_arrived, after):
+    pairs, _, size, tokens = keep.shape
+    piece = jax.ShapeDtypeStruct((size, tokens), bf16)
+    return pl.pallas_call(
+        functools.partial(join_kernel, group),
+        out_shape=(jax.ShapeDtypeStruct((size, tokens), f32), *[piece] * (pairs - 1)),
+        in_specs=[whole] * 4 + [anywhere] * len(after),
+        out_specs=(whole,) * pairs,
         compiler_params=vmem_params(16),
-        cost_estimate=cost(4 * keep.size, 6 * keep.size),
+        cost_estimate=cost(4 * pairs * size * tokens, 6 * pairs * size * tokens),
         name="joined",
-    )(keep, arrived, factor, factor_arrived)
-
-
-high = 896
+    )(keep, arrived, factor, factor_arrived, *after)
 
 
 def match_cost(rows, tokens, units):
     return cost(4 * rows * units * tokens, 8 * rows * tokens, rows * units)
 
 
-def by_rows(width):
-    return pl.BlockSpec((high, width), lambda j: (j, 0))
-
-
-def by_columns(rows):
-    return pl.BlockSpec((rows, high), lambda j: (0, j))
+def match_specs(rows, tokens, groups):
+    high = rows // groups
+    by_rows = pl.BlockSpec((high, tokens), lambda j: (j, 0))
+    return by_rows, *[pl.BlockSpec((n, high), lambda j: (0, j)) for n in (1, 2)]
 
 
 def unblocked(value):
     return pl.BlockSpec(value.shape, lambda j: (0, 0))
 
 
-def match(refs, columns, before=()):
+def match(refs, columns, groups, before=()):
     rows, tokens = refs.shape
     units = sum(source.shape[1] for source in columns)
+    by_rows, one_row, _ = match_specs(rows, tokens, groups)
     return pl.pallas_call(
         functools.partial(match_kernel, len(columns)),
-        grid=(rows // high,),
+        grid=(groups,),
         out_shape=(
             jax.ShapeDtypeStruct((rows, tokens), f32),
-            jax.ShapeDtypeStruct((2, rows), f32),
+            jax.ShapeDtypeStruct((1, rows), f32),
         ),
-        in_specs=[by_rows(tokens)]
+        in_specs=[by_rows]
         + [unblocked(source) for source in columns]
-        + [by_rows(tokens), by_columns(2)][: len(before)],
-        out_specs=(by_rows(tokens), by_columns(2)),
-        compiler_params=vmem_params(20),
+        + [by_rows, one_row][: len(before)],
+        out_specs=(by_rows, one_row),
+        compiler_params=vmem_params(24),
         cost_estimate=match_cost(rows, tokens, units),
         name="match",
     )(refs, *columns, *before)
@@ -338,19 +320,17 @@
 
 def match_last(refs, columns, before, sums, clients, groups):
     rows, tokens = refs.shape
-    size = rows // groups // clients
-    steps = rows // groups // high
-    pairs = max(1, clients // 2 // steps)
-    shape = (clients // 2, groups, size, tokens)
-    pieces = pl.BlockSpec((pairs, 1, size, tokens), lambda j: (j % steps, j // steps, 0, 0))
+    by_rows, one_row, two_rows = match_specs(rows, tokens, groups)
+    shape = (clients // 2, groups, rows // groups // clients, tokens)
+    pieces = pl.BlockSpec((shape[0], 1, shape[2], tokens), lambda j: (0, j, 0, 0))
     halves = jax.ShapeDtypeStruct(shape, bf16)
     return pl.pallas_call(
         match_last_kernel,
-        grid=(rows // high,),
+        grid=(groups,),
         out_shape=(halves, halves, jax.ShapeDtypeStruct((2, rows), f32)),
-        in_specs=[by_rows(tokens), unblocked(columns), by_rows(tokens), by_columns(2)],
-        out_specs=(pieces, pieces, by_columns(2)),
-        compiler_params=vmem_params(20),
+        in_specs=[by_rows, unblocked(columns), by_rows, one_row],
+        out_specs=(pieces, pieces, two_rows),
+        compiler_params=vmem_params(24),
         cost_estimate=match_cost(rows, tokens, columns.shape[1]),
         name="match_last",
     )(refs, columns, before, sums)
@@ -372,24 +352,34 @@
 
 
 def place_kernel(place, *refs):
-    *pieces, out = refs
-    size = pieces[0].shape[0]
-    for p, piece in enumerate(pieces):
-        at = pl.ds(pl.multiple_of((place[1] ^ p) * size, 8), size)
-        out[at, :] = piece[...].astype(f32)
-
-
-def placed(place, pieces):
+    *pieces, out, wide, sems = refs
+    pieces = pieces[: wide.shape[0]]
+    size = wide.shape[1]
+    copies = []
+    for i, piece in enumerate(pieces):
+        at = pl.ds(pl.multiple_of((place[1] ^ i) * size, 8), size)
+        wide[i] = piece[...].astype(f32)
+        copies.append(pltpu.make_async_copy(wide.at[i], out.at[at, :], sems.at[i]))
+        copies[-1].start()
+    for copy in copies:
+        copy.wait()
+
+
+def placed(place, pieces, units, after):
     size, tokens = pieces[0].shape
     return pl.pallas_call(
         place_kernel,
-        out_shape=jax.ShapeDtypeStruct((size * len(pieces), tokens), f32),
-        in_specs=[scalars] + [whole] * len(pieces),
-        out_specs=whole,
+        out_shape=jax.ShapeDtypeStruct((units, tokens), f32),
+        in_specs=[scalars] + [whole] * len(pieces) + [anywhere] * len(after),
+        out_specs=anywhere,
+        scratch_shapes=[
+            pltpu.VMEM((len(pieces), size, tokens), f32),
+            pltpu.SemaphoreType.DMA((len(pieces),)),
+        ],
         compiler_params=vmem_params(16),
-        cost_estimate=cost(1e5, 6 * size * len(pieces) * tokens),
+        cost_estimate=cost(1e5, 6 * units * tokens),
         name="placed",
-    )(place, *pieces)
+    )(place, *pieces, *after)
 
 
 def body(clients, parts, token_ids, embed_table, norm_gain, client_gate, client_up, ref_gate, ref_up):
@@ -444,16 +434,17 @@
     refs = jnp.stack(gathered(ref_pieces), axis=1).reshape(groups * clients * piece, tokens)
 
     units = client_gate.shape[2]
-    cuts = [0, 5 * units // 7, units]
+    cuts = [0, 3 * units // 7, units]
     own = [
         client_activations(place, blocks, client_gate, client_up, first, last)
         for first, last in zip(cuts, cuts[1:])
     ]
     theirs = [over_units(part, mask=1) for part in own]
-    numerator, sums = match(refs, own)
-    numerator, sums = match(refs, theirs[:1], (numerator, sums))
+    numerator, sums = match(refs, own, groups)
+    numerator, sums = match(refs, theirs[:1], groups, (numerator, sums))
     keep, send, sums = match_last(refs, theirs[1], numerator, sums, clients, groups)
     arrived = over_clients(send, mask=1)
+
     sums = sums.reshape(2, groups, clients * piece)
     all_sums = sums
     for k in even[1:]:
@@ -461,11 +452,15 @@
         all_sums = all_sums + jnp.stack([other[:, g ^ (k // 2)] for g in range(groups)], axis=1)
     colsum, weighted = all_sums[0], all_sums[1]
     factor = (sums[0] * (1.0 / clients) / colsum).reshape(1, groups * clients * piece)
-    first, others = joined(keep, arrived, factor, over_clients(factor, mask=1))
-    arrived = [over_clients(others[p // 2 - 1], mask=p) for p in range(2, clients, 2)]
-    reduced = first
-    for other in arrived:
-        reduced = reduced + other.astype(f32)
+    factor_arrived = over_clients(factor, mask=1)
+    reduced = [None] * groups
+    after = ()
+    for g in reversed(range(groups)):
+        first, *others = joined(g, keep, arrived, factor, factor_arrived, after)
+        after = others[:1]
+        reduced[g] = first
+        for p in range(2, clients, 2):
+            reduced[g] = reduced[g] + over_clients(others[p // 2 - 1], mask=p).astype(f32)
 
     score = (weighted[0] / colsum[0]).reshape(clients, piece)
     here = jnp.arange(clients)[:, None] ^ client == jnp.arange(clients)[None, :]
@@ -475,7 +470,8 @@
     mine = reduced[0]
     for k in even[1:]:
         mine = mine + over_units(reduced[k // 2].astype(bf16), mask=k).astype(f32)
-    merged = placed(place, gathered(mine.astype(bf16)))
+    pieces = gathered(mine.astype(bf16))
+    merged = placed(place, pieces, units, [score])
     return (merged, score)
 
 

time: 158 us -> 149 us (0.943)
  waiting for transfers between devices: 65.1 us -> 54.2 us
  starting transfers between devices: 44.8 us -> 52 us
  Pallas kernels: 41 us -> 37.4 us
    ppermute x46 -> x49, waiting for transfers between devices: 65.1 us -> 54.2 us  [xor_permute(): return lax.ppermute(value, axis, [(i, i ^ mask) for i in range(size)])]
    ppermute x46 -> x49, starting transfers between devices: 44.8 us -> 52 us  [xor_permute(): return lax.ppermute(value, axis, [(i, i ^ mask) for i in range(size)])]
    pallas_call x5 -> x6, Pallas kernels: 21.8 us -> 18.9 us  [the longest x2 10.8 us: match(): pl.pallas_call(functools.partial(match_kernel, len(columns)), grid=(group...]
  transfers between devices with their start and end apart: 46 -> 49, of which waited for: 27 -> 26; matrix products, arithmetic and copies ran while one was open for 1% -> 1% of each run, Pallas kernels for 17% -> 15%
where the time goes in v4:
time: 149 us
  waiting for transfers between devices  54.2 us (36%)
  starting transfers between devices  52 us (35%)
  Pallas kernels  37.4 us (25%)
  other arithmetic  2.19 us (1%)
  local copies, waits for them, and re-layouts  2.01 us (1%)
    ppermute x49, waiting for transfers between devices, xor_permute(): return lax.ppermute(value, axis, [(i, i ^ mask) for i in range(size)])  54.2 us
    ppermute x49, starting transfers between devices, xor_permute(): return lax.ppermute(value, axis, [(i, i ^ mask) for i in range(size)])  52 us
    pallas_call x2, Pallas kernels, client_activations(): pl.pallas_call(functools.partial(client_kernel, start), grid=(units // wi...  11.8 us
    pallas_call x2, Pallas kernels, match(): pl.pallas_call(functools.partial(match_kernel, len(columns)), grid=(group...  10.8 us
    pallas_call x1, Pallas kernels, match_last(): pl.pallas_call(match_last_kernel, grid=(groups,), out_shape=(halves, halv...  5.45 us
    pallas_call x1, Pallas kernels, select_rows(): pl.pallas_call(select_kernel, out_shape=(half, half), in_specs=[scalars,...  4.81 us
  transfers between devices with their start and end apart: 49, of which 26 were waited for; matrix products, arithmetic and copies ran while one was open for 1% of the time, Pallas kernels for 15%

profile of v4, /device:TPU:0, one launch (start us, length us, event | category | flops | bytes accessed | tf_op | source)
XLA Modules:
  0.0 149.1 jit_solution(13299747394958922208)
XLA Ops:
  2.1 4.8 %select_rows.1 = (bf16[4,256,512]{2,1,0:T(8,128)(2,1)S(1)}, bf16[4,256,512]{2,1,0:T(8,128)(2,1)S(1)}) custom-call(s32[2]{0:T(128)S(1)} %pad_add_fusion.place, s32[256]{0:T(256)S(1)} %copy-done.5, f32[1,4096]{1,0:T(1,128)S(1)} %bitcast.90, bf16[2048,4096]{1,0:T(8,128)(2,1)} %table.1), custom_call_target="tpu_custom_call" | custom-call | flops 4000000 | bytes 4000000 | tf_op jit(solution)/shard_map/select_rows/pallas_call | solution.py:99
  7.0 2.6 %collective-permute-done = bf16[4,256,512]{2,1,0:T(8,128)(2,1)S(1)} collective-permute-done((bf16[4,256,512]{2,1,0:T(8,128)(2,1)S(1)}, bf16[4,256,512]{2,1,0:T(8,128)(2,1)S(1)}, u32[]{:S(2)}, u32[]{:S(2)}) %collective-permute-start) | collective-permute-done | bytes 1048608 | tf_op jit(solution)/shard_map/ppermute | solution.py:33
  10.1 3.2 %collective-permute-start.1 = (bf16[128,512]{1,0:T(8,128)(2,1)S(1)}, bf16[128,512]{1,0:T(8,128)(2,1)S(1)}, u32[]{:S(2)}, u32[]{:S(2)}) collective-permute-start(bf16[128,512]{1,0:T(8,128)(2,1)S(1)} %get-tuple-element.48), channel_id=1, source_target_pairs={{0,8},{4,12},{8,0},{12,4},{16,24},{20,28},{24,16},{28,20},{1,9},{5... | collective-permute-start | bytes 393224 | tf_op jit(solution)/shard_map/ppermute | solution.py:33
  18.8 2.3 %collective-permute-start.8 = (bf16[128,512]{1,0:T(8,128)(2,1)S(1)}, bf16[128,512]{1,0:T(8,128)(2,1)S(1)}, u32[]{:S(2)}, u32[]{:S(2)}) collective-permute-start(bf16[128,512]{1,0:T(8,128)(2,1)S(1)} %get-tuple-element.49), channel_id=1, source_target_pairs={{0,24},{4,28},{8,16},{12,20},{16,8},{20,12},{24,0},{28,4},{1,25},{... | collective-permute-start | bytes 393224 | tf_op jit(solution)/shard_map/ppermute | solution.py:33
  24.0 3.5 %collective-permute-done.7 = bf16[128,512]{1,0:T(8,128)(2,1)S(1)} collective-permute-done((bf16[128,512]{1,0:T(8,128)(2,1)S(1)}, bf16[128,512]{1,0:T(8,128)(2,1)S(1)}, u32[]{:S(2)}, u32[]{:S(2)}) %collective-permute-start.7) | collective-permute-done | bytes 131104 | tf_op jit(solution)/shard_map/ppermute | solution.py:33
  27.6 2.1 %collective-permute-start.4 = (bf16[128,512]{1,0:T(8,128)(2,1)S(1)}, bf16[128,512]{1,0:T(8,128)(2,1)S(1)}, u32[]{:S(2)}, u32[]{:S(2)}) collective-permute-start(bf16[128,512]{1,0:T(8,128)(2,1)S(1)} %get-tuple-element.44), channel_id=1, source_target_pairs={{0,1},{1,0},{2,3},{3,2},{4,5},{5,4},{6,7},{7,6},{8,9},{9,8},{10,11... | collective-permute-start | bytes 393224 | tf_op jit(solution)/shard_map/ppermute | solution.py:33
  29.9 3.9 %collective-permute-done.4 = bf16[128,512]{1,0:T(8,128)(2,1)S(1)} collective-permute-done((bf16[128,512]{1,0:T(8,128)(2,1)S(1)}, bf16[128,512]{1,0:T(8,128)(2,1)S(1)}, u32[]{:S(2)}, u32[]{:S(2)}) %collective-permute-start.4) | collective-permute-done | bytes 131104 | tf_op jit(solution)/shard_map/ppermute | solution.py:33
  33.8 5.7 %collective-permute-start.5 = (bf16[128,512]{1,0:T(8,128)(2,1)S(1)}, bf16[128,512]{1,0:T(8,128)(2,1)S(1)}, u32[]{:S(2)}, u32[]{:S(2)}) collective-permute-start(bf16[128,512]{1,0:T(8,128)(2,1)S(1)} %add.99), channel_id=1, source_target_pairs={{0,2},{1,3},{2,0},{3,1},{4,6},{5,7},{6,4},{7,5},{8,10},{9,11},{10,... | collective-permute-start | bytes 393224 | tf_op jit(solution)/shard_map/ppermute | solution.py:33
  39.6 2.8 %collective-permute-start.10 = (bf16[128,512]{1,0:T(8,128)(2,1)S(1)}, bf16[128,512]{1,0:T(8,128)(2,1)S(1)}, u32[]{:S(2)}, u32[]{:S(2)}) collective-permute-start(bf16[128,512]{1,0:T(8,128)(2,1)S(1)} %add.104), channel_id=1, source_target_pairs={{0,2},{1,3},{2,0},{3,1},{4,6},{5,7},{6,4},{7,5},{8,10},{9,11},{10,... | collective-permute-start | bytes 393224 | tf_op jit(solution)/shard_map/ppermute | solution.py:33
  42.3 5.1 %collective-permute-done.5 = bf16[128,512]{1,0:T(8,128)(2,1)S(1)} collective-permute-done((bf16[128,512]{1,0:T(8,128)(2,1)S(1)}, bf16[128,512]{1,0:T(8,128)(2,1)S(1)}, u32[]{:S(2)}, u32[]{:S(2)}) %collective-permute-start.5) | collective-permute-done | bytes 131104 | tf_op jit(solution)/shard_map/ppermute | solution.py:33
  50.9 2.5 %collective-permute-done.11 = bf16[4,2,224,256]{3,2,1,0:T(8,128)(2,1)S(1)} collective-permute-done((bf16[4,2,224,256]{3,2,1,0:T(8,128)(2,1)S(1)}, bf16[4,2,224,256]{3,2,1,0:T(8,128)(2,1)S(1)}, u32[]{:S(2)}, u32[]{:S(2)}) %collective-permute-start.11) | collective-permute-done | bytes 917536 | tf_op jit(solution)/shard_map/ppermute | solution.py:33
  57.5 4.8 %collective-permute-done.12 = bf16[2,224,256]{2,1,0:T(8,128)(2,1)S(1)} collective-permute-done((bf16[2,224,256]{2,1,0:T(8,128)(2,1)S(1)}, bf16[2,224,256]{2,1,0:T(8,128)(2,1)S(1)}, u32[]{:S(2)}, u32[]{:S(2)}) %collective-permute-start.12) | collective-permute-done | bytes 229408 | tf_op jit(solution)/shard_map/ppermute | solution.py:33
  62.9 5.7 %collective-permute-start.28 = (bf16[256,512]{1,0:T(8,128)(2,1)S(1)}, bf16[256,512]{1,0:T(8,128)(2,1)S(1)}, u32[]{:S(2)}, u32[]{:S(2)}) collective-permute-start(bf16[256,512]{1,0:T(8,128)(2,1)S(1)} %tied.1), channel_id=1, source_target_pairs={{0,24},{4,28},{8,16},{12,20},{16,8},{20,12},{24,0},{28,4},{1,25},{... | collective-permute-start | bytes 786440 | tf_op jit(solution)/shard_map/ppermute | solution.py:33
  69.3 3.6 %collective-permute-done.24.refs_2_ = bf16[256,512]{1,0:T(8,128)(2,1)S(1)} collective-permute-done((bf16[256,512]{1,0:T(8,128)(2,1)S(1)}, bf16[256,512]{1,0:T(8,128)(2,1)S(1)}, u32[]{:S(2)}, u32[]{:S(2)}) %collective-permute-start.24) | collective-permute-done | bytes 262176 | tf_op jit(solution)/shard_map/ppermute | solution.py:33
  73.4 4.3 %collective-permute-done.28.refs_6_ = bf16[256,512]{1,0:T(8,128)(2,1)S(1)} collective-permute-done((bf16[256,512]{1,0:T(8,128)(2,1)S(1)}, bf16[256,512]{1,0:T(8,128)(2,1)S(1)}, u32[]{:S(2)}, u32[]{:S(2)}) %collective-permute-start.28) | collective-permute-done | bytes 262176 | tf_op jit(solution)/shard_map/ppermute | solution.py:33
  82.1 5.2 %client_activations.3.rest_0_ = bf16[256,768]{1,0:T(8,128)(2,1)S(1)} custom-call(s32[2]{0:T(128)S(1)} %pad_add_fusion.place, bf16[256,512]{1,0:T(8,128)(2,1)S(1)} %pad_maximum_fusion.rows.value.refs_0_, bf16[256,512]{1,0:T(8,128)(2,1)S(1)} %collective-permute-done.23.refs_1_, bf16[256,512]{1,0:T(8,128)(2,1)S(1)} %collective-permute-done.24.refs_2_, ...), custom_call_target="tpu_custom_call" | custom-call | flops 3221225472 | bytes 12582912 | tf_op jit(solution)/shard_map/client_activations/pallas_call | solution.py:151
  87.4 6.6 %client_activations.2.rest_1_ = bf16[256,1024]{1,0:T(8,128)(2,1)S(1)} custom-call(s32[2]{0:T(128)S(1)} %pad_add_fusion.place, bf16[256,512]{1,0:T(8,128)(2,1)S(1)} %pad_maximum_fusion.rows.value.refs_0_, bf16[256,512]{1,0:T(8,128)(2,1)S(1)} %collective-permute-done.23.refs_1_, bf16[256,512]{1,0:T(8,128)(2,1)S(1)} %collective-permute-done.24.refs_2_, ...), custom_call_target="tpu_custom_call" | custom-call | flops 4294967296 | bytes 16777216 | tf_op jit(solution)/shard_map/client_activations/pallas_call | solution.py:151
  98.3 7.3 %match.2 = (f32[3584,256]{1,0:T(8,128)S(1)}, f32[1,3584]{1,0:T(1,128)S(1)}) custom-call(bf16[3584,256]{1,0:T(8,128)(2,1)S(1)} %bitcast.87, bf16[256,768]{1,0:T(8,128)(2,1)S(1)} %client_activations.3.rest_0_, bf16[256,1024]{1,0:T(8,128)(2,1)S(1)} %client_activations.2.rest_1_), custom_call_target="tpu_custom_call" | custom-call | flops 6576668672 | bytes 7340032 | tf_op jit(solution)/shard_map/match/pallas_call | solution.py:304
  105.6 3.5 %match.3 = (f32[3584,256]{1,0:T(8,128)S(1)}, f32[1,3584]{1,0:T(1,128)S(1)}) custom-call(bf16[3584,256]{1,0:T(8,128)(2,1)S(1)} %bitcast.88, bf16[256,768]{1,0:T(8,128)(2,1)S(1)} %collective-permute-done.31.rest_0_, f32[3584,256]{1,0:T(8,128)S(1)} %get-tuple-element.25.rest_1_, f32[1,3584]{1,0:T(1,128)S(1)} %get-tuple-element.26.rest_2_), custom_call_target="tpu_custom_call" | custom-call | flops 2818572288 | bytes 7340032 | tf_op jit(solution)/shard_map/match/pallas_call | solution.py:304
  109.3 5.4 %match_last.1 = (bf16[4,2,224,256]{3,2,1,0:T(8,128)(2,1)S(1)}, bf16[4,2,224,256]{3,2,1,0:T(8,128)(2,1)S(1)}, f32[2,3584]{1,0:T(2,128)S(1)}) custom-call(bf16[3584,256]{1,0:T(8,128)(2,1)S(1)} %bitcast.89, bf16[256,1024]{1,0:T(8,128)(2,1)S(1)} %collective-permute-done.30.columns, f32[3584,256]{1,0:T(8,128)S(1)} %get-tuple-element.27.before, ...), custom_call_target="tpu_custom_call" | custom-call | flops 3758096384 | bytes 7340032 | tf_op jit(solution)/shard_map/match_last/pallas_call | solution.py:327
  115.8 3.8 %collective-permute-done.33 = f32[2,2,1792]{2,1,0:T(2,128)S(1)} collective-permute-done((f32[2,2,1792]{2,1,0:T(2,128)S(1)}, f32[2,2,1792]{2,1,0:T(2,128)S(1)}, u32[]{:S(2)}, u32[]{:S(2)}) %collective-permute-start.33) | collective-permute-done | bytes 28704 | tf_op jit(solution)/shard_map/ppermute | solution.py:33
  133.0 2.5 %collective-permute-done.36 = bf16[224,256]{1,0:T(8,128)(2,1)S(1)} collective-permute-done((bf16[224,256]{1,0:T(8,128)(2,1)S(1)}, bf16[224,256]{1,0:T(8,128)(2,1)S(1)}, u32[]{:S(2)}, u32[]{:S(2)}) %collective-permute-start.36) | collective-permute-done | bytes 114720 | tf_op jit(solution)/shard_map/ppermute | solution.py:33
  135.5 2.4 %collective-permute-done.41 = bf16[224,256]{1,0:T(8,128)(2,1)S(1)} collective-permute-done((bf16[224,256]{1,0:T(8,128)(2,1)S(1)}, bf16[224,256]{1,0:T(8,128)(2,1)S(1)}, u32[]{:S(2)}, u32[]{:S(2)}) %collective-permute-start.41) | collective-permute-done | bytes 114720 | tf_op jit(solution)/shard_map/ppermute | solution.py:33
  143.4 2.3 %collective-permute-done.47.refs_6_ = bf16[224,256]{1,0:T(8,128)(2,1)S(1)} collective-permute-done((bf16[224,256]{1,0:T(8,128)(2,1)S(1)}, bf16[224,256]{1,0:T(8,128)(2,1)S(1)}, u32[]{:S(2)}, u32[]{:S(2)}) %collective-permute-start.47) | collective-permute-done | bytes 114720 | tf_op jit(solution)/shard_map/ppermute | solution.py:33
  (148 shorter events, 51.8 us)
Async XLA Ops:
  10.1 8.7 %collective-permute-start.1 = (bf16[128,512]{1,0:T(8,128)(2,1)S(1)}, bf16[128,512]{1,0:T(8,128)(2,1)S(1)}, u32[]{:S(2)}, u32[]{:S(2)}) collective-permute-start(bf16[128,512]{1,0:T(8,128)(2,1)S(1)} %get-tuple-element.48), channel_id=1, source_target_pairs={{0,8},{4,12},{8,0},{12,4},{16,24},{20,28},{24,16},{28,20},{1,9},{5... | collective-permute-start | bytes 393224 | tf_op jit(solution)/shard_map/ppermute | solution.py:33
  13.3 9.0 %collective-permute-start.2 = (bf16[128,512]{1,0:T(8,128)(2,1)S(1)}, bf16[128,512]{1,0:T(8,128)(2,1)S(1)}, u32[]{:S(2)}, u32[]{:S(2)}) collective-permute-start(bf16[128,512]{1,0:T(8,128)(2,1)S(1)} %get-tuple-element.53), channel_id=1, source_target_pairs={{0,16},{4,20},{8,24},{12,28},{16,0},{20,4},{24,8},{28,12},{1,17},{... | collective-permute-start | bytes 393224 | tf_op jit(solution)/shard_map/ppermute | solution.py:33
  15.3 8.7 %collective-permute-start.6 = (bf16[128,512]{1,0:T(8,128)(2,1)S(1)}, bf16[128,512]{1,0:T(8,128)(2,1)S(1)}, u32[]{:S(2)}, u32[]{:S(2)}) collective-permute-start(bf16[128,512]{1,0:T(8,128)(2,1)S(1)} %get-tuple-element.51), channel_id=1, source_target_pairs={{0,8},{4,12},{8,0},{12,4},{16,24},{20,28},{24,16},{28,20},{1,9},{5... | collective-permute-start | bytes 393224 | tf_op jit(solution)/shard_map/ppermute | solution.py:33
  16.8 10.7 %collective-permute-start.7 = (bf16[128,512]{1,0:T(8,128)(2,1)S(1)}, bf16[128,512]{1,0:T(8,128)(2,1)S(1)}, u32[]{:S(2)}, u32[]{:S(2)}) collective-permute-start(bf16[128,512]{1,0:T(8,128)(2,1)S(1)} %get-tuple-element.50), channel_id=1, source_target_pairs={{0,16},{4,20},{8,24},{12,28},{16,0},{20,4},{24,8},{28,12},{1,17},{... | collective-permute-start | bytes 393224 | tf_op jit(solution)/shard_map/ppermute | solution.py:33
  18.8 8.7 %collective-permute-start.8 = (bf16[128,512]{1,0:T(8,128)(2,1)S(1)}, bf16[128,512]{1,0:T(8,128)(2,1)S(1)}, u32[]{:S(2)}, u32[]{:S(2)}) collective-permute-start(bf16[128,512]{1,0:T(8,128)(2,1)S(1)} %get-tuple-element.49), channel_id=1, source_target_pairs={{0,24},{4,28},{8,16},{12,20},{16,8},{20,12},{24,0},{28,4},{1,25},{... | collective-permute-start | bytes 393224 | tf_op jit(solution)/shard_map/ppermute | solution.py:33
  29.8 9.7 %collective-permute-start.9 = (bf16[128,512]{1,0:T(8,128)(2,1)S(1)}, bf16[128,512]{1,0:T(8,128)(2,1)S(1)}, u32[]{:S(2)}, u32[]{:S(2)}) collective-permute-start(bf16[128,512]{1,0:T(8,128)(2,1)S(1)} %get-tuple-element.45), channel_id=1, source_target_pairs={{0,1},{1,0},{2,3},{3,2},{4,5},{5,4},{6,7},{7,6},{8,9},{9,8},{10,11... | collective-permute-start | bytes 393224 | tf_op jit(solution)/shard_map/ppermute | solution.py:33
  33.8 13.7 %collective-permute-start.5 = (bf16[128,512]{1,0:T(8,128)(2,1)S(1)}, bf16[128,512]{1,0:T(8,128)(2,1)S(1)}, u32[]{:S(2)}, u32[]{:S(2)}) collective-permute-start(bf16[128,512]{1,0:T(8,128)(2,1)S(1)} %add.99), channel_id=1, source_target_pairs={{0,2},{1,3},{2,0},{3,1},{4,6},{5,7},{6,4},{7,5},{8,10},{9,11},{10,... | collective-permute-start | bytes 393224 | tf_op jit(solution)/shard_map/ppermute | solution.py:33
  39.6 9.3 %collective-permute-start.10 = (bf16[128,512]{1,0:T(8,128)(2,1)S(1)}, bf16[128,512]{1,0:T(8,128)(2,1)S(1)}, u32[]{:S(2)}, u32[]{:S(2)}) collective-permute-start(bf16[128,512]{1,0:T(8,128)(2,1)S(1)} %add.104), channel_id=1, source_target_pairs={{0,2},{1,3},{2,0},{3,1},{4,6},{5,7},{6,4},{7,5},{8,10},{9,11},{10,... | collective-permute-start | bytes 393224 | tf_op jit(solution)/shard_map/ppermute | solution.py:33
  53.7 8.5 %collective-permute-start.12 = (bf16[2,224,256]{2,1,0:T(8,128)(2,1)S(1)}, bf16[2,224,256]{2,1,0:T(8,128)(2,1)S(1)}, u32[]{:S(2)}, u32[]{:S(2)}) collective-permute-start(bf16[2,224,256]{2,1,0:T(8,128)(2,1)S(1)} %get-tuple-element.54), channel_id=1, source_target_pairs={{0,8},{4,12},{8,0},{12,4},{16,24},{20,28},{24,16},{28,20},{1,9},{5... | collective-permute-start | bytes 688136 | tf_op jit(solution)/shard_map/ppermute | solution.py:33
  53.8 9.0 %collective-permute-start.13 = (bf16[2,224,256]{2,1,0:T(8,128)(2,1)S(1)}, bf16[2,224,256]{2,1,0:T(8,128)(2,1)S(1)}, u32[]{:S(2)}, u32[]{:S(2)}) collective-permute-start(bf16[2,224,256]{2,1,0:T(8,128)(2,1)S(1)} %get-tuple-element.56), channel_id=1, source_target_pairs={{0,16},{4,20},{8,24},{12,28},{16,0},{20,4},{24,8},{28,12},{1,17},{... | collective-permute-start | bytes 688136 | tf_op jit(solution)/shard_map/ppermute | solution.py:33
  55.7 12.9 %collective-permute-start.14 = (bf16[2,224,256]{2,1,0:T(8,128)(2,1)S(1)}, bf16[2,224,256]{2,1,0:T(8,128)(2,1)S(1)}, u32[]{:S(2)}, u32[]{:S(2)}) collective-permute-start(bf16[2,224,256]{2,1,0:T(8,128)(2,1)S(1)} %get-tuple-element.55), channel_id=1, source_target_pairs={{0,24},{4,28},{8,16},{12,20},{16,8},{20,12},{24,0},{28,4},{1,25},{... | collective-permute-start | bytes 688136 | tf_op jit(solution)/shard_map/ppermute | solution.py:33
  57.3 21.2 %collective-permute-start.23 = (bf16[256,512]{1,0:T(8,128)(2,1)S(1)}, bf16[256,512]{1,0:T(8,128)(2,1)S(1)}, u32[]{:S(2)}, u32[]{:S(2)}) collective-permute-start(bf16[256,512]{1,0:T(8,128)(2,1)S(1)} %pad_maximum_fusion.rows.value.refs_0_), channel_id=1, source_target_pairs={{0,4},{4,0},{8,12},{12,8},{16,20},{20,16},{24,28},{28,24},{1,5},{5... | collective-permute-start | bytes 786440 | tf_op jit(solution)/shard_map/ppermute | solution.py:33
  57.3 15.5 %collective-permute-start.24 = (bf16[256,512]{1,0:T(8,128)(2,1)S(1)}, bf16[256,512]{1,0:T(8,128)(2,1)S(1)}, u32[]{:S(2)}, u32[]{:S(2)}) collective-permute-start(bf16[256,512]{1,0:T(8,128)(2,1)S(1)} %tied.1), channel_id=1, source_target_pairs={{0,8},{4,12},{8,0},{12,4},{16,24},{20,28},{24,16},{28,20},{1,9},{5... | collective-permute-start | bytes 786440 | tf_op jit(solution)/shard_map/ppermute | solution.py:33
  62.3 10.6 %collective-permute-start.26 = (bf16[256,512]{1,0:T(8,128)(2,1)S(1)}, bf16[256,512]{1,0:T(8,128)(2,1)S(1)}, u32[]{:S(2)}, u32[]{:S(2)}) collective-permute-start(bf16[256,512]{1,0:T(8,128)(2,1)S(1)} %tied.1), channel_id=1, source_target_pairs={{0,16},{4,20},{8,24},{12,28},{16,0},{20,4},{24,8},{28,12},{1,17},{... | collective-permute-start | bytes 786440 | tf_op jit(solution)/shard_map/ppermute | solution.py:33
  62.9 14.8 %collective-permute-start.28 = (bf16[256,512]{1,0:T(8,128)(2,1)S(1)}, bf16[256,512]{1,0:T(8,128)(2,1)S(1)}, u32[]{:S(2)}, u32[]{:S(2)}) collective-permute-start(bf16[256,512]{1,0:T(8,128)(2,1)S(1)} %tied.1), channel_id=1, source_target_pairs={{0,24},{4,28},{8,16},{12,20},{16,8},{20,12},{24,0},{28,4},{1,25},{... | collective-permute-start | bytes 786440 | tf_op jit(solution)/shard_map/ppermute | solution.py:33
  69.2 8.6 %collective-permute-start.15 = (bf16[224,256]{1,0:T(8,128)(2,1)S(1)}, bf16[224,256]{1,0:T(8,128)(2,1)S(1)}, u32[]{:S(2)}, u32[]{:S(2)}) collective-permute-start(bf16[224,256]{1,0:T(8,128)(2,1)S(1)} %multiply_convert_fusion), channel_id=1, source_target_pairs={{0,2},{1,3},{2,0},{3,1},{4,6},{5,7},{6,4},{7,5},{8,10},{9,11},{10,... | collective-permute-start | bytes 344072 | tf_op jit(solution)/shard_map/ppermute | solution.py:33
  72.9 8.0 %collective-permute-start.27 = (bf16[256,512]{1,0:T(8,128)(2,1)S(1)}, bf16[256,512]{1,0:T(8,128)(2,1)S(1)}, u32[]{:S(2)}, u32[]{:S(2)}) collective-permute-start(bf16[256,512]{1,0:T(8,128)(2,1)S(1)} %collective-permute-done.26.refs_4_), channel_id=1, source_target_pairs={{0,4},{4,0},{8,12},{12,8},{16,20},{20,16},{24,28},{28,24},{1,5},{5... | collective-permute-start | bytes 786440 | tf_op jit(solution)/shard_map/ppermute | solution.py:33
  77.9 16.1 %collective-permute-start.16 = (bf16[2,224,256]{2,1,0:T(8,128)(2,1)S(1)}, bf16[2,224,256]{2,1,0:T(8,128)(2,1)S(1)}, u32[]{:S(2)}, u32[]{:S(2)}) collective-permute-start(bf16[2,224,256]{2,1,0:T(8,128)(2,1)S(1)} %pad_maximum_fusion.1), channel_id=1, source_target_pairs={{0,4},{4,0},{8,12},{12,8},{16,20},{20,16},{24,28},{28,24},{1,5},{5... | collective-permute-start | bytes 688136 | tf_op jit(solution)/shard_map/ppermute | solution.py:33
  78.5 17.5 %collective-permute-start.17 = (bf16[2,224,256]{2,1,0:T(8,128)(2,1)S(1)}, bf16[2,224,256]{2,1,0:T(8,128)(2,1)S(1)}, u32[]{:S(2)}, u32[]{:S(2)}) collective-permute-start(bf16[2,224,256]{2,1,0:T(8,128)(2,1)S(1)} %pad_maximum_fusion.1), channel_id=1, source_target_pairs={{0,8},{4,12},{8,0},{12,4},{16,24},{20,28},{24,16},{28,20},{1,9},{5... | collective-permute-start | bytes 688136 | tf_op jit(solution)/shard_map/ppermute | solution.py:33
  80.2 15.8 %collective-permute-start.19 = (bf16[2,224,256]{2,1,0:T(8,128)(2,1)S(1)}, bf16[2,224,256]{2,1,0:T(8,128)(2,1)S(1)}, u32[]{:S(2)}, u32[]{:S(2)}) collective-permute-start(bf16[2,224,256]{2,1,0:T(8,128)(2,1)S(1)} %pad_maximum_fusion.1), channel_id=1, source_target_pairs={{0,16},{4,20},{8,24},{12,28},{16,0},{20,4},{24,8},{28,12},{1,17},{... | collective-permute-start | bytes 688136 | tf_op jit(solution)/shard_map/ppermute | solution.py:33
  80.8 15.7 %collective-permute-start.21 = (bf16[2,224,256]{2,1,0:T(8,128)(2,1)S(1)}, bf16[2,224,256]{2,1,0:T(8,128)(2,1)S(1)}, u32[]{:S(2)}, u32[]{:S(2)}) collective-permute-start(bf16[2,224,256]{2,1,0:T(8,128)(2,1)S(1)} %pad_maximum_fusion.1), channel_id=1, source_target_pairs={{0,24},{4,28},{8,16},{12,20},{16,8},{20,12},{24,0},{28,4},{1,25},{... | collective-permute-start | bytes 688136 | tf_op jit(solution)/shard_map/ppermute | solution.py:33
  87.3 18.4 %collective-permute-start.31 = (bf16[256,768]{1,0:T(8,128)(2,1)S(1)}, bf16[256,768]{1,0:T(8,128)(2,1)S(1)}, u32[]{:S(2)}, u32[]{:S(2)}) collective-permute-start(bf16[256,768]{1,0:T(8,128)(2,1)S(1)} %client_activations.3.rest_0_), channel_id=1, source_target_pairs={{0,1},{1,0},{2,3},{3,2},{4,5},{5,4},{6,7},{7,6},{8,9},{9,8},{10,11... | collective-permute-start | bytes 1179656 | tf_op jit(solution)/shard_map/ppermute | solution.py:33
  93.9 15.3 %collective-permute-start.30 = (bf16[256,1024]{1,0:T(8,128)(2,1)S(1)}, bf16[256,1024]{1,0:T(8,128)(2,1)S(1)}, u32[]{:S(2)}, u32[]{:S(2)}) collective-permute-start(bf16[256,1024]{1,0:T(8,128)(2,1)S(1)} %client_activations.2.rest_1_), channel_id=1, source_target_pairs={{0,1},{1,0},{2,3},{3,2},{4,5},{5,4},{6,7},{7,6},{8,9},{9,8},{10,11... | collective-permute-start | bytes 1572872 | tf_op jit(solution)/shard_map/ppermute | solution.py:33
  127.2 8.3 %collective-permute-start.36 = (bf16[224,256]{1,0:T(8,128)(2,1)S(1)}, bf16[224,256]{1,0:T(8,128)(2,1)S(1)}, u32[]{:S(2)}, u32[]{:S(2)}) collective-permute-start(bf16[224,256]{1,0:T(8,128)(2,1)S(1)} %get-tuple-element.35), channel_id=1, source_target_pairs={{0,16},{4,20},{8,24},{12,28},{16,0},{20,4},{24,8},{28,12},{1,17},{... | collective-permute-start | bytes 344072 | tf_op jit(solution)/shard_map/ppermute | solution.py:33
  (35 other events, 547.9 us)

commit v5 on v4

--- a/solution.py
+++ b/solution.py
@@ -415,8 +415,12 @@
     half = total.shape[1] // 2
     halves = [total[:, :half], total[:, half:]]
     halves = [(part, sent(part)) for part in halves]
-    halves = [summed(*part).astype(bf16) for part in halves]
-    bit = 1
+    early, late = halves
+    early = summed(*early).astype(bf16)
+    met = over_units(early, mask=1)
+    late = summed([tied(late[0][0], met)], late[1]).astype(bf16)
+    halves = [early + met, late + over_units(late, mask=1)]
+    bit = 2
     while bit < parts:
         halves = [part + over_units(part, mask=bit) for part in halves]
         bit *= 2

time: 149 us -> 145 us (0.973)
  starting transfers between devices: 52 us -> 44.8 us
  waiting for transfers between devices: 54.2 us -> 57.6 us
    ppermute x49, starting transfers between devices: 52 us -> 44.8 us  [xor_permute(): return lax.ppermute(value, axis, [(i, i ^ mask) for i in range(size)])]
    ppermute x49, waiting for transfers between devices: 54.2 us -> 57.6 us  [xor_permute(): return lax.ppermute(value, axis, [(i, i ^ mask) for i in range(size)])]
  transfers between devices with their start and end apart: 49 -> 49, of which waited for: 26 -> 26; matrix products, arithmetic and copies ran while one was open for 1% -> 1% of each run, Pallas kernels for 15% -> 16%
where the time goes in v5:
time: 145 us
  waiting for transfers between devices  57.6 us (40%)
  starting transfers between devices  44.8 us (31%)
  Pallas kernels  37.4 us (26%)
  other arithmetic  2.18 us (2%)
  local copies, waits for them, and re-layouts  2.05 us (1%)
    ppermute x49, waiting for transfers between devices, xor_permute(): return lax.ppermute(value, axis, [(i, i ^ mask) for i in range(size)])  57.6 us
    ppermute x49, starting transfers between devices, xor_permute(): return lax.ppermute(value, axis, [(i, i ^ mask) for i in range(size)])  44.8 us
    pallas_call x2, Pallas kernels, client_activations(): pl.pallas_call(functools.partial(client_kernel, start), grid=(units // wi...  11.8 us
    pallas_call x2, Pallas kernels, match(): pl.pallas_call(functools.partial(match_kernel, len(columns)), grid=(group...  10.8 us
    pallas_call x1, Pallas kernels, match_last(): pl.pallas_call(match_last_kernel, grid=(groups,), out_shape=(halves, halv...  5.47 us
    pallas_call x1, Pallas kernels, select_rows(): pl.pallas_call(select_kernel, out_shape=(half, half), in_specs=[scalars,...  4.74 us
  transfers between devices with their start and end apart: 49, of which 26 were waited for; matrix products, arithmetic and copies ran while one was open for 1% of the time, Pallas kernels for 16%

profile of v5, /device:TPU:0, one launch (start us, length us, event | category | flops | bytes accessed | tf_op | source)
XLA Modules:
  0.0 145.4 jit_solution(12712048536433882849)
XLA Ops:
  2.1 4.7 %select_rows.1 = (bf16[4,256,512]{2,1,0:T(8,128)(2,1)S(1)}, bf16[4,256,512]{2,1,0:T(8,128)(2,1)S(1)}) custom-call(s32[2]{0:T(128)S(1)} %pad_add_fusion.place, s32[256]{0:T(256)S(1)} %copy-done.5, f32[1,4096]{1,0:T(1,128)S(1)} %bitcast.82, bf16[2048,4096]{1,0:T(8,128)(2,1)} %table.1), custom_call_target="tpu_custom_call" | custom-call | flops 4000000 | bytes 4000000 | tf_op jit(solution)/shard_map/select_rows/pallas_call | solution.py:99
  6.9 2.6 %collective-permute-done = bf16[4,256,512]{2,1,0:T(8,128)(2,1)S(1)} collective-permute-done((bf16[4,256,512]{2,1,0:T(8,128)(2,1)S(1)}, bf16[4,256,512]{2,1,0:T(8,128)(2,1)S(1)}, u32[]{:S(2)}, u32[]{:S(2)}) %collective-permute-start) | collective-permute-done | bytes 1048608 | tf_op jit(solution)/shard_map/ppermute | solution.py:33
  10.1 3.3 %collective-permute-start.1 = (bf16[128,512]{1,0:T(8,128)(2,1)S(1)}, bf16[128,512]{1,0:T(8,128)(2,1)S(1)}, u32[]{:S(2)}, u32[]{:S(2)}) collective-permute-start(bf16[128,512]{1,0:T(8,128)(2,1)S(1)} %get-tuple-element.51), channel_id=1, source_target_pairs={{0,8},{4,12},{8,0},{12,4},{16,24},{20,28},{24,16},{28,20},{1,9},{5... | collective-permute-start | bytes 393224 | tf_op jit(solution)/shard_map/ppermute | solution.py:33
  13.4 4.7 %collective-permute-start.2 = (bf16[128,512]{1,0:T(8,128)(2,1)S(1)}, bf16[128,512]{1,0:T(8,128)(2,1)S(1)}, u32[]{:S(2)}, u32[]{:S(2)}) collective-permute-start(bf16[128,512]{1,0:T(8,128)(2,1)S(1)} %get-tuple-element.50), channel_id=1, source_target_pairs={{0,16},{4,20},{8,24},{12,28},{16,0},{20,4},{24,8},{28,12},{1,17},{... | collective-permute-start | bytes 393224 | tf_op jit(solution)/shard_map/ppermute | solution.py:33
  21.7 2.3 %collective-permute-start.8 = (bf16[128,512]{1,0:T(8,128)(2,1)S(1)}, bf16[128,512]{1,0:T(8,128)(2,1)S(1)}, u32[]{:S(2)}, u32[]{:S(2)}) collective-permute-start(bf16[128,512]{1,0:T(8,128)(2,1)S(1)} %get-tuple-element.47), channel_id=1, source_target_pairs={{0,24},{4,28},{8,16},{12,20},{16,8},{20,12},{24,0},{28,4},{1,25},{... | collective-permute-start | bytes 393224 | tf_op jit(solution)/shard_map/ppermute | solution.py:33
  25.7 4.9 %collective-permute-done.4.rest_0_ = bf16[128,512]{1,0:T(8,128)(2,1)S(1)} collective-permute-done((bf16[128,512]{1,0:T(8,128)(2,1)S(1)}, bf16[128,512]{1,0:T(8,128)(2,1)S(1)}, u32[]{:S(2)}, u32[]{:S(2)}) %collective-permute-start.4) | collective-permute-done | bytes 131104 | tf_op jit(solution)/shard_map/ppermute | solution.py:33
  31.4 5.6 %collective-permute-done.9 = bf16[128,512]{1,0:T(8,128)(2,1)S(1)} collective-permute-done((bf16[128,512]{1,0:T(8,128)(2,1)S(1)}, bf16[128,512]{1,0:T(8,128)(2,1)S(1)}, u32[]{:S(2)}, u32[]{:S(2)}) %collective-permute-start.9) | collective-permute-done | bytes 131104 | tf_op jit(solution)/shard_map/ppermute | solution.py:33
  37.1 2.9 %collective-permute-done.5 = bf16[128,512]{1,0:T(8,128)(2,1)S(1)} collective-permute-done((bf16[128,512]{1,0:T(8,128)(2,1)S(1)}, bf16[128,512]{1,0:T(8,128)(2,1)S(1)}, u32[]{:S(2)}, u32[]{:S(2)}) %collective-permute-start.5) | collective-permute-done | bytes 131104 | tf_op jit(solution)/shard_map/ppermute | solution.py:33
  40.0 4.1 %collective-permute-done.10 = bf16[128,512]{1,0:T(8,128)(2,1)S(1)} collective-permute-done((bf16[128,512]{1,0:T(8,128)(2,1)S(1)}, bf16[128,512]{1,0:T(8,128)(2,1)S(1)}, u32[]{:S(2)}, u32[]{:S(2)}) %collective-permute-start.10) | collective-permute-done | bytes 131104 | tf_op jit(solution)/shard_map/ppermute | solution.py:33
  46.2 2.5 %collective-permute-done.11 = bf16[4,2,224,256]{3,2,1,0:T(8,128)(2,1)S(1)} collective-permute-done((bf16[4,2,224,256]{3,2,1,0:T(8,128)(2,1)S(1)}, bf16[4,2,224,256]{3,2,1,0:T(8,128)(2,1)S(1)}, u32[]{:S(2)}, u32[]{:S(2)}) %collective-permute-start.11) | collective-permute-done | bytes 917536 | tf_op jit(solution)/shard_map/ppermute | solution.py:33
  54.5 3.0 %collective-permute-done.12 = bf16[2,224,256]{2,1,0:T(8,128)(2,1)S(1)} collective-permute-done((bf16[2,224,256]{2,1,0:T(8,128)(2,1)S(1)}, bf16[2,224,256]{2,1,0:T(8,128)(2,1)S(1)}, u32[]{:S(2)}, u32[]{:S(2)}) %collective-permute-start.12) | collective-permute-done | bytes 229408 | tf_op jit(solution)/shard_map/ppermute | solution.py:33
  57.5 2.6 %collective-permute-start.26 = (bf16[256,512]{1,0:T(8,128)(2,1)S(1)}, bf16[256,512]{1,0:T(8,128)(2,1)S(1)}, u32[]{:S(2)}, u32[]{:S(2)}) collective-permute-start(bf16[256,512]{1,0:T(8,128)(2,1)S(1)} %tied.3), channel_id=1, source_target_pairs={{0,16},{4,20},{8,24},{12,28},{16,0},{20,4},{24,8},{28,12},{1,17},{... | collective-permute-start | bytes 786440 | tf_op jit(solution)/shard_map/ppermute | solution.py:33
  60.0 2.5 %collective-permute-done.13 = bf16[2,224,256]{2,1,0:T(8,128)(2,1)S(1)} collective-permute-done((bf16[2,224,256]{2,1,0:T(8,128)(2,1)S(1)}, bf16[2,224,256]{2,1,0:T(8,128)(2,1)S(1)}, u32[]{:S(2)}, u32[]{:S(2)}) %collective-permute-start.13) | collective-permute-done | bytes 229408 | tf_op jit(solution)/shard_map/ppermute | solution.py:33
  62.5 3.6 %collective-permute-start.28 = (bf16[256,512]{1,0:T(8,128)(2,1)S(1)}, bf16[256,512]{1,0:T(8,128)(2,1)S(1)}, u32[]{:S(2)}, u32[]{:S(2)}) collective-permute-start(bf16[256,512]{1,0:T(8,128)(2,1)S(1)} %tied.3), channel_id=1, source_target_pairs={{0,24},{4,28},{8,16},{12,20},{16,8},{20,12},{24,0},{28,4},{1,25},{... | collective-permute-start | bytes 786440 | tf_op jit(solution)/shard_map/ppermute | solution.py:33
  68.1 4.9 %collective-permute-done.26.refs_4_ = bf16[256,512]{1,0:T(8,128)(2,1)S(1)} collective-permute-done((bf16[256,512]{1,0:T(8,128)(2,1)S(1)}, bf16[256,512]{1,0:T(8,128)(2,1)S(1)}, u32[]{:S(2)}, u32[]{:S(2)}) %collective-permute-start.26) | collective-permute-done | bytes 262176 | tf_op jit(solution)/shard_map/ppermute | solution.py:33
  79.3 5.2 %client_activations.3.rest_0_ = bf16[256,768]{1,0:T(8,128)(2,1)S(1)} custom-call(s32[2]{0:T(128)S(1)} %pad_add_fusion.place, bf16[256,512]{1,0:T(8,128)(2,1)S(1)} %pad_maximum_fusion.rows.value.refs_0_, bf16[256,512]{1,0:T(8,128)(2,1)S(1)} %collective-permute-done.23.refs_1_, bf16[256,512]{1,0:T(8,128)(2,1)S(1)} %collective-permute-done.24.refs_2_, ...), custom_call_target="tpu_custom_call" | custom-call | flops 3221225472 | bytes 12582912 | tf_op jit(solution)/shard_map/client_activations/pallas_call | solution.py:151
  84.6 6.6 %client_activations.2.rest_1_ = bf16[256,1024]{1,0:T(8,128)(2,1)S(1)} custom-call(s32[2]{0:T(128)S(1)} %pad_add_fusion.place, bf16[256,512]{1,0:T(8,128)(2,1)S(1)} %pad_maximum_fusion.rows.value.refs_0_, bf16[256,512]{1,0:T(8,128)(2,1)S(1)} %collective-permute-done.23.refs_1_, bf16[256,512]{1,0:T(8,128)(2,1)S(1)} %collective-permute-done.24.refs_2_, ...), custom_call_target="tpu_custom_call" | custom-call | flops 4294967296 | bytes 16777216 | tf_op jit(solution)/shard_map/client_activations/pallas_call | solution.py:151
  91.1 2.1 %collective-permute-start.30 = (bf16[256,1024]{1,0:T(8,128)(2,1)S(1)}, bf16[256,1024]{1,0:T(8,128)(2,1)S(1)}, u32[]{:S(2)}, u32[]{:S(2)}) collective-permute-start(bf16[256,1024]{1,0:T(8,128)(2,1)S(1)} %client_activations.2.rest_1_), channel_id=1, source_target_pairs={{0,1},{1,0},{2,3},{3,2},{4,5},{5,4},{6,7},{7,6},{8,9},{9,8},{10,11... | collective-permute-start | bytes 1572872 | tf_op jit(solution)/shard_map/ppermute | solution.py:33
  95.5 7.3 %match.2 = (f32[3584,256]{1,0:T(8,128)S(1)}, f32[1,3584]{1,0:T(1,128)S(1)}) custom-call(bf16[3584,256]{1,0:T(8,128)(2,1)S(1)} %bitcast.79, bf16[256,768]{1,0:T(8,128)(2,1)S(1)} %client_activations.3.rest_0_, bf16[256,1024]{1,0:T(8,128)(2,1)S(1)} %client_activations.2.rest_1_), custom_call_target="tpu_custom_call" | custom-call | flops 6576668672 | bytes 7340032 | tf_op jit(solution)/shard_map/match/pallas_call | solution.py:304
  102.8 3.5 %match.3 = (f32[3584,256]{1,0:T(8,128)S(1)}, f32[1,3584]{1,0:T(1,128)S(1)}) custom-call(bf16[3584,256]{1,0:T(8,128)(2,1)S(1)} %bitcast.80, bf16[256,768]{1,0:T(8,128)(2,1)S(1)} %collective-permute-done.31.rest_0_, f32[3584,256]{1,0:T(8,128)S(1)} %get-tuple-element.25.rest_1_, f32[1,3584]{1,0:T(1,128)S(1)} %get-tuple-element.26.rest_2_), custom_call_target="tpu_custom_call" | custom-call | flops 2818572288 | bytes 7340032 | tf_op jit(solution)/shard_map/match/pallas_call | solution.py:304
  106.3 5.5 %match_last.1 = (bf16[4,2,224,256]{3,2,1,0:T(8,128)(2,1)S(1)}, bf16[4,2,224,256]{3,2,1,0:T(8,128)(2,1)S(1)}, f32[2,3584]{1,0:T(2,128)S(1)}) custom-call(bf16[3584,256]{1,0:T(8,128)(2,1)S(1)} %bitcast.81, bf16[256,1024]{1,0:T(8,128)(2,1)S(1)} %collective-permute-done.30.columns, f32[3584,256]{1,0:T(8,128)S(1)} %get-tuple-element.27.before, ...), custom_call_target="tpu_custom_call" | custom-call | flops 3758096384 | bytes 7340032 | tf_op jit(solution)/shard_map/match_last/pallas_call | solution.py:327
  112.2 4.5 %collective-permute-done.33 = f32[2,2,1792]{2,1,0:T(2,128)S(1)} collective-permute-done((f32[2,2,1792]{2,1,0:T(2,128)S(1)}, f32[2,2,1792]{2,1,0:T(2,128)S(1)}, u32[]{:S(2)}, u32[]{:S(2)}) %collective-permute-start.33) | collective-permute-done | bytes 28704 | tf_op jit(solution)/shard_map/ppermute | solution.py:33
  129.5 2.1 %collective-permute-done.36 = bf16[224,256]{1,0:T(8,128)(2,1)S(1)} collective-permute-done((bf16[224,256]{1,0:T(8,128)(2,1)S(1)}, bf16[224,256]{1,0:T(8,128)(2,1)S(1)}, u32[]{:S(2)}, u32[]{:S(2)}) %collective-permute-start.36) | collective-permute-done | bytes 114720 | tf_op jit(solution)/shard_map/ppermute | solution.py:33
  131.6 3.1 %collective-permute-done.41 = bf16[224,256]{1,0:T(8,128)(2,1)S(1)} collective-permute-done((bf16[224,256]{1,0:T(8,128)(2,1)S(1)}, bf16[224,256]{1,0:T(8,128)(2,1)S(1)}, u32[]{:S(2)}, u32[]{:S(2)}) %collective-permute-start.41) | collective-permute-done | bytes 114720 | tf_op jit(solution)/shard_map/ppermute | solution.py:33
  (151 shorter events, 49.9 us)
Async XLA Ops:
  10.1 11.6 %collective-permute-start.1 = (bf16[128,512]{1,0:T(8,128)(2,1)S(1)}, bf16[128,512]{1,0:T(8,128)(2,1)S(1)}, u32[]{:S(2)}, u32[]{:S(2)}) collective-permute-start(bf16[128,512]{1,0:T(8,128)(2,1)S(1)} %get-tuple-element.51), channel_id=1, source_target_pairs={{0,8},{4,12},{8,0},{12,4},{16,24},{20,28},{24,16},{28,20},{1,9},{5... | collective-permute-start | bytes 393224 | tf_op jit(solution)/shard_map/ppermute | solution.py:33
  13.4 12.0 %collective-permute-start.2 = (bf16[128,512]{1,0:T(8,128)(2,1)S(1)}, bf16[128,512]{1,0:T(8,128)(2,1)S(1)}, u32[]{:S(2)}, u32[]{:S(2)}) collective-permute-start(bf16[128,512]{1,0:T(8,128)(2,1)S(1)} %get-tuple-element.50), channel_id=1, source_target_pairs={{0,16},{4,20},{8,24},{12,28},{16,0},{20,4},{24,8},{28,12},{1,17},{... | collective-permute-start | bytes 393224 | tf_op jit(solution)/shard_map/ppermute | solution.py:33
  18.2 7.3 %collective-permute-start.3 = (bf16[128,512]{1,0:T(8,128)(2,1)S(1)}, bf16[128,512]{1,0:T(8,128)(2,1)S(1)}, u32[]{:S(2)}, u32[]{:S(2)}) collective-permute-start(bf16[128,512]{1,0:T(8,128)(2,1)S(1)} %get-tuple-element.49), channel_id=1, source_target_pairs={{0,24},{4,28},{8,16},{12,20},{16,8},{20,12},{24,0},{28,4},{1,25},{... | collective-permute-start | bytes 393224 | tf_op jit(solution)/shard_map/ppermute | solution.py:33
  18.2 12.4 %collective-permute-start.6 = (bf16[128,512]{1,0:T(8,128)(2,1)S(1)}, bf16[128,512]{1,0:T(8,128)(2,1)S(1)}, u32[]{:S(2)}, u32[]{:S(2)}) collective-permute-start(bf16[128,512]{1,0:T(8,128)(2,1)S(1)} %get-tuple-element.46), channel_id=1, source_target_pairs={{0,8},{4,12},{8,0},{12,4},{16,24},{20,28},{24,16},{28,20},{1,9},{5... | collective-permute-start | bytes 393224 | tf_op jit(solution)/shard_map/ppermute | solution.py:33
  19.6 11.0 %collective-permute-start.7 = (bf16[128,512]{1,0:T(8,128)(2,1)S(1)}, bf16[128,512]{1,0:T(8,128)(2,1)S(1)}, u32[]{:S(2)}, u32[]{:S(2)}) collective-permute-start(bf16[128,512]{1,0:T(8,128)(2,1)S(1)} %get-tuple-element.48), channel_id=1, source_target_pairs={{0,16},{4,20},{8,24},{12,28},{16,0},{20,4},{24,8},{28,12},{1,17},{... | collective-permute-start | bytes 393224 | tf_op jit(solution)/shard_map/ppermute | solution.py:33
  21.7 9.0 %collective-permute-start.8 = (bf16[128,512]{1,0:T(8,128)(2,1)S(1)}, bf16[128,512]{1,0:T(8,128)(2,1)S(1)}, u32[]{:S(2)}, u32[]{:S(2)}) collective-permute-start(bf16[128,512]{1,0:T(8,128)(2,1)S(1)} %get-tuple-element.47), channel_id=1, source_target_pairs={{0,24},{4,28},{8,16},{12,20},{16,8},{20,12},{24,0},{28,4},{1,25},{... | collective-permute-start | bytes 393224 | tf_op jit(solution)/shard_map/ppermute | solution.py:33
  30.8 9.2 %collective-permute-start.5 = (bf16[128,512]{1,0:T(8,128)(2,1)S(1)}, bf16[128,512]{1,0:T(8,128)(2,1)S(1)}, u32[]{:S(2)}, u32[]{:S(2)}) collective-permute-start(bf16[128,512]{1,0:T(8,128)(2,1)S(1)} %add.99), channel_id=1, source_target_pairs={{0,2},{1,3},{2,0},{3,1},{4,6},{5,7},{6,4},{7,5},{8,10},{9,11},{10,... | collective-permute-start | bytes 393224 | tf_op jit(solution)/shard_map/ppermute | solution.py:33
  49.0 8.5 %collective-permute-start.12 = (bf16[2,224,256]{2,1,0:T(8,128)(2,1)S(1)}, bf16[2,224,256]{2,1,0:T(8,128)(2,1)S(1)}, u32[]{:S(2)}, u32[]{:S(2)}) collective-permute-start(bf16[2,224,256]{2,1,0:T(8,128)(2,1)S(1)} %get-tuple-element.52), channel_id=1, source_target_pairs={{0,8},{4,12},{8,0},{12,4},{16,24},{20,28},{24,16},{28,20},{1,9},{5... | collective-permute-start | bytes 688136 | tf_op jit(solution)/shard_map/ppermute | solution.py:33
  50.9 11.6 %collective-permute-start.13 = (bf16[2,224,256]{2,1,0:T(8,128)(2,1)S(1)}, bf16[2,224,256]{2,1,0:T(8,128)(2,1)S(1)}, u32[]{:S(2)}, u32[]{:S(2)}) collective-permute-start(bf16[2,224,256]{2,1,0:T(8,128)(2,1)S(1)} %get-tuple-element.54), channel_id=1, source_target_pairs={{0,16},{4,20},{8,24},{12,28},{16,0},{20,4},{24,8},{28,12},{1,17},{... | collective-permute-start | bytes 688136 | tf_op jit(solution)/shard_map/ppermute | solution.py:33
  51.7 14.5 %collective-permute-start.14 = (bf16[2,224,256]{2,1,0:T(8,128)(2,1)S(1)}, bf16[2,224,256]{2,1,0:T(8,128)(2,1)S(1)}, u32[]{:S(2)}, u32[]{:S(2)}) collective-permute-start(bf16[2,224,256]{2,1,0:T(8,128)(2,1)S(1)} %get-tuple-element.53), channel_id=1, source_target_pairs={{0,24},{4,28},{8,16},{12,20},{16,8},{20,12},{24,0},{28,4},{1,25},{... | collective-permute-start | bytes 688136 | tf_op jit(solution)/shard_map/ppermute | solution.py:33
  53.1 22.6 %collective-permute-start.23 = (bf16[256,512]{1,0:T(8,128)(2,1)S(1)}, bf16[256,512]{1,0:T(8,128)(2,1)S(1)}, u32[]{:S(2)}, u32[]{:S(2)}) collective-permute-start(bf16[256,512]{1,0:T(8,128)(2,1)S(1)} %pad_maximum_fusion.rows.value.refs_0_), channel_id=1, source_target_pairs={{0,4},{4,0},{8,12},{12,8},{16,20},{20,16},{24,28},{28,24},{1,5},{5... | collective-permute-start | bytes 786440 | tf_op jit(solution)/shard_map/ppermute | solution.py:33
  53.1 15.0 %collective-permute-start.24 = (bf16[256,512]{1,0:T(8,128)(2,1)S(1)}, bf16[256,512]{1,0:T(8,128)(2,1)S(1)}, u32[]{:S(2)}, u32[]{:S(2)}) collective-permute-start(bf16[256,512]{1,0:T(8,128)(2,1)S(1)} %tied.3), channel_id=1, source_target_pairs={{0,8},{4,12},{8,0},{12,4},{16,24},{20,28},{24,16},{28,20},{1,9},{5... | collective-permute-start | bytes 786440 | tf_op jit(solution)/shard_map/ppermute | solution.py:33
  57.5 15.5 %collective-permute-start.26 = (bf16[256,512]{1,0:T(8,128)(2,1)S(1)}, bf16[256,512]{1,0:T(8,128)(2,1)S(1)}, u32[]{:S(2)}, u32[]{:S(2)}) collective-permute-start(bf16[256,512]{1,0:T(8,128)(2,1)S(1)} %tied.3), channel_id=1, source_target_pairs={{0,16},{4,20},{8,24},{12,28},{16,0},{20,4},{24,8},{28,12},{1,17},{... | collective-permute-start | bytes 786440 | tf_op jit(solution)/shard_map/ppermute | solution.py:33
  62.5 12.3 %collective-permute-start.28 = (bf16[256,512]{1,0:T(8,128)(2,1)S(1)}, bf16[256,512]{1,0:T(8,128)(2,1)S(1)}, u32[]{:S(2)}, u32[]{:S(2)}) collective-permute-start(bf16[256,512]{1,0:T(8,128)(2,1)S(1)} %tied.3), channel_id=1, source_target_pairs={{0,24},{4,28},{8,16},{12,20},{16,8},{20,12},{24,0},{28,4},{1,25},{... | collective-permute-start | bytes 786440 | tf_op jit(solution)/shard_map/ppermute | solution.py:33
  66.8 8.3 %collective-permute-start.15 = (bf16[224,256]{1,0:T(8,128)(2,1)S(1)}, bf16[224,256]{1,0:T(8,128)(2,1)S(1)}, u32[]{:S(2)}, u32[]{:S(2)}) collective-permute-start(bf16[224,256]{1,0:T(8,128)(2,1)S(1)} %multiply_convert_fusion), channel_id=1, source_target_pairs={{0,2},{1,3},{2,0},{3,1},{4,6},{5,7},{6,4},{7,5},{8,10},{9,11},{10,... | collective-permute-start | bytes 344072 | tf_op jit(solution)/shard_map/ppermute | solution.py:33
  68.1 8.2 %collective-permute-start.25 = (bf16[256,512]{1,0:T(8,128)(2,1)S(1)}, bf16[256,512]{1,0:T(8,128)(2,1)S(1)}, u32[]{:S(2)}, u32[]{:S(2)}) collective-permute-start(bf16[256,512]{1,0:T(8,128)(2,1)S(1)} %collective-permute-done.24.refs_2_), channel_id=1, source_target_pairs={{0,4},{4,0},{8,12},{12,8},{16,20},{20,16},{24,28},{28,24},{1,5},{5... | collective-permute-start | bytes 786440 | tf_op jit(solution)/shard_map/ppermute | solution.py:33
  75.0 16.1 %collective-permute-start.16 = (bf16[2,224,256]{2,1,0:T(8,128)(2,1)S(1)}, bf16[2,224,256]{2,1,0:T(8,128)(2,1)S(1)}, u32[]{:S(2)}, u32[]{:S(2)}) collective-permute-start(bf16[2,224,256]{2,1,0:T(8,128)(2,1)S(1)} %pad_maximum_fusion.1), channel_id=1, source_target_pairs={{0,4},{4,0},{8,12},{12,8},{16,20},{20,16},{24,28},{28,24},{1,5},{5... | collective-permute-start | bytes 688136 | tf_op jit(solution)/shard_map/ppermute | solution.py:33
  75.6 17.5 %collective-permute-start.17 = (bf16[2,224,256]{2,1,0:T(8,128)(2,1)S(1)}, bf16[2,224,256]{2,1,0:T(8,128)(2,1)S(1)}, u32[]{:S(2)}, u32[]{:S(2)}) collective-permute-start(bf16[2,224,256]{2,1,0:T(8,128)(2,1)S(1)} %pad_maximum_fusion.1), channel_id=1, source_target_pairs={{0,8},{4,12},{8,0},{12,4},{16,24},{20,28},{24,16},{28,20},{1,9},{5... | collective-permute-start | bytes 688136 | tf_op jit(solution)/shard_map/ppermute | solution.py:33
  76.3 16.9 %collective-permute-start.19 = (bf16[2,224,256]{2,1,0:T(8,128)(2,1)S(1)}, bf16[2,224,256]{2,1,0:T(8,128)(2,1)S(1)}, u32[]{:S(2)}, u32[]{:S(2)}) collective-permute-start(bf16[2,224,256]{2,1,0:T(8,128)(2,1)S(1)} %pad_maximum_fusion.1), channel_id=1, source_target_pairs={{0,16},{4,20},{8,24},{12,28},{16,0},{20,4},{24,8},{28,12},{1,17},{... | collective-permute-start | bytes 688136 | tf_op jit(solution)/shard_map/ppermute | solution.py:33
  78.0 15.7 %collective-permute-start.21 = (bf16[2,224,256]{2,1,0:T(8,128)(2,1)S(1)}, bf16[2,224,256]{2,1,0:T(8,128)(2,1)S(1)}, u32[]{:S(2)}, u32[]{:S(2)}) collective-permute-start(bf16[2,224,256]{2,1,0:T(8,128)(2,1)S(1)} %pad_maximum_fusion.1), channel_id=1, source_target_pairs={{0,24},{4,28},{8,16},{12,20},{16,8},{20,12},{24,0},{28,4},{1,25},{... | collective-permute-start | bytes 688136 | tf_op jit(solution)/shard_map/ppermute | solution.py:33
  84.5 18.4 %collective-permute-start.31 = (bf16[256,768]{1,0:T(8,128)(2,1)S(1)}, bf16[256,768]{1,0:T(8,128)(2,1)S(1)}, u32[]{:S(2)}, u32[]{:S(2)}) collective-permute-start(bf16[256,768]{1,0:T(8,128)(2,1)S(1)} %client_activations.3.rest_0_), channel_id=1, source_target_pairs={{0,1},{1,0},{2,3},{3,2},{4,5},{5,4},{6,7},{7,6},{8,9},{9,8},{10,11... | collective-permute-start | bytes 1179656 | tf_op jit(solution)/shard_map/ppermute | solution.py:33
  91.1 15.2 %collective-permute-start.30 = (bf16[256,1024]{1,0:T(8,128)(2,1)S(1)}, bf16[256,1024]{1,0:T(8,128)(2,1)S(1)}, u32[]{:S(2)}, u32[]{:S(2)}) collective-permute-start(bf16[256,1024]{1,0:T(8,128)(2,1)S(1)} %client_activations.2.rest_1_), channel_id=1, source_target_pairs={{0,1},{1,0},{2,3},{3,2},{4,5},{5,4},{6,7},{7,6},{8,9},{9,8},{10,11... | collective-permute-start | bytes 1572872 | tf_op jit(solution)/shard_map/ppermute | solution.py:33
  119.3 7.1 %collective-permute-start.39 = (bf16[224,256]{1,0:T(8,128)(2,1)S(1)}, bf16[224,256]{1,0:T(8,128)(2,1)S(1)}, u32[]{:S(2)}, u32[]{:S(2)}) collective-permute-start(bf16[224,256]{1,0:T(8,128)(2,1)S(1)} %get-tuple-element.38), channel_id=1, source_target_pairs={{0,16},{4,20},{8,24},{12,28},{16,0},{20,4},{24,8},{28,12},{1,17},{... | collective-permute-start | bytes 344072 | tf_op jit(solution)/shard_map/ppermute | solution.py:33
  123.3 8.3 %collective-permute-start.36 = (bf16[224,256]{1,0:T(8,128)(2,1)S(1)}, bf16[224,256]{1,0:T(8,128)(2,1)S(1)}, u32[]{:S(2)}, u32[]{:S(2)}) collective-permute-start(bf16[224,256]{1,0:T(8,128)(2,1)S(1)} %get-tuple-element.35), channel_id=1, source_target_pairs={{0,16},{4,20},{8,24},{12,28},{16,0},{20,4},{24,8},{28,12},{1,17},{... | collective-permute-start | bytes 344072 | tf_op jit(solution)/shard_map/ppermute | solution.py:33
  (35 other events, 478.8 us)

commit v6 on v5

--- a/solution.py
+++ b/solution.py
@@ -76,8 +76,7 @@
         row_in_group = lax.rem(ids[t] - start, group_rows)
         block = slots[lax.rem(k, fetch_slots)].astype(f32)
         row = jnp.sum(jnp.where(sublane == row_in_group, block, 0.0), axis=0, keepdims=True)
-        scale = lax.rsqrt(jnp.sum(row * row, axis=1, keepdims=True) * (1.0 / width) + 1e-05)
-        rows[pl.ds(t, 1), :] = row * scale * gain[...]
+        rows[pl.ds(t, 1), :] = row
 
         @pl.when(k + fetch_slots < count)
         def _():
@@ -86,11 +85,17 @@
         return carry
 
     lax.fori_loop(0, count, place_row, 0)
+    lanes = 128
+    squares = jnp.zeros((tokens, lanes), f32)
+    for k in range(0, width, lanes):
+        some = rows[:, k : k + lanes]
+        squares += some * some
+    scale = lax.rsqrt(jnp.sum(squares, axis=1, keepdims=True) * (1.0 / width) + 1e-05)
     span = keep.shape[2]
     for p in range(2 * keep.shape[0]):
-        source = pl.multiple_of((client ^ p) * span, span)
+        source = pl.ds(pl.multiple_of((client ^ p) * span, span), span)
         target = send if p % 2 else keep
-        target[p // 2] = rows[:, pl.ds(source, span)].astype(bf16)
+        target[p // 2] = (rows[:, source] * scale * gain[:, source]).astype(bf16)
 
 
 def select_rows(token_ids, place, norm_gain, embed_table, clients):

time: 145 us -> 145 us (level)
  transfers between devices with their start and end apart: 49 -> 49, of which waited for: 26 -> 27; matrix products, arithmetic and copies ran while one was open for 1% -> 1% of each run, Pallas kernels for 16% -> 16%
where the time goes in v6:
time: 145 us; the launch traced here: 144 us
  waiting for transfers between devices  58.4 us (40%)
  starting transfers between devices  43.5 us (30%)
  Pallas kernels  37 us (26%)
  other arithmetic  2.18 us (2%)
  local copies, waits for them, and re-layouts  2.05 us (1%)
    ppermute x49, waiting for transfers between devices, xor_permute(): return lax.ppermute(value, axis, [(i, i ^ mask) for i in range(size)])  58.4 us
    ppermute x49, starting transfers between devices, xor_permute(): return lax.ppermute(value, axis, [(i, i ^ mask) for i in range(size)])  43.5 us
    pallas_call x2, Pallas kernels, client_activations(): pl.pallas_call(functools.partial(client_kernel, start), grid=(units // wi...  11.8 us
    pallas_call x2, Pallas kernels, match(): pl.pallas_call(functools.partial(match_kernel, len(columns)), grid=(group...  10.8 us
    pallas_call x1, Pallas kernels, match_last(): pl.pallas_call(match_last_kernel, grid=(groups,), out_shape=(halves, halv...  5.45 us
    pallas_call x1, Pallas kernels, select_rows(): pl.pallas_call(select_kernel, out_shape=(half, half), in_specs=[scalars,...  4.32 us
  transfers between devices with their start and end apart: 49, of which 27 were waited for; matrix products, arithmetic and copies ran while one was open for 1% of the time, Pallas kernels for 16%

profile of v6, /device:TPU:0, one launch (start us, length us, event | category | flops | bytes accessed | tf_op | source)
XLA Modules:
  0.0 144.4 jit_solution(11185930023799165513)
XLA Ops:
  2.1 4.3 %select_rows.1 = (bf16[4,256,512]{2,1,0:T(8,128)(2,1)S(1)}, bf16[4,256,512]{2,1,0:T(8,128)(2,1)S(1)}) custom-call(s32[2]{0:T(128)S(1)} %pad_add_fusion.place, s32[256]{0:T(256)S(1)} %copy-done.5, f32[1,4096]{1,0:T(1,128)S(1)} %bitcast.82, bf16[2048,4096]{1,0:T(8,128)(2,1)} %table.1), custom_call_target="tpu_custom_call" | custom-call | flops 4000000 | bytes 4000000 | tf_op jit(solution)/shard_map/select_rows/pallas_call | solution.py:104
  7.4 2.3 %collective-permute-done = bf16[4,256,512]{2,1,0:T(8,128)(2,1)S(1)} collective-permute-done((bf16[4,256,512]{2,1,0:T(8,128)(2,1)S(1)}, bf16[4,256,512]{2,1,0:T(8,128)(2,1)S(1)}, u32[]{:S(2)}, u32[]{:S(2)}) %collective-permute-start) | collective-permute-done | bytes 1048608 | tf_op jit(solution)/shard_map/ppermute | solution.py:33
  10.2 2.4 %collective-permute-start.1 = (bf16[128,512]{1,0:T(8,128)(2,1)S(1)}, bf16[128,512]{1,0:T(8,128)(2,1)S(1)}, u32[]{:S(2)}, u32[]{:S(2)}) collective-permute-start(bf16[128,512]{1,0:T(8,128)(2,1)S(1)} %get-tuple-element.51), channel_id=1, source_target_pairs={{0,8},{4,12},{8,0},{12,4},{16,24},{20,28},{24,16},{28,20},{1,9},{5... | collective-permute-start | bytes 393224 | tf_op jit(solution)/shard_map/ppermute | solution.py:33
  17.5 2.2 %collective-permute-start.8 = (bf16[128,512]{1,0:T(8,128)(2,1)S(1)}, bf16[128,512]{1,0:T(8,128)(2,1)S(1)}, u32[]{:S(2)}, u32[]{:S(2)}) collective-permute-start(bf16[128,512]{1,0:T(8,128)(2,1)S(1)} %get-tuple-element.47), channel_id=1, source_target_pairs={{0,24},{4,28},{8,16},{12,20},{16,8},{20,12},{24,0},{28,4},{1,25},{... | collective-permute-start | bytes 393224 | tf_op jit(solution)/shard_map/ppermute | solution.py:33
  22.1 3.0 %collective-permute-start.4 = (bf16[128,512]{1,0:T(8,128)(2,1)S(1)}, bf16[128,512]{1,0:T(8,128)(2,1)S(1)}, u32[]{:S(2)}, u32[]{:S(2)}) collective-permute-start(bf16[128,512]{1,0:T(8,128)(2,1)S(1)} %fusion.6), channel_id=1, source_target_pairs={{0,1},{1,0},{2,3},{3,2},{4,5},{5,4},{6,7},{7,6},{8,9},{9,8},{10,11... | collective-permute-start | bytes 393224 | tf_op jit(solution)/shard_map/ppermute | solution.py:33
  25.1 2.9 %collective-permute-done.4.rest_0_ = bf16[128,512]{1,0:T(8,128)(2,1)S(1)} collective-permute-done((bf16[128,512]{1,0:T(8,128)(2,1)S(1)}, bf16[128,512]{1,0:T(8,128)(2,1)S(1)}, u32[]{:S(2)}, u32[]{:S(2)}) %collective-permute-start.4) | collective-permute-done | bytes 131104 | tf_op jit(solution)/shard_map/ppermute | solution.py:33
  28.2 2.1 %collective-permute-start.9 = (bf16[128,512]{1,0:T(8,128)(2,1)S(1)}, bf16[128,512]{1,0:T(8,128)(2,1)S(1)}, u32[]{:S(2)}, u32[]{:S(2)}) collective-permute-start(bf16[128,512]{1,0:T(8,128)(2,1)S(1)} %add_convert_fusion), channel_id=1, source_target_pairs={{0,1},{1,0},{2,3},{3,2},{4,5},{5,4},{6,7},{7,6},{8,9},{9,8},{10,11... | collective-permute-start | bytes 393224 | tf_op jit(solution)/shard_map/ppermute | solution.py:33
  31.1 3.1 %collective-permute-done.9 = bf16[128,512]{1,0:T(8,128)(2,1)S(1)} collective-permute-done((bf16[128,512]{1,0:T(8,128)(2,1)S(1)}, bf16[128,512]{1,0:T(8,128)(2,1)S(1)}, u32[]{:S(2)}, u32[]{:S(2)}) %collective-permute-start.9) | collective-permute-done | bytes 131104 | tf_op jit(solution)/shard_map/ppermute | solution.py:33
  35.6 5.2 %collective-permute-done.5 = bf16[128,512]{1,0:T(8,128)(2,1)S(1)} collective-permute-done((bf16[128,512]{1,0:T(8,128)(2,1)S(1)}, bf16[128,512]{1,0:T(8,128)(2,1)S(1)}, u32[]{:S(2)}, u32[]{:S(2)}) %collective-permute-start.5) | collective-permute-done | bytes 131104 | tf_op jit(solution)/shard_map/ppermute | solution.py:33
  40.8 3.1 %collective-permute-done.10 = bf16[128,512]{1,0:T(8,128)(2,1)S(1)} collective-permute-done((bf16[128,512]{1,0:T(8,128)(2,1)S(1)}, bf16[128,512]{1,0:T(8,128)(2,1)S(1)}, u32[]{:S(2)}, u32[]{:S(2)}) %collective-permute-start.10) | collective-permute-done | bytes 131104 | tf_op jit(solution)/shard_map/ppermute | solution.py:33
  45.9 2.5 %collective-permute-done.11 = bf16[4,2,224,256]{3,2,1,0:T(8,128)(2,1)S(1)} collective-permute-done((bf16[4,2,224,256]{3,2,1,0:T(8,128)(2,1)S(1)}, bf16[4,2,224,256]{3,2,1,0:T(8,128)(2,1)S(1)}, u32[]{:S(2)}, u32[]{:S(2)}) %collective-permute-start.11) | collective-permute-done | bytes 917536 | tf_op jit(solution)/shard_map/ppermute | solution.py:33
  50.2 2.1 %collective-permute-start.14 = (bf16[2,224,256]{2,1,0:T(8,128)(2,1)S(1)}, bf16[2,224,256]{2,1,0:T(8,128)(2,1)S(1)}, u32[]{:S(2)}, u32[]{:S(2)}) collective-permute-start(bf16[2,224,256]{2,1,0:T(8,128)(2,1)S(1)} %get-tuple-element.53), channel_id=1, source_target_pairs={{0,24},{4,28},{8,16},{12,20},{16,8},{20,12},{24,0},{28,4},{1,25},{... | collective-permute-start | bytes 688136 | tf_op jit(solution)/shard_map/ppermute | solution.py:33
  53.7 3.5 %collective-permute-done.12 = bf16[2,224,256]{2,1,0:T(8,128)(2,1)S(1)} collective-permute-done((bf16[2,224,256]{2,1,0:T(8,128)(2,1)S(1)}, bf16[2,224,256]{2,1,0:T(8,128)(2,1)S(1)}, u32[]{:S(2)}, u32[]{:S(2)}) %collective-permute-start.12) | collective-permute-done | bytes 229408 | tf_op jit(solution)/shard_map/ppermute | solution.py:33
  58.6 3.7 %collective-permute-done.13 = bf16[2,224,256]{2,1,0:T(8,128)(2,1)S(1)} collective-permute-done((bf16[2,224,256]{2,1,0:T(8,128)(2,1)S(1)}, bf16[2,224,256]{2,1,0:T(8,128)(2,1)S(1)}, u32[]{:S(2)}, u32[]{:S(2)}) %collective-permute-start.13) | collective-permute-done | bytes 229408 | tf_op jit(solution)/shard_map/ppermute | solution.py:33
  64.0 3.8 %collective-permute-done.24.refs_2_ = bf16[256,512]{1,0:T(8,128)(2,1)S(1)} collective-permute-done((bf16[256,512]{1,0:T(8,128)(2,1)S(1)}, bf16[256,512]{1,0:T(8,128)(2,1)S(1)}, u32[]{:S(2)}, u32[]{:S(2)}) %collective-permute-start.24) | collective-permute-done | bytes 262176 | tf_op jit(solution)/shard_map/ppermute | solution.py:33
  67.8 5.8 %collective-permute-done.26.refs_4_ = bf16[256,512]{1,0:T(8,128)(2,1)S(1)} collective-permute-done((bf16[256,512]{1,0:T(8,128)(2,1)S(1)}, bf16[256,512]{1,0:T(8,128)(2,1)S(1)}, u32[]{:S(2)}, u32[]{:S(2)}) %collective-permute-start.26) | collective-permute-done | bytes 262176 | tf_op jit(solution)/shard_map/ppermute | solution.py:33
  78.1 5.2 %client_activations.3.rest_0_ = bf16[256,768]{1,0:T(8,128)(2,1)S(1)} custom-call(s32[2]{0:T(128)S(1)} %pad_add_fusion.place, bf16[256,512]{1,0:T(8,128)(2,1)S(1)} %pad_maximum_fusion.rows.value.refs_0_, bf16[256,512]{1,0:T(8,128)(2,1)S(1)} %collective-permute-done.23.refs_1_, bf16[256,512]{1,0:T(8,128)(2,1)S(1)} %collective-permute-done.24.refs_2_, ...), custom_call_target="tpu_custom_call" | custom-call | flops 3221225472 | bytes 12582912 | tf_op jit(solution)/shard_map/client_activations/pallas_call | solution.py:156
  83.4 6.6 %client_activations.2.rest_1_ = bf16[256,1024]{1,0:T(8,128)(2,1)S(1)} custom-call(s32[2]{0:T(128)S(1)} %pad_add_fusion.place, bf16[256,512]{1,0:T(8,128)(2,1)S(1)} %pad_maximum_fusion.rows.value.refs_0_, bf16[256,512]{1,0:T(8,128)(2,1)S(1)} %collective-permute-done.23.refs_1_, bf16[256,512]{1,0:T(8,128)(2,1)S(1)} %collective-permute-done.24.refs_2_, ...), custom_call_target="tpu_custom_call" | custom-call | flops 4294967296 | bytes 16777216 | tf_op jit(solution)/shard_map/client_activations/pallas_call | solution.py:156
  94.3 7.3 %match.2 = (f32[3584,256]{1,0:T(8,128)S(1)}, f32[1,3584]{1,0:T(1,128)S(1)}) custom-call(bf16[3584,256]{1,0:T(8,128)(2,1)S(1)} %bitcast.79, bf16[256,768]{1,0:T(8,128)(2,1)S(1)} %client_activations.3.rest_0_, bf16[256,1024]{1,0:T(8,128)(2,1)S(1)} %client_activations.2.rest_1_), custom_call_target="tpu_custom_call" | custom-call | flops 6576668672 | bytes 7340032 | tf_op jit(solution)/shard_map/match/pallas_call | solution.py:309
  101.7 3.5 %match.3 = (f32[3584,256]{1,0:T(8,128)S(1)}, f32[1,3584]{1,0:T(1,128)S(1)}) custom-call(bf16[3584,256]{1,0:T(8,128)(2,1)S(1)} %bitcast.80, bf16[256,768]{1,0:T(8,128)(2,1)S(1)} %collective-permute-done.31.rest_0_, f32[3584,256]{1,0:T(8,128)S(1)} %get-tuple-element.25.rest_1_, f32[1,3584]{1,0:T(1,128)S(1)} %get-tuple-element.26.rest_2_), custom_call_target="tpu_custom_call" | custom-call | flops 2818572288 | bytes 7340032 | tf_op jit(solution)/shard_map/match/pallas_call | solution.py:309
  105.3 5.4 %match_last.1 = (bf16[4,2,224,256]{3,2,1,0:T(8,128)(2,1)S(1)}, bf16[4,2,224,256]{3,2,1,0:T(8,128)(2,1)S(1)}, f32[2,3584]{1,0:T(2,128)S(1)}) custom-call(bf16[3584,256]{1,0:T(8,128)(2,1)S(1)} %bitcast.81, bf16[256,1024]{1,0:T(8,128)(2,1)S(1)} %collective-permute-done.30.columns, f32[3584,256]{1,0:T(8,128)S(1)} %get-tuple-element.27.before, ...), custom_call_target="tpu_custom_call" | custom-call | flops 3758096384 | bytes 7340032 | tf_op jit(solution)/shard_map/match_last/pallas_call | solution.py:332
  111.0 4.6 %collective-permute-done.33 = f32[2,2,1792]{2,1,0:T(2,128)S(1)} collective-permute-done((f32[2,2,1792]{2,1,0:T(2,128)S(1)}, f32[2,2,1792]{2,1,0:T(2,128)S(1)}, u32[]{:S(2)}, u32[]{:S(2)}) %collective-permute-start.33) | collective-permute-done | bytes 28704 | tf_op jit(solution)/shard_map/ppermute | solution.py:33
  128.4 2.1 %collective-permute-done.36 = bf16[224,256]{1,0:T(8,128)(2,1)S(1)} collective-permute-done((bf16[224,256]{1,0:T(8,128)(2,1)S(1)}, bf16[224,256]{1,0:T(8,128)(2,1)S(1)}, u32[]{:S(2)}, u32[]{:S(2)}) %collective-permute-start.36) | collective-permute-done | bytes 114720 | tf_op jit(solution)/shard_map/ppermute | solution.py:33
  130.5 2.7 %collective-permute-done.41 = bf16[224,256]{1,0:T(8,128)(2,1)S(1)} collective-permute-done((bf16[224,256]{1,0:T(8,128)(2,1)S(1)}, bf16[224,256]{1,0:T(8,128)(2,1)S(1)}, u32[]{:S(2)}, u32[]{:S(2)}) %collective-permute-start.41) | collective-permute-done | bytes 114720 | tf_op jit(solution)/shard_map/ppermute | solution.py:33
  (151 shorter events, 53.7 us)
Async XLA Ops:
  10.2 7.3 %collective-permute-start.1 = (bf16[128,512]{1,0:T(8,128)(2,1)S(1)}, bf16[128,512]{1,0:T(8,128)(2,1)S(1)}, u32[]{:S(2)}, u32[]{:S(2)}) collective-permute-start(bf16[128,512]{1,0:T(8,128)(2,1)S(1)} %get-tuple-element.51), channel_id=1, source_target_pairs={{0,8},{4,12},{8,0},{12,4},{16,24},{20,28},{24,16},{28,20},{1,9},{5... | collective-permute-start | bytes 393224 | tf_op jit(solution)/shard_map/ppermute | solution.py:33
  12.6 8.4 %collective-permute-start.2 = (bf16[128,512]{1,0:T(8,128)(2,1)S(1)}, bf16[128,512]{1,0:T(8,128)(2,1)S(1)}, u32[]{:S(2)}, u32[]{:S(2)}) collective-permute-start(bf16[128,512]{1,0:T(8,128)(2,1)S(1)} %get-tuple-element.50), channel_id=1, source_target_pairs={{0,16},{4,20},{8,24},{12,28},{16,0},{20,4},{24,8},{28,12},{1,17},{... | collective-permute-start | bytes 393224 | tf_op jit(solution)/shard_map/ppermute | solution.py:33
  14.0 8.1 %collective-permute-start.3 = (bf16[128,512]{1,0:T(8,128)(2,1)S(1)}, bf16[128,512]{1,0:T(8,128)(2,1)S(1)}, u32[]{:S(2)}, u32[]{:S(2)}) collective-permute-start(bf16[128,512]{1,0:T(8,128)(2,1)S(1)} %get-tuple-element.49), channel_id=1, source_target_pairs={{0,24},{4,28},{8,16},{12,20},{16,8},{20,12},{24,0},{28,4},{1,25},{... | collective-permute-start | bytes 393224 | tf_op jit(solution)/shard_map/ppermute | solution.py:33
  14.9 13.2 %collective-permute-start.6 = (bf16[128,512]{1,0:T(8,128)(2,1)S(1)}, bf16[128,512]{1,0:T(8,128)(2,1)S(1)}, u32[]{:S(2)}, u32[]{:S(2)}) collective-permute-start(bf16[128,512]{1,0:T(8,128)(2,1)S(1)} %get-tuple-element.46), channel_id=1, source_target_pairs={{0,8},{4,12},{8,0},{12,4},{16,24},{20,28},{24,16},{28,20},{1,9},{5... | collective-permute-start | bytes 393224 | tf_op jit(solution)/shard_map/ppermute | solution.py:33
  16.1 12.0 %collective-permute-start.7 = (bf16[128,512]{1,0:T(8,128)(2,1)S(1)}, bf16[128,512]{1,0:T(8,128)(2,1)S(1)}, u32[]{:S(2)}, u32[]{:S(2)}) collective-permute-start(bf16[128,512]{1,0:T(8,128)(2,1)S(1)} %get-tuple-element.48), channel_id=1, source_target_pairs={{0,16},{4,20},{8,24},{12,28},{16,0},{20,4},{24,8},{28,12},{1,17},{... | collective-permute-start | bytes 393224 | tf_op jit(solution)/shard_map/ppermute | solution.py:33
  17.5 10.6 %collective-permute-start.8 = (bf16[128,512]{1,0:T(8,128)(2,1)S(1)}, bf16[128,512]{1,0:T(8,128)(2,1)S(1)}, u32[]{:S(2)}, u32[]{:S(2)}) collective-permute-start(bf16[128,512]{1,0:T(8,128)(2,1)S(1)} %get-tuple-element.47), channel_id=1, source_target_pairs={{0,24},{4,28},{8,16},{12,20},{16,8},{20,12},{24,0},{28,4},{1,25},{... | collective-permute-start | bytes 393224 | tf_op jit(solution)/shard_map/ppermute | solution.py:33
  30.3 10.5 %collective-permute-start.5 = (bf16[128,512]{1,0:T(8,128)(2,1)S(1)}, bf16[128,512]{1,0:T(8,128)(2,1)S(1)}, u32[]{:S(2)}, u32[]{:S(2)}) collective-permute-start(bf16[128,512]{1,0:T(8,128)(2,1)S(1)} %add.99), channel_id=1, source_target_pairs={{0,2},{1,3},{2,0},{3,1},{4,6},{5,7},{6,4},{7,5},{8,10},{9,11},{10,... | collective-permute-start | bytes 393224 | tf_op jit(solution)/shard_map/ppermute | solution.py:33
  34.2 9.6 %collective-permute-start.10 = (bf16[128,512]{1,0:T(8,128)(2,1)S(1)}, bf16[128,512]{1,0:T(8,128)(2,1)S(1)}, u32[]{:S(2)}, u32[]{:S(2)}) collective-permute-start(bf16[128,512]{1,0:T(8,128)(2,1)S(1)} %add.104), channel_id=1, source_target_pairs={{0,2},{1,3},{2,0},{3,1},{4,6},{5,7},{6,4},{7,5},{8,10},{9,11},{10,... | collective-permute-start | bytes 393224 | tf_op jit(solution)/shard_map/ppermute | solution.py:33
  48.7 8.5 %collective-permute-start.12 = (bf16[2,224,256]{2,1,0:T(8,128)(2,1)S(1)}, bf16[2,224,256]{2,1,0:T(8,128)(2,1)S(1)}, u32[]{:S(2)}, u32[]{:S(2)}) collective-permute-start(bf16[2,224,256]{2,1,0:T(8,128)(2,1)S(1)} %get-tuple-element.52), channel_id=1, source_target_pairs={{0,8},{4,12},{8,0},{12,4},{16,24},{20,28},{24,16},{28,20},{1,9},{5... | collective-permute-start | bytes 688136 | tf_op jit(solution)/shard_map/ppermute | solution.py:33
  50.2 12.1 %collective-permute-start.13 = (bf16[2,224,256]{2,1,0:T(8,128)(2,1)S(1)}, bf16[2,224,256]{2,1,0:T(8,128)(2,1)S(1)}, u32[]{:S(2)}, u32[]{:S(2)}) collective-permute-start(bf16[2,224,256]{2,1,0:T(8,128)(2,1)S(1)} %get-tuple-element.54), channel_id=1, source_target_pairs={{0,16},{4,20},{8,24},{12,28},{16,0},{20,4},{24,8},{28,12},{1,17},{... | collective-permute-start | bytes 688136 | tf_op jit(solution)/shard_map/ppermute | solution.py:33
  50.2 13.2 %collective-permute-start.14 = (bf16[2,224,256]{2,1,0:T(8,128)(2,1)S(1)}, bf16[2,224,256]{2,1,0:T(8,128)(2,1)S(1)}, u32[]{:S(2)}, u32[]{:S(2)}) collective-permute-start(bf16[2,224,256]{2,1,0:T(8,128)(2,1)S(1)} %get-tuple-element.53), channel_id=1, source_target_pairs={{0,24},{4,28},{8,16},{12,20},{16,8},{20,12},{24,0},{28,4},{1,25},{... | collective-permute-start | bytes 688136 | tf_op jit(solution)/shard_map/ppermute | solution.py:33
  52.3 22.2 %collective-permute-start.23 = (bf16[256,512]{1,0:T(8,128)(2,1)S(1)}, bf16[256,512]{1,0:T(8,128)(2,1)S(1)}, u32[]{:S(2)}, u32[]{:S(2)}) collective-permute-start(bf16[256,512]{1,0:T(8,128)(2,1)S(1)} %pad_maximum_fusion.rows.value.refs_0_), channel_id=1, source_target_pairs={{0,4},{4,0},{8,12},{12,8},{16,20},{20,16},{24,28},{28,24},{1,5},{5... | collective-permute-start | bytes 786440 | tf_op jit(solution)/shard_map/ppermute | solution.py:33
  52.3 15.5 %collective-permute-start.24 = (bf16[256,512]{1,0:T(8,128)(2,1)S(1)}, bf16[256,512]{1,0:T(8,128)(2,1)S(1)}, u32[]{:S(2)}, u32[]{:S(2)}) collective-permute-start(bf16[256,512]{1,0:T(8,128)(2,1)S(1)} %tied.3), channel_id=1, source_target_pairs={{0,8},{4,12},{8,0},{12,4},{16,24},{20,28},{24,16},{28,20},{1,9},{5... | collective-permute-start | bytes 786440 | tf_op jit(solution)/shard_map/ppermute | solution.py:33
  57.3 16.4 %collective-permute-start.26 = (bf16[256,512]{1,0:T(8,128)(2,1)S(1)}, bf16[256,512]{1,0:T(8,128)(2,1)S(1)}, u32[]{:S(2)}, u32[]{:S(2)}) collective-permute-start(bf16[256,512]{1,0:T(8,128)(2,1)S(1)} %tied.3), channel_id=1, source_target_pairs={{0,16},{4,20},{8,24},{12,28},{16,0},{20,4},{24,8},{28,12},{1,17},{... | collective-permute-start | bytes 786440 | tf_op jit(solution)/shard_map/ppermute | solution.py:33
  62.3 11.4 %collective-permute-start.28 = (bf16[256,512]{1,0:T(8,128)(2,1)S(1)}, bf16[256,512]{1,0:T(8,128)(2,1)S(1)}, u32[]{:S(2)}, u32[]{:S(2)}) collective-permute-start(bf16[256,512]{1,0:T(8,128)(2,1)S(1)} %tied.3), channel_id=1, source_target_pairs={{0,24},{4,28},{8,16},{12,20},{16,8},{20,12},{24,0},{28,4},{1,25},{... | collective-permute-start | bytes 786440 | tf_op jit(solution)/shard_map/ppermute | solution.py:33
  64.0 10.4 %collective-permute-start.15 = (bf16[224,256]{1,0:T(8,128)(2,1)S(1)}, bf16[224,256]{1,0:T(8,128)(2,1)S(1)}, u32[]{:S(2)}, u32[]{:S(2)}) collective-permute-start(bf16[224,256]{1,0:T(8,128)(2,1)S(1)} %multiply_convert_fusion), channel_id=1, source_target_pairs={{0,2},{1,3},{2,0},{3,1},{4,6},{5,7},{6,4},{7,5},{8,10},{9,11},{10,... | collective-permute-start | bytes 344072 | tf_op jit(solution)/shard_map/ppermute | solution.py:33
  67.8 7.4 %collective-permute-start.25 = (bf16[256,512]{1,0:T(8,128)(2,1)S(1)}, bf16[256,512]{1,0:T(8,128)(2,1)S(1)}, u32[]{:S(2)}, u32[]{:S(2)}) collective-permute-start(bf16[256,512]{1,0:T(8,128)(2,1)S(1)} %collective-permute-done.24.refs_2_), channel_id=1, source_target_pairs={{0,4},{4,0},{8,12},{12,8},{16,20},{20,16},{24,28},{28,24},{1,5},{5... | collective-permute-start | bytes 786440 | tf_op jit(solution)/shard_map/ppermute | solution.py:33
  74.4 15.6 %collective-permute-start.16 = (bf16[2,224,256]{2,1,0:T(8,128)(2,1)S(1)}, bf16[2,224,256]{2,1,0:T(8,128)(2,1)S(1)}, u32[]{:S(2)}, u32[]{:S(2)}) collective-permute-start(bf16[2,224,256]{2,1,0:T(8,128)(2,1)S(1)} %pad_maximum_fusion.1), channel_id=1, source_target_pairs={{0,4},{4,0},{8,12},{12,8},{16,20},{20,16},{24,28},{28,24},{1,5},{5... | collective-permute-start | bytes 688136 | tf_op jit(solution)/shard_map/ppermute | solution.py:33
  74.5 17.5 %collective-permute-start.17 = (bf16[2,224,256]{2,1,0:T(8,128)(2,1)S(1)}, bf16[2,224,256]{2,1,0:T(8,128)(2,1)S(1)}, u32[]{:S(2)}, u32[]{:S(2)}) collective-permute-start(bf16[2,224,256]{2,1,0:T(8,128)(2,1)S(1)} %pad_maximum_fusion.1), channel_id=1, source_target_pairs={{0,8},{4,12},{8,0},{12,4},{16,24},{20,28},{24,16},{28,20},{1,9},{5... | collective-permute-start | bytes 688136 | tf_op jit(solution)/shard_map/ppermute | solution.py:33
  75.2 16.8 %collective-permute-start.19 = (bf16[2,224,256]{2,1,0:T(8,128)(2,1)S(1)}, bf16[2,224,256]{2,1,0:T(8,128)(2,1)S(1)}, u32[]{:S(2)}, u32[]{:S(2)}) collective-permute-start(bf16[2,224,256]{2,1,0:T(8,128)(2,1)S(1)} %pad_maximum_fusion.1), channel_id=1, source_target_pairs={{0,16},{4,20},{8,24},{12,28},{16,0},{20,4},{24,8},{28,12},{1,17},{... | collective-permute-start | bytes 688136 | tf_op jit(solution)/shard_map/ppermute | solution.py:33
  76.6 16.0 %collective-permute-start.21 = (bf16[2,224,256]{2,1,0:T(8,128)(2,1)S(1)}, bf16[2,224,256]{2,1,0:T(8,128)(2,1)S(1)}, u32[]{:S(2)}, u32[]{:S(2)}) collective-permute-start(bf16[2,224,256]{2,1,0:T(8,128)(2,1)S(1)} %pad_maximum_fusion.1), channel_id=1, source_target_pairs={{0,24},{4,28},{8,16},{12,20},{16,8},{20,12},{24,0},{28,4},{1,25},{... | collective-permute-start | bytes 688136 | tf_op jit(solution)/shard_map/ppermute | solution.py:33
  83.3 18.4 %collective-permute-start.31 = (bf16[256,768]{1,0:T(8,128)(2,1)S(1)}, bf16[256,768]{1,0:T(8,128)(2,1)S(1)}, u32[]{:S(2)}, u32[]{:S(2)}) collective-permute-start(bf16[256,768]{1,0:T(8,128)(2,1)S(1)} %client_activations.3.rest_0_), channel_id=1, source_target_pairs={{0,1},{1,0},{2,3},{3,2},{4,5},{5,4},{6,7},{7,6},{8,9},{9,8},{10,11... | collective-permute-start | bytes 1179656 | tf_op jit(solution)/shard_map/ppermute | solution.py:33
  90.0 15.3 %collective-permute-start.30 = (bf16[256,1024]{1,0:T(8,128)(2,1)S(1)}, bf16[256,1024]{1,0:T(8,128)(2,1)S(1)}, u32[]{:S(2)}, u32[]{:S(2)}) collective-permute-start(bf16[256,1024]{1,0:T(8,128)(2,1)S(1)} %client_activations.2.rest_1_), channel_id=1, source_target_pairs={{0,1},{1,0},{2,3},{3,2},{4,5},{5,4},{6,7},{7,6},{8,9},{9,8},{10,11... | collective-permute-start | bytes 1572872 | tf_op jit(solution)/shard_map/ppermute | solution.py:33
  122.2 8.3 %collective-permute-start.36 = (bf16[224,256]{1,0:T(8,128)(2,1)S(1)}, bf16[224,256]{1,0:T(8,128)(2,1)S(1)}, u32[]{:S(2)}, u32[]{:S(2)}) collective-permute-start(bf16[224,256]{1,0:T(8,128)(2,1)S(1)} %get-tuple-element.35), channel_id=1, source_target_pairs={{0,16},{4,20},{8,24},{12,28},{16,0},{20,4},{24,8},{28,12},{1,17},{... | collective-permute-start | bytes 344072 | tf_op jit(solution)/shard_map/ppermute | solution.py:33
  (35 other events, 476.1 us)

commit v7 on v6

--- a/solution.py
+++ b/solution.py
@@ -10,7 +10,7 @@
 sharpness = 40.0
 log2_e = 1.4426950408889634
 group_rows = 16
-fetch_slots = 16
+fetch_slots = 32
 bf16 = jnp.bfloat16
 f32 = jnp.float32
 whole = pl.BlockSpec(memory_space=pltpu.VMEM)

time: 145 us -> 145 us (level)
  transfers between devices with their start and end apart: 49 -> 49, of which waited for: 27 -> 26; matrix products, arithmetic and copies ran while one was open for 1% -> 1% of each run, Pallas kernels for 16% -> 16%
where the time goes in v7:
time: 145 us
  waiting for transfers between devices  58 us (40%)
  starting transfers between devices  43.5 us (30%)
  Pallas kernels  38 us (26%)
  other arithmetic  2.18 us (2%)
  local copies, waits for them, and re-layouts  2.05 us (1%)
    ppermute x49, waiting for transfers between devices, xor_permute(): return lax.ppermute(value, axis, [(i, i ^ mask) for i in range(size)])  58 us
    ppermute x49, starting transfers between devices, xor_permute(): return lax.ppermute(value, axis, [(i, i ^ mask) for i in range(size)])  43.5 us
    pallas_call x2, Pallas kernels, client_activations(): pl.pallas_call(functools.partial(client_kernel, start), grid=(units // wi...  11.8 us
    pallas_call x2, Pallas kernels, match(): pl.pallas_call(functools.partial(match_kernel, len(columns)), grid=(group...  10.8 us
    pallas_call x1, Pallas kernels, match_last(): pl.pallas_call(match_last_kernel, grid=(groups,), out_shape=(halves, halv...  5.45 us
    pallas_call x1, Pallas kernels, select_rows(): pl.pallas_call(select_kernel, out_shape=(half, half), in_specs=[scalars,...  5.41 us
  transfers between devices with their start and end apart: 49, of which 26 were waited for; matrix products, arithmetic and copies ran while one was open for 1% of the time, Pallas kernels for 16%

profile of v7, /device:TPU:0, one launch (start us, length us, event | category | flops | bytes accessed | tf_op | source)
XLA Modules:
  0.0 145.2 jit_solution(5152017858833699561)
XLA Ops:
  2.1 5.4 %select_rows.1 = (bf16[4,256,512]{2,1,0:T(8,128)(2,1)S(1)}, bf16[4,256,512]{2,1,0:T(8,128)(2,1)S(1)}) custom-call(s32[2]{0:T(128)S(1)} %pad_add_fusion.place, s32[256]{0:T(256)S(1)} %copy-done.5, f32[1,4096]{1,0:T(1,128)S(1)} %bitcast.82, bf16[2048,4096]{1,0:T(8,128)(2,1)} %table.1), custom_call_target="tpu_custom_call" | custom-call | flops 4000000 | bytes 4000000 | tf_op jit(solution)/shard_map/select_rows/pallas_call | solution.py:104
  7.6 2.6 %collective-permute-done = bf16[4,256,512]{2,1,0:T(8,128)(2,1)S(1)} collective-permute-done((bf16[4,256,512]{2,1,0:T(8,128)(2,1)S(1)}, bf16[4,256,512]{2,1,0:T(8,128)(2,1)S(1)}, u32[]{:S(2)}, u32[]{:S(2)}) %collective-permute-start) | collective-permute-done | bytes 1048608 | tf_op jit(solution)/shard_map/ppermute | solution.py:33
  10.8 3.6 %collective-permute-start.1 = (bf16[128,512]{1,0:T(8,128)(2,1)S(1)}, bf16[128,512]{1,0:T(8,128)(2,1)S(1)}, u32[]{:S(2)}, u32[]{:S(2)}) collective-permute-start(bf16[128,512]{1,0:T(8,128)(2,1)S(1)} %get-tuple-element.51), channel_id=1, source_target_pairs={{0,8},{4,12},{8,0},{12,4},{16,24},{20,28},{24,16},{28,20},{1,9},{5... | collective-permute-start | bytes 393224 | tf_op jit(solution)/shard_map/ppermute | solution.py:33
  18.4 2.3 %collective-permute-start.8 = (bf16[128,512]{1,0:T(8,128)(2,1)S(1)}, bf16[128,512]{1,0:T(8,128)(2,1)S(1)}, u32[]{:S(2)}, u32[]{:S(2)}) collective-permute-start(bf16[128,512]{1,0:T(8,128)(2,1)S(1)} %get-tuple-element.47), channel_id=1, source_target_pairs={{0,24},{4,28},{8,16},{12,20},{16,8},{20,12},{24,0},{28,4},{1,25},{... | collective-permute-start | bytes 393224 | tf_op jit(solution)/shard_map/ppermute | solution.py:33
  20.7 4.0 %collective-permute-done.2 = bf16[128,512]{1,0:T(8,128)(2,1)S(1)} collective-permute-done((bf16[128,512]{1,0:T(8,128)(2,1)S(1)}, bf16[128,512]{1,0:T(8,128)(2,1)S(1)}, u32[]{:S(2)}, u32[]{:S(2)}) %collective-permute-start.2) | collective-permute-done | bytes 131104 | tf_op jit(solution)/shard_map/ppermute | solution.py:33
  24.8 4.9 %collective-permute-done.4.rest_0_ = bf16[128,512]{1,0:T(8,128)(2,1)S(1)} collective-permute-done((bf16[128,512]{1,0:T(8,128)(2,1)S(1)}, bf16[128,512]{1,0:T(8,128)(2,1)S(1)}, u32[]{:S(2)}, u32[]{:S(2)}) %collective-permute-start.4) | collective-permute-done | bytes 131104 | tf_op jit(solution)/shard_map/ppermute | solution.py:33
  30.0 5.0 %collective-permute-start.5 = (bf16[128,512]{1,0:T(8,128)(2,1)S(1)}, bf16[128,512]{1,0:T(8,128)(2,1)S(1)}, u32[]{:S(2)}, u32[]{:S(2)}) collective-permute-start(bf16[128,512]{1,0:T(8,128)(2,1)S(1)} %add.99), channel_id=1, source_target_pairs={{0,2},{1,3},{2,0},{3,1},{4,6},{5,7},{6,4},{7,5},{8,10},{9,11},{10,... | collective-permute-start | bytes 393224 | tf_op jit(solution)/shard_map/ppermute | solution.py:33
  36.0 3.1 %collective-permute-start.10 = (bf16[128,512]{1,0:T(8,128)(2,1)S(1)}, bf16[128,512]{1,0:T(8,128)(2,1)S(1)}, u32[]{:S(2)}, u32[]{:S(2)}) collective-permute-start(bf16[128,512]{1,0:T(8,128)(2,1)S(1)} %add.104), channel_id=1, source_target_pairs={{0,2},{1,3},{2,0},{3,1},{4,6},{5,7},{6,4},{7,5},{8,10},{9,11},{10,... | collective-permute-start | bytes 393224 | tf_op jit(solution)/shard_map/ppermute | solution.py:33
  39.1 2.9 %collective-permute-done.5 = bf16[128,512]{1,0:T(8,128)(2,1)S(1)} collective-permute-done((bf16[128,512]{1,0:T(8,128)(2,1)S(1)}, bf16[128,512]{1,0:T(8,128)(2,1)S(1)}, u32[]{:S(2)}, u32[]{:S(2)}) %collective-permute-start.5) | collective-permute-done | bytes 131104 | tf_op jit(solution)/shard_map/ppermute | solution.py:33
  42.0 3.0 %collective-permute-done.10 = bf16[128,512]{1,0:T(8,128)(2,1)S(1)} collective-permute-done((bf16[128,512]{1,0:T(8,128)(2,1)S(1)}, bf16[128,512]{1,0:T(8,128)(2,1)S(1)}, u32[]{:S(2)}, u32[]{:S(2)}) %collective-permute-start.10) | collective-permute-done | bytes 131104 | tf_op jit(solution)/shard_map/ppermute | solution.py:33
  47.0 2.5 %collective-permute-done.11 = bf16[4,2,224,256]{3,2,1,0:T(8,128)(2,1)S(1)} collective-permute-done((bf16[4,2,224,256]{3,2,1,0:T(8,128)(2,1)S(1)}, bf16[4,2,224,256]{3,2,1,0:T(8,128)(2,1)S(1)}, u32[]{:S(2)}, u32[]{:S(2)}) %collective-permute-start.11) | collective-permute-done | bytes 917536 | tf_op jit(solution)/shard_map/ppermute | solution.py:33
  54.0 4.3 %collective-permute-done.12 = bf16[2,224,256]{2,1,0:T(8,128)(2,1)S(1)} collective-permute-done((bf16[2,224,256]{2,1,0:T(8,128)(2,1)S(1)}, bf16[2,224,256]{2,1,0:T(8,128)(2,1)S(1)}, u32[]{:S(2)}, u32[]{:S(2)}) %collective-permute-start.12) | collective-permute-done | bytes 229408 | tf_op jit(solution)/shard_map/ppermute | solution.py:33
  58.3 4.8 %collective-permute-done.13 = bf16[2,224,256]{2,1,0:T(8,128)(2,1)S(1)} collective-permute-done((bf16[2,224,256]{2,1,0:T(8,128)(2,1)S(1)}, bf16[2,224,256]{2,1,0:T(8,128)(2,1)S(1)}, u32[]{:S(2)}, u32[]{:S(2)}) %collective-permute-start.13) | collective-permute-done | bytes 229408 | tf_op jit(solution)/shard_map/ppermute | solution.py:33
  64.7 4.2 %collective-permute-done.24.refs_2_ = bf16[256,512]{1,0:T(8,128)(2,1)S(1)} collective-permute-done((bf16[256,512]{1,0:T(8,128)(2,1)S(1)}, bf16[256,512]{1,0:T(8,128)(2,1)S(1)}, u32[]{:S(2)}, u32[]{:S(2)}) %collective-permute-start.24) | collective-permute-done | bytes 262176 | tf_op jit(solution)/shard_map/ppermute | solution.py:33
  68.9 5.0 %collective-permute-done.26.refs_4_ = bf16[256,512]{1,0:T(8,128)(2,1)S(1)} collective-permute-done((bf16[256,512]{1,0:T(8,128)(2,1)S(1)}, bf16[256,512]{1,0:T(8,128)(2,1)S(1)}, u32[]{:S(2)}, u32[]{:S(2)}) %collective-permute-start.26) | collective-permute-done | bytes 262176 | tf_op jit(solution)/shard_map/ppermute | solution.py:33
  78.4 5.2 %client_activations.3.rest_0_ = bf16[256,768]{1,0:T(8,128)(2,1)S(1)} custom-call(s32[2]{0:T(128)S(1)} %pad_add_fusion.place, bf16[256,512]{1,0:T(8,128)(2,1)S(1)} %pad_maximum_fusion.rows.value.refs_0_, bf16[256,512]{1,0:T(8,128)(2,1)S(1)} %collective-permute-done.23.refs_1_, bf16[256,512]{1,0:T(8,128)(2,1)S(1)} %collective-permute-done.24.refs_2_, ...), custom_call_target="tpu_custom_call" | custom-call | flops 3221225472 | bytes 12582912 | tf_op jit(solution)/shard_map/client_activations/pallas_call | solution.py:156
  83.7 6.6 %client_activations.2.rest_1_ = bf16[256,1024]{1,0:T(8,128)(2,1)S(1)} custom-call(s32[2]{0:T(128)S(1)} %pad_add_fusion.place, bf16[256,512]{1,0:T(8,128)(2,1)S(1)} %pad_maximum_fusion.rows.value.refs_0_, bf16[256,512]{1,0:T(8,128)(2,1)S(1)} %collective-permute-done.23.refs_1_, bf16[256,512]{1,0:T(8,128)(2,1)S(1)} %collective-permute-done.24.refs_2_, ...), custom_call_target="tpu_custom_call" | custom-call | flops 4294967296 | bytes 16777216 | tf_op jit(solution)/shard_map/client_activations/pallas_call | solution.py:156
  90.2 2.1 %collective-permute-start.30 = (bf16[256,1024]{1,0:T(8,128)(2,1)S(1)}, bf16[256,1024]{1,0:T(8,128)(2,1)S(1)}, u32[]{:S(2)}, u32[]{:S(2)}) collective-permute-start(bf16[256,1024]{1,0:T(8,128)(2,1)S(1)} %client_activations.2.rest_1_), channel_id=1, source_target_pairs={{0,1},{1,0},{2,3},{3,2},{4,5},{5,4},{6,7},{7,6},{8,9},{9,8},{10,11... | collective-permute-start | bytes 1572872 | tf_op jit(solution)/shard_map/ppermute | solution.py:33
  94.6 7.3 %match.2 = (f32[3584,256]{1,0:T(8,128)S(1)}, f32[1,3584]{1,0:T(1,128)S(1)}) custom-call(bf16[3584,256]{1,0:T(8,128)(2,1)S(1)} %bitcast.79, bf16[256,768]{1,0:T(8,128)(2,1)S(1)} %client_activations.3.rest_0_, bf16[256,1024]{1,0:T(8,128)(2,1)S(1)} %client_activations.2.rest_1_), custom_call_target="tpu_custom_call" | custom-call | flops 6576668672 | bytes 7340032 | tf_op jit(solution)/shard_map/match/pallas_call | solution.py:309
  102.0 3.5 %match.3 = (f32[3584,256]{1,0:T(8,128)S(1)}, f32[1,3584]{1,0:T(1,128)S(1)}) custom-call(bf16[3584,256]{1,0:T(8,128)(2,1)S(1)} %bitcast.80, bf16[256,768]{1,0:T(8,128)(2,1)S(1)} %collective-permute-done.31.rest_0_, f32[3584,256]{1,0:T(8,128)S(1)} %get-tuple-element.25.rest_1_, f32[1,3584]{1,0:T(1,128)S(1)} %get-tuple-element.26.rest_2_), custom_call_target="tpu_custom_call" | custom-call | flops 2818572288 | bytes 7340032 | tf_op jit(solution)/shard_map/match/pallas_call | solution.py:309
  105.5 5.4 %match_last.1 = (bf16[4,2,224,256]{3,2,1,0:T(8,128)(2,1)S(1)}, bf16[4,2,224,256]{3,2,1,0:T(8,128)(2,1)S(1)}, f32[2,3584]{1,0:T(2,128)S(1)}) custom-call(bf16[3584,256]{1,0:T(8,128)(2,1)S(1)} %bitcast.81, bf16[256,1024]{1,0:T(8,128)(2,1)S(1)} %collective-permute-done.30.columns, f32[3584,256]{1,0:T(8,128)S(1)} %get-tuple-element.27.before, ...), custom_call_target="tpu_custom_call" | custom-call | flops 3758096384 | bytes 7340032 | tf_op jit(solution)/shard_map/match_last/pallas_call | solution.py:332
  112.4 3.6 %collective-permute-done.33 = f32[2,2,1792]{2,1,0:T(2,128)S(1)} collective-permute-done((f32[2,2,1792]{2,1,0:T(2,128)S(1)}, f32[2,2,1792]{2,1,0:T(2,128)S(1)}, u32[]{:S(2)}, u32[]{:S(2)}) %collective-permute-start.33) | collective-permute-done | bytes 28704 | tf_op jit(solution)/shard_map/ppermute | solution.py:33
  129.2 2.4 %collective-permute-done.36 = bf16[224,256]{1,0:T(8,128)(2,1)S(1)} collective-permute-done((bf16[224,256]{1,0:T(8,128)(2,1)S(1)}, bf16[224,256]{1,0:T(8,128)(2,1)S(1)}, u32[]{:S(2)}, u32[]{:S(2)}) %collective-permute-start.36) | collective-permute-done | bytes 114720 | tf_op jit(solution)/shard_map/ppermute | solution.py:33
  131.6 2.4 %collective-permute-done.41 = bf16[224,256]{1,0:T(8,128)(2,1)S(1)} collective-permute-done((bf16[224,256]{1,0:T(8,128)(2,1)S(1)}, bf16[224,256]{1,0:T(8,128)(2,1)S(1)}, u32[]{:S(2)}, u32[]{:S(2)}) %collective-permute-start.41) | collective-permute-done | bytes 114720 | tf_op jit(solution)/shard_map/ppermute | solution.py:33
  (151 shorter events, 47.8 us)
Async XLA Ops:
  10.8 7.6 %collective-permute-start.1 = (bf16[128,512]{1,0:T(8,128)(2,1)S(1)}, bf16[128,512]{1,0:T(8,128)(2,1)S(1)}, u32[]{:S(2)}, u32[]{:S(2)}) collective-permute-start(bf16[128,512]{1,0:T(8,128)(2,1)S(1)} %get-tuple-element.51), channel_id=1, source_target_pairs={{0,8},{4,12},{8,0},{12,4},{16,24},{20,28},{24,16},{28,20},{1,9},{5... | collective-permute-start | bytes 393224 | tf_op jit(solution)/shard_map/ppermute | solution.py:33
  14.4 10.2 %collective-permute-start.2 = (bf16[128,512]{1,0:T(8,128)(2,1)S(1)}, bf16[128,512]{1,0:T(8,128)(2,1)S(1)}, u32[]{:S(2)}, u32[]{:S(2)}) collective-permute-start(bf16[128,512]{1,0:T(8,128)(2,1)S(1)} %get-tuple-element.50), channel_id=1, source_target_pairs={{0,16},{4,20},{8,24},{12,28},{16,0},{20,4},{24,8},{28,12},{1,17},{... | collective-permute-start | bytes 393224 | tf_op jit(solution)/shard_map/ppermute | solution.py:33
  14.9 9.7 %collective-permute-start.3 = (bf16[128,512]{1,0:T(8,128)(2,1)S(1)}, bf16[128,512]{1,0:T(8,128)(2,1)S(1)}, u32[]{:S(2)}, u32[]{:S(2)}) collective-permute-start(bf16[128,512]{1,0:T(8,128)(2,1)S(1)} %get-tuple-element.49), channel_id=1, source_target_pairs={{0,24},{4,28},{8,16},{12,20},{16,8},{20,12},{24,0},{28,4},{1,25},{... | collective-permute-start | bytes 393224 | tf_op jit(solution)/shard_map/ppermute | solution.py:33
  15.9 13.8 %collective-permute-start.6 = (bf16[128,512]{1,0:T(8,128)(2,1)S(1)}, bf16[128,512]{1,0:T(8,128)(2,1)S(1)}, u32[]{:S(2)}, u32[]{:S(2)}) collective-permute-start(bf16[128,512]{1,0:T(8,128)(2,1)S(1)} %get-tuple-element.46), channel_id=1, source_target_pairs={{0,8},{4,12},{8,0},{12,4},{16,24},{20,28},{24,16},{28,20},{1,9},{5... | collective-permute-start | bytes 393224 | tf_op jit(solution)/shard_map/ppermute | solution.py:33
  17.9 11.9 %collective-permute-start.7 = (bf16[128,512]{1,0:T(8,128)(2,1)S(1)}, bf16[128,512]{1,0:T(8,128)(2,1)S(1)}, u32[]{:S(2)}, u32[]{:S(2)}) collective-permute-start(bf16[128,512]{1,0:T(8,128)(2,1)S(1)} %get-tuple-element.48), channel_id=1, source_target_pairs={{0,16},{4,20},{8,24},{12,28},{16,0},{20,4},{24,8},{28,12},{1,17},{... | collective-permute-start | bytes 393224 | tf_op jit(solution)/shard_map/ppermute | solution.py:33
  18.4 11.4 %collective-permute-start.8 = (bf16[128,512]{1,0:T(8,128)(2,1)S(1)}, bf16[128,512]{1,0:T(8,128)(2,1)S(1)}, u32[]{:S(2)}, u32[]{:S(2)}) collective-permute-start(bf16[128,512]{1,0:T(8,128)(2,1)S(1)} %get-tuple-element.47), channel_id=1, source_target_pairs={{0,24},{4,28},{8,16},{12,20},{16,8},{20,12},{24,0},{28,4},{1,25},{... | collective-permute-start | bytes 393224 | tf_op jit(solution)/shard_map/ppermute | solution.py:33
  30.0 12.0 %collective-permute-start.5 = (bf16[128,512]{1,0:T(8,128)(2,1)S(1)}, bf16[128,512]{1,0:T(8,128)(2,1)S(1)}, u32[]{:S(2)}, u32[]{:S(2)}) collective-permute-start(bf16[128,512]{1,0:T(8,128)(2,1)S(1)} %add.99), channel_id=1, source_target_pairs={{0,2},{1,3},{2,0},{3,1},{4,6},{5,7},{6,4},{7,5},{8,10},{9,11},{10,... | collective-permute-start | bytes 393224 | tf_op jit(solution)/shard_map/ppermute | solution.py:33
  36.0 8.9 %collective-permute-start.10 = (bf16[128,512]{1,0:T(8,128)(2,1)S(1)}, bf16[128,512]{1,0:T(8,128)(2,1)S(1)}, u32[]{:S(2)}, u32[]{:S(2)}) collective-permute-start(bf16[128,512]{1,0:T(8,128)(2,1)S(1)} %add.104), channel_id=1, source_target_pairs={{0,2},{1,3},{2,0},{3,1},{4,6},{5,7},{6,4},{7,5},{8,10},{9,11},{10,... | collective-permute-start | bytes 393224 | tf_op jit(solution)/shard_map/ppermute | solution.py:33
  49.8 8.5 %collective-permute-start.12 = (bf16[2,224,256]{2,1,0:T(8,128)(2,1)S(1)}, bf16[2,224,256]{2,1,0:T(8,128)(2,1)S(1)}, u32[]{:S(2)}, u32[]{:S(2)}) collective-permute-start(bf16[2,224,256]{2,1,0:T(8,128)(2,1)S(1)} %get-tuple-element.52), channel_id=1, source_target_pairs={{0,8},{4,12},{8,0},{12,4},{16,24},{20,28},{24,16},{28,20},{1,9},{5... | collective-permute-start | bytes 688136 | tf_op jit(solution)/shard_map/ppermute | solution.py:33
  50.4 12.7 %collective-permute-start.13 = (bf16[2,224,256]{2,1,0:T(8,128)(2,1)S(1)}, bf16[2,224,256]{2,1,0:T(8,128)(2,1)S(1)}, u32[]{:S(2)}, u32[]{:S(2)}) collective-permute-start(bf16[2,224,256]{2,1,0:T(8,128)(2,1)S(1)} %get-tuple-element.54), channel_id=1, source_target_pairs={{0,16},{4,20},{8,24},{12,28},{16,0},{20,4},{24,8},{28,12},{1,17},{... | collective-permute-start | bytes 688136 | tf_op jit(solution)/shard_map/ppermute | solution.py:33
  51.9 11.3 %collective-permute-start.14 = (bf16[2,224,256]{2,1,0:T(8,128)(2,1)S(1)}, bf16[2,224,256]{2,1,0:T(8,128)(2,1)S(1)}, u32[]{:S(2)}, u32[]{:S(2)}) collective-permute-start(bf16[2,224,256]{2,1,0:T(8,128)(2,1)S(1)} %get-tuple-element.53), channel_id=1, source_target_pairs={{0,24},{4,28},{8,16},{12,20},{16,8},{20,12},{24,0},{28,4},{1,25},{... | collective-permute-start | bytes 688136 | tf_op jit(solution)/shard_map/ppermute | solution.py:33
  53.4 21.4 %collective-permute-start.23 = (bf16[256,512]{1,0:T(8,128)(2,1)S(1)}, bf16[256,512]{1,0:T(8,128)(2,1)S(1)}, u32[]{:S(2)}, u32[]{:S(2)}) collective-permute-start(bf16[256,512]{1,0:T(8,128)(2,1)S(1)} %pad_maximum_fusion.rows.value.refs_0_), channel_id=1, source_target_pairs={{0,4},{4,0},{8,12},{12,8},{16,20},{20,16},{24,28},{28,24},{1,5},{5... | collective-permute-start | bytes 786440 | tf_op jit(solution)/shard_map/ppermute | solution.py:33
  53.4 15.5 %collective-permute-start.24 = (bf16[256,512]{1,0:T(8,128)(2,1)S(1)}, bf16[256,512]{1,0:T(8,128)(2,1)S(1)}, u32[]{:S(2)}, u32[]{:S(2)}) collective-permute-start(bf16[256,512]{1,0:T(8,128)(2,1)S(1)} %tied.3), channel_id=1, source_target_pairs={{0,8},{4,12},{8,0},{12,4},{16,24},{20,28},{24,16},{28,20},{1,9},{5... | collective-permute-start | bytes 786440 | tf_op jit(solution)/shard_map/ppermute | solution.py:33
  58.3 15.6 %collective-permute-start.26 = (bf16[256,512]{1,0:T(8,128)(2,1)S(1)}, bf16[256,512]{1,0:T(8,128)(2,1)S(1)}, u32[]{:S(2)}, u32[]{:S(2)}) collective-permute-start(bf16[256,512]{1,0:T(8,128)(2,1)S(1)} %tied.3), channel_id=1, source_target_pairs={{0,16},{4,20},{8,24},{12,28},{16,0},{20,4},{24,8},{28,12},{1,17},{... | collective-permute-start | bytes 786440 | tf_op jit(solution)/shard_map/ppermute | solution.py:33
  63.2 10.8 %collective-permute-start.28 = (bf16[256,512]{1,0:T(8,128)(2,1)S(1)}, bf16[256,512]{1,0:T(8,128)(2,1)S(1)}, u32[]{:S(2)}, u32[]{:S(2)}) collective-permute-start(bf16[256,512]{1,0:T(8,128)(2,1)S(1)} %tied.3), channel_id=1, source_target_pairs={{0,24},{4,28},{8,16},{12,20},{16,8},{20,12},{24,0},{28,4},{1,25},{... | collective-permute-start | bytes 786440 | tf_op jit(solution)/shard_map/ppermute | solution.py:33
  63.8 10.8 %collective-permute-start.15 = (bf16[224,256]{1,0:T(8,128)(2,1)S(1)}, bf16[224,256]{1,0:T(8,128)(2,1)S(1)}, u32[]{:S(2)}, u32[]{:S(2)}) collective-permute-start(bf16[224,256]{1,0:T(8,128)(2,1)S(1)} %multiply_convert_fusion), channel_id=1, source_target_pairs={{0,2},{1,3},{2,0},{3,1},{4,6},{5,7},{6,4},{7,5},{8,10},{9,11},{10,... | collective-permute-start | bytes 344072 | tf_op jit(solution)/shard_map/ppermute | solution.py:33
  74.6 15.6 %collective-permute-start.16 = (bf16[2,224,256]{2,1,0:T(8,128)(2,1)S(1)}, bf16[2,224,256]{2,1,0:T(8,128)(2,1)S(1)}, u32[]{:S(2)}, u32[]{:S(2)}) collective-permute-start(bf16[2,224,256]{2,1,0:T(8,128)(2,1)S(1)} %pad_maximum_fusion.1), channel_id=1, source_target_pairs={{0,4},{4,0},{8,12},{12,8},{16,20},{20,16},{24,28},{28,24},{1,5},{5... | collective-permute-start | bytes 688136 | tf_op jit(solution)/shard_map/ppermute | solution.py:33
  74.8 17.5 %collective-permute-start.17 = (bf16[2,224,256]{2,1,0:T(8,128)(2,1)S(1)}, bf16[2,224,256]{2,1,0:T(8,128)(2,1)S(1)}, u32[]{:S(2)}, u32[]{:S(2)}) collective-permute-start(bf16[2,224,256]{2,1,0:T(8,128)(2,1)S(1)} %pad_maximum_fusion.1), channel_id=1, source_target_pairs={{0,8},{4,12},{8,0},{12,4},{16,24},{20,28},{24,16},{28,20},{1,9},{5... | collective-permute-start | bytes 688136 | tf_op jit(solution)/shard_map/ppermute | solution.py:33
  76.3 16.0 %collective-permute-start.19 = (bf16[2,224,256]{2,1,0:T(8,128)(2,1)S(1)}, bf16[2,224,256]{2,1,0:T(8,128)(2,1)S(1)}, u32[]{:S(2)}, u32[]{:S(2)}) collective-permute-start(bf16[2,224,256]{2,1,0:T(8,128)(2,1)S(1)} %pad_maximum_fusion.1), channel_id=1, source_target_pairs={{0,16},{4,20},{8,24},{12,28},{16,0},{20,4},{24,8},{28,12},{1,17},{... | collective-permute-start | bytes 688136 | tf_op jit(solution)/shard_map/ppermute | solution.py:33
  76.6 16.2 %collective-permute-start.21 = (bf16[2,224,256]{2,1,0:T(8,128)(2,1)S(1)}, bf16[2,224,256]{2,1,0:T(8,128)(2,1)S(1)}, u32[]{:S(2)}, u32[]{:S(2)}) collective-permute-start(bf16[2,224,256]{2,1,0:T(8,128)(2,1)S(1)} %pad_maximum_fusion.1), channel_id=1, source_target_pairs={{0,24},{4,28},{8,16},{12,20},{16,8},{20,12},{24,0},{28,4},{1,25},{... | collective-permute-start | bytes 688136 | tf_op jit(solution)/shard_map/ppermute | solution.py:33
  83.6 18.4 %collective-permute-start.31 = (bf16[256,768]{1,0:T(8,128)(2,1)S(1)}, bf16[256,768]{1,0:T(8,128)(2,1)S(1)}, u32[]{:S(2)}, u32[]{:S(2)}) collective-permute-start(bf16[256,768]{1,0:T(8,128)(2,1)S(1)} %client_activations.3.rest_0_), channel_id=1, source_target_pairs={{0,1},{1,0},{2,3},{3,2},{4,5},{5,4},{6,7},{7,6},{8,9},{9,8},{10,11... | collective-permute-start | bytes 1179656 | tf_op jit(solution)/shard_map/ppermute | solution.py:33
  90.2 15.3 %collective-permute-start.30 = (bf16[256,1024]{1,0:T(8,128)(2,1)S(1)}, bf16[256,1024]{1,0:T(8,128)(2,1)S(1)}, u32[]{:S(2)}, u32[]{:S(2)}) collective-permute-start(bf16[256,1024]{1,0:T(8,128)(2,1)S(1)} %client_activations.2.rest_1_), channel_id=1, source_target_pairs={{0,1},{1,0},{2,3},{3,2},{4,5},{5,4},{6,7},{7,6},{8,9},{9,8},{10,11... | collective-permute-start | bytes 1572872 | tf_op jit(solution)/shard_map/ppermute | solution.py:33
  123.2 8.3 %collective-permute-start.36 = (bf16[224,256]{1,0:T(8,128)(2,1)S(1)}, bf16[224,256]{1,0:T(8,128)(2,1)S(1)}, u32[]{:S(2)}, u32[]{:S(2)}) collective-permute-start(bf16[224,256]{1,0:T(8,128)(2,1)S(1)} %get-tuple-element.35), channel_id=1, source_target_pairs={{0,16},{4,20},{8,24},{12,28},{16,0},{20,4},{24,8},{28,12},{1,17},{... | collective-permute-start | bytes 344072 | tf_op jit(solution)/shard_map/ppermute | solution.py:33
  123.6 8.0 %collective-permute-start.37 = (bf16[224,256]{1,0:T(8,128)(2,1)S(1)}, bf16[224,256]{1,0:T(8,128)(2,1)S(1)}, u32[]{:S(2)}, u32[]{:S(2)}) collective-permute-start(bf16[224,256]{1,0:T(8,128)(2,1)S(1)} %get-tuple-element.36), channel_id=1, source_target_pairs={{0,24},{4,28},{8,16},{12,20},{16,8},{20,12},{24,0},{28,4},{1,25},{... | collective-permute-start | bytes 344072 | tf_op jit(solution)/shard_map/ppermute | solution.py:33
  (35 other events, 473.6 us)
